TPU v7x, 256 devices: a whole 4x4x8 slice. The times are simulated.
256 devices in a mesh: pipe: 2 (over core), tensor: 4 (over x), dp: 32 (over z, y).
Axes of the slice: x: 4, y: 4, z: 8, core: 2. Of those that a mesh axis runs over, the one named last changes fastest.
Arguments:
- section_input: bfloat16 [2, 4096, 4096], P('pipe', 'dp'), may hold values from -8 to 8
- norm_gain: float32 [2, 4096], P('pipe'), may hold values from 0.25 to 1.75
- cotangent: bfloat16 [4096, 4096], P('dp'), may hold values from -6 to 6
- qkv_base: bfloat16 [2, 5120, 4096], P('pipe', 'tensor', 'dp'), may hold values from -1 to 1
- qkv_sign: bfloat16 [2, 5120, 4096], P('pipe', 'tensor', 'dp'), may hold values from -1 to 1, as said below
- qkv_scale: float32 [2, 5120], P('pipe', 'tensor'), may hold values from 0.002 to 0.02
- out_base: bfloat16 [2, 4096, 4096], P('pipe', None, 'tensor'), may hold values from -0.09375 to 0.09375
Outputs:
- qkv_scale_grad: float32 [2, 5120], P('pipe', 'tensor')
Inputs may be any that keep to these rules, and one draw needn't show every extreme that they name: `qkv_sign`: every entry is -1 or +1.
All inputs are finite; a program needn't handle non-finite values.
Results may differ from a plain program's by a relative error of at most 0.02.
Values may be sent and summed in bfloat16 or wider, within the bound.
No kernel may reach another device: no remote copies, remote signals or barrier semaphores. Data moves between devices by JAX's collectives and lax.ppermute only.
A program may use at most 128 MiB of HBM per device.

v0:
```python
import math

import jax
import jax.numpy as jnp
from jax import lax
from jax.sharding import PartitionSpec as P

HD = 128
QH = 8


def shifted(value, axis, steps):
    count = lax.axis_size(axis)
    leading, last = (max(0, -steps), min(count, count - steps))
    return lax.ppermute(value, axis, [(source, source + steps) for source in range(leading, last)])


def norm_parts(inputs, gain_row):
    values = inputs.astype(jnp.float32)
    factor = lax.rsqrt(jnp.mean(values * values, axis=-1, keepdims=True) + 1e-05)
    normed = values * factor
    return ((normed * gain_row).astype(jnp.bfloat16), normed, factor)


def norm_back(grad_hidden, normed, factor, gain_row):
    grad_normed = grad_hidden * gain_row
    return factor * (grad_normed - normed * jnp.mean(grad_normed * normed, axis=-1, keepdims=True))


def split_heads(packed, head_count, head_width):
    queries = packed[..., : head_count * head_width]
    queries = jnp.moveaxis(queries.reshape(packed.shape[:-1] + (head_count, head_width)), -2, -3)
    key_rows = packed[..., head_count * head_width : (head_count + 1) * head_width]
    value_rows = packed[..., (head_count + 1) * head_width :]
    return (queries, key_rows, value_rows)


def merge_heads(heads_in):
    moved = jnp.moveaxis(heads_in, -3, -2)
    return moved.reshape(moved.shape[:-2] + (moved.shape[-2] * moved.shape[-1],))


def attend(queries, key_rows, value_rows):
    head_width = queries.shape[-1]
    seq_length = queries.shape[-2]
    scores = jnp.einsum("...hqd,...kd->...hqk", queries, key_rows) / math.sqrt(head_width)
    row_ids = lax.broadcasted_iota(jnp.int32, (seq_length, seq_length), 0)
    col_ids = lax.broadcasted_iota(jnp.int32, (seq_length, seq_length), 1)
    scores = jnp.where(col_ids <= row_ids, scores, -1000000000.0)
    weights = jax.nn.softmax(scores, axis=-1)
    return jnp.einsum("...hqk,...kd->...hqd", weights, value_rows)


def local(section_input, norm_gain, cotangent, qkv_base, qkv_sign, qkv_scale, out_base):
    inputs = section_input[0]
    gain_row = norm_gain[0]
    seq_length = inputs.shape[0]
    width_full = cotangent.shape[1]
    dp_count = lax.axis_size("dp")
    pipe_index = lax.axis_index("pipe")
    pipe_count = lax.axis_size("pipe")
    weight_out = out_base[0]
    base_qkv, sign_qkv = (
        lax.all_gather(qkv_base[0], "dp", axis=1, tiled=True),
        lax.all_gather(qkv_sign[0], "dp", axis=1, tiled=True),
    )
    weight_qkv = (
        base_qkv.astype(jnp.float32) + qkv_scale[0][:, None] * sign_qkv.astype(jnp.float32)
    ).astype(jnp.bfloat16)
    qkv_rows = weight_qkv.shape[0]
    hidden, normed, factor = norm_parts(inputs, gain_row)
    packed = lax.dot_general(
        hidden, weight_qkv, (((1,), (1,)), ((), ())), preferred_element_type=jnp.float32
    ).astype(jnp.bfloat16)
    queries, key_rows, value_rows = split_heads(packed.astype(jnp.float32), QH, HD)
    attended, attend_back = jax.vjp(attend, queries, key_rows, value_rows)

    def local_back(grad_y):
        grad_mixed = jnp.dot(grad_y, weight_out, preferred_element_type=jnp.float32).astype(
            jnp.bfloat16
        )
        grad_heads = jnp.moveaxis(grad_mixed.astype(jnp.float32).reshape(seq_length, QH, HD), 1, 0)
        grad_q, grad_k, grad_v = attend_back(grad_heads)
        grad_packed = jnp.concatenate([merge_heads(grad_q), grad_k, grad_v], axis=-1).astype(
            jnp.bfloat16
        )
        grad_hidden = jnp.dot(grad_packed, weight_qkv, preferred_element_type=jnp.float32)
        return (grad_packed, grad_hidden)

    def spare_back(grad_y):
        return (
            jnp.zeros((seq_length, qkv_rows), jnp.bfloat16),
            jnp.zeros((seq_length, width_full), jnp.float32),
        )

    grad_y = cotangent
    kept_packed = jnp.zeros((seq_length, qkv_rows), jnp.bfloat16)
    for section_step in range(pipe_count):
        active = pipe_index == pipe_count - 1 - section_step
        grad_packed, grad_hidden = lax.cond(active, local_back, spare_back, grad_y)
        kept_packed = jnp.where(active, grad_packed, kept_packed)
        if section_step + 1 < pipe_count:
            summed = lax.psum(grad_hidden.astype(jnp.bfloat16), "tensor").astype(jnp.float32)
            backward = (
                grad_y.astype(jnp.float32) + norm_back(summed, normed, factor, gain_row)
            ).astype(jnp.bfloat16)
            arrived = shifted(backward, "pipe", -1)
            grad_y = arrived
    inverse_count = 1.0 / (seq_length * dp_count)
    weight_grad_q = lax.dot_general(
        kept_packed, hidden, (((0,), (0,)), ((), ())), preferred_element_type=jnp.float32
    )
    partial_q = jnp.sum(weight_grad_q * sign_qkv.astype(jnp.float32), axis=1) * inverse_count
    total_q = lax.psum(partial_q, "dp")
    return total_q[None]


def solution(mesh):
    placed = (
        P("pipe", "dp", None),
        P("pipe", None),
        P("dp", None),
        P("pipe", "tensor", "dp"),
        P("pipe", "tensor", "dp"),
        P("pipe", "tensor"),
        P("pipe", None, "tensor"),
    )
    return jax.shard_map(
        local, mesh=mesh, in_specs=placed, out_specs=P("pipe", "tensor"), check_vma=False
    )
```

profile of v0, /device:TPU:2, one launch (start us, length us, event | category | flops | bytes accessed | tf_op | source)
XLA Modules:
  0.0 420.8 jit_solution(7917707908121016913)
XLA Ops:
  6.5 0.7 all-gather.7.cloned.1.call-update
  7.3 0.7 all-gather.5.cloned.1.call-update
  8.1 0.7 reduce
  8.8 1.5 fusion.25
  10.3 117.7 %all-gather.7.cloned.1.call-done = bf16[1,1280,4096]{2,1,0:T(8,128)(2,1)} async-done(((bf16[1,1280,128]{2,1,0:T(8,128)(2,1)}), bf16[1,1280,4096]{2,1,0:T(8,128)(2,1)}) %all-gather.7.cloned.1.call-update) | async-done | bytes 10485776 | tf_op jit(solution)/shard_map/all_gather | solution.py:65
  128.1 114.6 %all-gather.5.cloned.1.call-done = bf16[1,1280,4096]{2,1,0:T(8,128)(2,1)} async-done(((bf16[1,1280,128]{2,1,0:T(8,128)(2,1)}), bf16[1,1280,4096]{2,1,0:T(8,128)(2,1)}) %all-gather.5.cloned.1.call-update) | async-done | bytes 10485776 | tf_op jit(solution)/shard_map/all_gather | solution.py:64
  242.7 9.7 %fusion.14 = bf16[1280,4096]{1,0:T(8,128)(2,1)S(1)} fusion(bf16[1,1280,4096]{2,1,0:T(8,128)(2,1)} %all-gather.7.cloned.1.call-done, bf16[1,1280,4096]{2,1,0:T(8,128)(2,1)} %all-gather.5.cloned.1.call-done, f32[1280]{0:T(1024)S(1)} %reduce), kind=kLoop, calls=%fused_computation.30 | loop fusion | flops 26214400 | bytes 31462400 | tf_op jit(solution)/shard_map/convert_element_type | solution.py:69
  252.4 3.6 convolution_convert_fusion.4
  256.1 0.2 copy-done
  256.2 0.1 fusion.41
  256.3 0.6 fusion.42
  256.9 0.3 fusion.43
  257.3 0.8 copy.36
  258.2 0.7 broadcast_in_dim.35
  258.9 1.8 conditional.2
  258.9 1.1 broadcast.47
  260.0 0.8 broadcast.46
  260.8 56.2 %all-reduce.2.cloned.1.call-done = bf16[128,4096]{1,0:T(8,128)(2,1)} async-done(((bf16[128,4096]{1,0:T(8,128)(2,1)}), bf16[128,4096]{1,0:T(8,128)(2,1)}) %all-reduce.2.cloned.1.call-update) | async-done | bytes 1048592 | tf_op jit(solution)/shard_map/psum | solution.py:103
  317.0 1.9 fusion.20
  318.9 1.7 fusion.24
  320.6 1.3 collective-permute-start
  321.9 3.5 collective-permute-done
  325.4 6.2 %conditional.3 = (bf16[128,1280]{0,1:T(8,128)(2,1)S(1)}) conditional(s32[]{:T(128)} %convert_element_type.53, () %tuple.21, (bf16[128,4096]{1,0:T(8,128)(2,1)S(1)}, bf16[4096,1024]{1,0:T(8,128)(2,1)}, bf16[128,128]{1,0:T(8,128)(2,1)S(1)}, f32[8,128,1]{1,0,2:T(8,128)S(1)}, f32[8,128,1]{1,0,2:T(8,128)S(1)}, /*index=5*/f32[8,128,128]{1,2,0:T(8,128)S(1)}, ...), branch_computations={%region_8.9_spmd, %region_9.11_spmd} | conditional | flops 1210777600 | bytes 17465436 | solution.py:100
  325.4 4.7 %convolution_convert_fusion.3 = bf16[128,1024]{1,0:T(8,128)(2,1)S(1)} fusion(bf16[128,4096]{1,0:T(8,128)(2,1)S(1)} %get-tuple-element.62, bf16[4096,1024]{1,0:T(8,128)(2,1)} %get-tuple-element.63), kind=kOutput, calls=%fused_computation.14 | convolution fusion | flops 1073872896 | bytes 9699328 | tf_op jit(solution)/shard_map/cond/branch_1_fun/dot_general | solution.py:79
  330.1 0.2 copy.34
  330.2 0.2 multiply_reduce_fusion.1
  330.5 0.3 convolution_convert_fusion.2
  330.8 0.2 copy-done.5
  331.0 0.3 fusion.6
  331.3 0.2 fusion.8
  331.6 5.9 %fusion.15 = f32[1280]{0:T(1024)S(1)} fusion(bf16[1,1280,4096]{2,1,0:T(8,128)(2,1)} %all-gather.7.cloned.1.call-done, bf16[128,1280]{0,1:T(8,128)(2,1)S(1)} %get-tuple-element.110, bf16[128,1280]{0,1:T(8,128)(2,1)} %get-tuple-element.74, pred[]{:T(512)S(6)} %eq.7, pred[]{:T(512)S(6)} %eq.6, bf16[1,128,4096]{2,1,0:T(8,128)(2,1)S(1)} %copy-done.1, ...), kind=kOutput, calls=%fused_computation.31 | convolution fusion | flops 1360329472 | bytes 12211714 | tf_op jit(solution)/shard_map/dot_general | solution.py:110
  337.5 76.7 %psum.15 = f32[1,1280]{1,0:T(1,128)} all-reduce(f32[1,1280]{1,0:T(1,128)S(1)} %broadcast_in_dim.38), channel_id=1, replica_groups=mesh['pipe'=2,'tensor'=4,'dp'=32] {'dp'}, use_global_device_ids=true, to_apply=%region_12.13 | all-reduce | flops 1280 | bytes 10240 | tf_op jit(solution)/shard_map/psum | solution.py:114
  (27 shorter events, 0.3 us)
Async XLA Ops:
  6.5 121.6 %all-gather.7.cloned.1.call-start = ((), (), s32[]{:S(2)}) async-start(), calls=%async_computation.2 | async-start | bytes 10813440 | tf_op jit(solution)/shard_map/all_gather | solution.py:65
  7.3 235.4 %all-gather.5.cloned.1.call-start = ((), (), s32[]{:S(2)}) async-start(), calls=%async_computation.1 | async-start | bytes 10813440 | tf_op jit(solution)/shard_map/all_gather | solution.py:64
  8.0 309.0 %all-reduce.2.cloned.1.call-start = ((), (), s32[]{:S(2)}) async-start(), calls=%async_computation | async-start | bytes 2097152 | tf_op jit(solution)/shard_map/psum | solution.py:103
  10.3 242.1 %copy-start.1 = (bf16[1,128,4096]{2,1,0:T(8,128)(2,1)S(1)}, bf16[1,128,4096]{2,1,0:T(8,128)(2,1)}, u32[]{:S(2)}) copy-start(bf16[1,128,4096]{2,1,0:T(8,128)(2,1)} %param.11) | copy-start | bytes 3145732
  10.3 242.1 %copy-start.6 = (f32[1,4096]{1,0:T(1,128)S(1)}, f32[1,4096]{1,0:T(1,128)}, u32[]{:S(2)}) copy-start(f32[1,4096]{1,0:T(1,128)} %param.12) | copy-start | bytes 49156
  252.4 3.8 copy-start
  256.2 2.7 copy-start.2
  317.0 1.9 copy-start.3
  320.6 4.8 %collective-permute-start = (bf16[128,4096]{1,0:T(8,128)(2,1)}, bf16[128,4096]{1,0:T(8,128)(2,1)S(1)}, u32[]{:S(2)}, u32[]{:S(2)}) collective-permute-start(bf16[128,4096]{1,0:T(8,128)(2,1)} %fusion.24), channel_id=1, source_target_pairs={{128,0},{129,1},{130,2},{131,3},{132,4},{133,5},{134,6},{135,7},{1... | collective-permute-start | bytes 3145736 | tf_op jit(solution)/shard_map/ppermute | solution.py:15
  325.4 5.1 %copy-start.8 = (pred[8,128,128]{1,2,0:T(32,128)(4,1)S(1)}, pred[8,128,128]{1,2,0:T(32,128)(4,1)}, u32[]{:S(2)}) copy-start(pred[8,128,128]{1,2,0:T(32,128)(4,1)} %get-tuple-element.61) | copy-start | bytes 393220 | tf_op jit(solution)/shard_map/cond
  325.4 5.1 %copy-start.10 = (bf16[128,128]{1,0:T(8,128)(2,1)S(1)}, bf16[128,128]{1,0:T(8,128)(2,1)}, u32[]{:S(2)}) copy-start(bf16[128,128]{1,0:T(8,128)(2,1)} %get-tuple-element.93) | copy-start | bytes 98308 | tf_op jit(solution)/shard_map/cond
  330.0 1.0 copy-start.5
Sparse Core Ops, SparseCore 0:
  9.8 118.2 all-gather.6
  130.5 112.1 all-gather.4
  260.9 56.0 all-reduce.1
where the time goes:
time: 421 us
  waiting for transfers between devices  293 us (70%)
  blocking collectives  76.7 us (18%)
  other arithmetic  15.6 us (4%)
  matrix products  15.6 us (4%)
  between operations  13.2 us (3%)
  local copies, waits for them, and re-layouts  4.62 us (1%)
    all_gather x1, waiting for transfers between devices, local(): lax.all_gather(qkv_sign[0], 'dp', axis=1, tiled=True)  118 us
    all_gather x1, waiting for transfers between devices, local(): lax.all_gather(qkv_base[0], 'dp', axis=1, tiled=True)  115 us
    psum x1, blocking collectives, local(): total_q = lax.psum(partial_q, 'dp')  76.7 us
    psum x1, waiting for transfers between devices, local(): lax.psum(grad_hidden.astype(jnp.bfloat16), 'tensor').astype(jnp.float32)  56.2 us
    convert_element_type x1, other arithmetic, local(): weight_qkv = (base_qkv.astype(jnp.float32) + qkv_scale[0][:, None] * sign...  9.68 us
  transfers between devices with their start and end apart: 4, of which 4 were waited for; matrix products, arithmetic and copies ran while one was open for 1% of the time, Pallas kernels for 0%

commit v1 on v0

v1 whole, which is shorter than its diff:
```python
import functools
import math

import jax
import jax.numpy as jnp
from jax import lax
from jax.experimental import pallas as pl
from jax.experimental.pallas import tpu as pltpu
from jax.sharding import Mesh
from jax.sharding import PartitionSpec as P

HD = 128
QH = 8
NY = 4
NX = 4

F32 = jnp.float32
BF16 = jnp.bfloat16


def dot_nn(a, b):
    return lax.dot_general(a, b, (((1,), (0,)), ((), ())), preferred_element_type=F32)


def dot_nt(a, b):
    return lax.dot_general(a, b, (((1,), (1,)), ((), ())), preferred_element_type=F32)


def dot_tn(a, b):
    return lax.dot_general(a, b, (((0,), (0,)), ((), ())), preferred_element_type=F32)


def attention_back_kernel(packed_ref, grad_ref, out_ref):
    length = packed_ref.shape[0]
    factor = 1.0 / math.sqrt(HD)
    queries = jnp.concatenate([packed_ref[:, h * HD : (h + 1) * HD] for h in range(QH)], axis=0)
    grads = jnp.concatenate([grad_ref[:, h * HD : (h + 1) * HD] for h in range(QH)], axis=0)
    keys = packed_ref[:, QH * HD : (QH + 1) * HD]
    values = packed_ref[:, (QH + 1) * HD :]
    scores = dot_nt(queries, keys) * factor
    rows = lax.broadcasted_iota(jnp.int32, scores.shape, 0) % length
    cols = lax.broadcasted_iota(jnp.int32, scores.shape, 1)
    scores = jnp.where(cols <= rows, scores, -1000000000.0)
    top = jnp.max(scores, axis=-1, keepdims=True)
    raised = jnp.exp(scores - top)
    weights = raised / jnp.sum(raised, axis=-1, keepdims=True)
    grad_weights = dot_nt(grads, values)
    inner = jnp.sum(grad_weights * weights, axis=-1, keepdims=True)
    grad_scores = (weights * (grad_weights - inner) * factor).astype(BF16)
    grad_queries = dot_nn(grad_scores, keys)
    for h in range(QH):
        out_ref[:, h * HD : (h + 1) * HD] = grad_queries[h * length : (h + 1) * length].astype(BF16)
    out_ref[:, QH * HD : (QH + 1) * HD] = dot_tn(grad_scores, queries).astype(BF16)
    out_ref[:, (QH + 1) * HD :] = dot_tn(weights.astype(BF16), grads).astype(BF16)


def attention_back(packed, grad_mixed):
    return pl.pallas_call(
        attention_back_kernel,
        out_shape=jax.ShapeDtypeStruct(packed.shape, BF16),
        in_specs=[pl.BlockSpec(memory_space=pltpu.VMEM)] * 2,
        out_specs=pl.BlockSpec(memory_space=pltpu.VMEM),
        compiler_params=pltpu.CompilerParams(vmem_limit_bytes=32 * 1024 * 1024),
        cost_estimate=pl.CostEstimate(flops=2 * 5 * 1024 * 128 * 128, bytes_accessed=1000000, transcendentals=131072),
    )(packed, grad_mixed)


def send_y(value, steps):
    return lax.ppermute(value, "y", [(i, (i + steps) % NY) for i in range(NY)])


def send_y_upper(value, steps):
    return lax.ppermute(
        value, ("pipe", "y"), [(NY + i, NY + (i + steps) % NY) for i in range(NY)]
    )


def send_x_upper(value, steps):
    return lax.ppermute(
        value, ("pipe", "tensor"), [(NX + i, NX + (i + steps) % NX) for i in range(NX)]
    )


def send_down(value, steps):
    return lax.ppermute(
        value, ("pipe", "tensor"), [(NX + i, (i + steps) % NX) for i in range(NX)]
    )


def turned(blocks, start):
    doubled = jnp.concatenate([blocks, blocks], axis=0)
    return lax.dynamic_slice_in_dim(doubled, start, blocks.shape[0], 0)


def summed_over_y(partial):
    own = partial.shape[0] // NY
    parts = partial.astype(BF16)
    total = partial[:own]
    for k in range(1, NY):
        total = total + send_y(parts[k * own : (k + 1) * own], -k).astype(F32)
    return total


def local(section_input, norm_gain, cotangent, qkv_base, qkv_sign, qkv_scale, out_base):
    inputs = section_input[0]
    gain_row = norm_gain[0][None, :]
    tokens, width = inputs.shape
    nz = lax.axis_size("z")
    piece = width // (nz * NY)
    slab = nz * piece
    chunk = tokens // NX
    pipe_index = lax.axis_index("pipe")
    x_index = lax.axis_index("tensor")
    y_index = lax.axis_index("y")
    weight_out = out_base[0]

    sign = qkv_sign[0]
    weight = (qkv_base[0].astype(F32) + qkv_scale[0][:, None] * sign.astype(F32)).astype(BF16)
    weight_slab = lax.all_gather(weight.T, "z", axis=0, tiled=True)
    sign_slab = lax.all_gather(sign.T, "z", axis=0, tiled=True)

    values = inputs.astype(F32)
    factor = lax.rsqrt(jnp.mean(values * values, axis=-1, keepdims=True) + 1e-05)
    hidden = (values * factor * gain_row).astype(BF16)
    by_y = hidden.reshape(tokens, nz, NY, piece).transpose(2, 0, 1, 3).reshape(NY, tokens, slab)
    by_y = turned(by_y, y_index)
    hidden_slab = jnp.concatenate([by_y[0]] + [send_y(by_y[k], k) for k in range(1, NY)], axis=0)

    packed = summed_over_y(dot_nn(hidden_slab, weight_slab)).astype(BF16)
    projected = summed_over_y(dot_nn(hidden_slab, sign_slab))

    grad_mixed = dot_nn(cotangent, weight_out).astype(BF16)
    grad_upper = attention_back(packed, grad_mixed)

    sent = turned(grad_upper.reshape(NX, chunk, -1), x_index)
    slab_rows = jnp.stack([sent] + [send_y_upper(sent, k) for k in range(1, NY)], axis=1)
    slab_rows = slab_rows.reshape(NX * NY * chunk, -1)
    back = dot_nt(slab_rows, weight_slab)
    back = back.reshape(NX, NY * chunk, slab)
    back_sent = back.astype(BF16)
    total = back[0]
    for j in range(1, NX):
        total = total + send_x_upper(back_sent[j], j).astype(F32)
    total = total.astype(BF16).reshape(NY, chunk, slab)
    whole = jnp.stack([total[0]] + [send_y_upper(total[k], -k) for k in range(1, NY)], axis=0)
    whole = turned(whole, (NY - y_index) % NY)
    grad_hidden = (
        whole.reshape(NY, chunk, nz, piece).transpose(1, 2, 0, 3).reshape(chunk, width).astype(F32)
    )
    rows = lax.dynamic_slice_in_dim(values, x_index * chunk, chunk, 0)
    rows_factor = lax.dynamic_slice_in_dim(factor, x_index * chunk, chunk, 0)
    rows_grad = lax.dynamic_slice_in_dim(cotangent, x_index * chunk, chunk, 0).astype(F32)
    normed = rows * rows_factor
    grad_normed = grad_hidden * gain_row
    backward = rows_grad + rows_factor * (
        grad_normed - normed * jnp.mean(grad_normed * normed, axis=-1, keepdims=True)
    )
    backward = backward.astype(BF16)
    arrived = [send_down(backward, j) for j in (0, 3, 2, 1)]
    arrived = jnp.concatenate(arrived, axis=0)
    grad_mixed_lower = dot_nn(arrived, weight_out).astype(BF16)
    grad_mixed_lower = turned(grad_mixed_lower.reshape(NX, chunk, -1), (NX - x_index) % NX)
    grad_lower = attention_back(packed, grad_mixed_lower.reshape(tokens, -1))

    kept = jnp.where(pipe_index == 1, grad_upper, grad_lower).astype(F32)
    count = tokens * nz * NY
    partial = jnp.sum(kept * projected, axis=0) * (1.0 / count)
    result = lax.psum(lax.psum(partial, "y"), "z")
    return result[None]


def solution(mesh):
    sizes = mesh.devices.shape
    fine = Mesh(mesh.devices.reshape(sizes[0], sizes[1], sizes[2] // NY, NY), ("pipe", "tensor", "z", "y"))
    dp = ("z", "y")
    placed = (
        P("pipe", dp, None),
        P("pipe", None),
        P(dp, None),
        P("pipe", "tensor", dp),
        P("pipe", "tensor", dp),
        P("pipe", "tensor"),
        P("pipe", None, "tensor"),
    )
    return jax.shard_map(
        local, mesh=fine, in_specs=placed, out_specs=P("pipe", "tensor"), check_vma=False
    )
```

time: 421 us -> 190 us (0.45)
  waiting for transfers between devices: 293 us -> 76.3 us
  blocking collectives: 76.7 us -> 23 us
  starting transfers between devices: 1.36 us -> 27.9 us
  matrix products: 15.6 us -> 21 us
  local copies, waits for them, and re-layouts: 4.62 us -> 9.27 us
    all_gather x2, waiting for transfers between devices: 232 us -> 43.9 us  [the longest x1 30.3 us: local(): weight_slab = lax.all_gather(weight.T, 'z', axis=0, tiled=True)]
    psum x1 -> x0, waiting for transfers between devices: 56.2 us -> none  [local(): lax.psum(grad_hidden.astype(jnp.bfloat16), 'tensor').astype(jnp.float32)]
    psum x1 -> x2, blocking collectives: 76.7 us -> 23 us  [local(): result = lax.psum(lax.psum(partial, 'y'), 'z')]
    ppermute x1 -> x22, waiting for transfers between devices: 3.46 us -> 31.7 us  [the longest x9 20.9 us: send_y(): return lax.ppermute(value, 'y', [(i, (i + steps) % NY) for i in range(NY)])]
    ppermute x1 -> x22, starting transfers between devices: 1.28 us -> 27.9 us  [the longest x9 15.2 us: send_y(): return lax.ppermute(value, 'y', [(i, (i + steps) % NY) for i in range(NY)])]
    convert_element_type x2 -> x5, other arithmetic: 11.4 us -> 4.08 us  [the longest x1 1.45 us: local(): values = inputs.astype(F32)]
    dot_general x7 -> x5, matrix products: 15.3 us -> 21 us  [the longest x4 18.2 us: dot_nn(): lax.dot_general(a, b, (((1,), (0,)), ((), ())), preferred_element_type=F32)]
  transfers between devices with their start and end apart: 4 -> 24, of which waited for: 4 -> 12; matrix products, arithmetic and copies ran while one was open for 1% -> 19% of each run, Pallas kernels for 0% -> 1%
where the time goes in v1:
time: 190 us; the launch traced here: 188 us
  waiting for transfers between devices  76.3 us (40%)
  starting transfers between devices  27.9 us (15%)
  blocking collectives  23 us (12%)
  matrix products  21 us (11%)
  other arithmetic  14.4 us (8%)
  between operations  13.9 us (7%)
  local copies, waits for them, and re-layouts  9.27 us (5%)
  Pallas kernels  1.98 us (1%)
    all_gather x1, waiting for transfers between devices, local(): weight_slab = lax.all_gather(weight.T, 'z', axis=0, tiled=True)  30.3 us
    psum x2, blocking collectives, local(): result = lax.psum(lax.psum(partial, 'y'), 'z')  23 us
    ppermute x9, waiting for transfers between devices, send_y(): return lax.ppermute(value, 'y', [(i, (i + steps) % NY) for i in range(NY)])  20.9 us
    dot_general x4, matrix products, dot_nn(): lax.dot_general(a, b, (((1,), (0,)), ((), ())), preferred_element_type=F32)  18.2 us
    ppermute x9, starting transfers between devices, send_y(): return lax.ppermute(value, 'y', [(i, (i + steps) % NY) for i in range(NY)])  15.2 us
    all_gather x1, waiting for transfers between devices, local(): sign_slab = lax.all_gather(sign.T, 'z', axis=0, tiled=True)  13.6 us
    ppermute x4, waiting for transfers between devices, send_down(): lax.ppermute(value, ('pipe', 'tensor'), [(NX + i, (i + steps) % NX) for i...  10.8 us
    ppermute x4, starting transfers between devices, send_down(): lax.ppermute(value, ('pipe', 'tensor'), [(NX + i, (i + steps) % NX) for i...  5.17 us
  transfers between devices with their start and end apart: 24, of which 12 were waited for; matrix products, arithmetic and copies ran while one was open for 19% of the time, Pallas kernels for 1%

profile of v1, /device:TPU:2, one launch (start us, length us, event | category | flops | bytes accessed | tf_op | source)
XLA Modules:
  0.0 187.8 jit_solution(13721848950056463974)
XLA Ops:
  7.3 2.0 %fusion.30 = bf16[128,1280]{0,1:T(8,128)(2,1)} fusion(bf16[1,1280,128]{2,1,0:T(8,128)(2,1)} %param.10, bf16[1,1280,128]{2,1,0:T(8,128)(2,1)} %param.11, f32[1280]{0:T(1024)S(1)} %reduce.1), kind=kLoop, calls=%fused_computation.44 | loop fusion | flops 819200 | bytes 988160 | tf_op jit(solution)/shard_map/transpose | solution.py:119
  10.2 1.3 copy.18
  11.5 1.4 convert_element_type.127
  15.4 1.6 fusion.11
  17.1 1.6 collective-permute-start
  18.7 2.9 %collective-permute-start.1 = (bf16[128,1024]{0,1:T(8,128)(2,1)S(1)}, bf16[128,1024]{0,1:T(8,128)(2,1)}, u32[]{:S(2)}, u32[]{:S(2)}) collective-permute-start(bf16[128,1024]{0,1:T(8,128)(2,1)S(1)} %get-tuple-element.15), channel_id=1, source_target_pairs={{0,2},{1,3},{2,0},{3,1},{4,6},{5,7},{6,4},{7,5},{8,10},{9,11},{10,... | collective-permute-start | bytes 786440 | tf_op jit(solution)/shard_map/ppermute | solution.py:69
  21.6 1.3 collective-permute-start.2
  22.9 3.6 %collective-permute-done = bf16[128,1024]{0,1:T(8,128)(2,1)} collective-permute-done((bf16[128,1024]{0,1:T(8,128)(2,1)S(1)}, bf16[128,1024]{0,1:T(8,128)(2,1)}, u32[]{:S(2)}, u32[]{:S(2)}) %collective-permute-start) | collective-permute-done | bytes 262176 | tf_op jit(solution)/shard_map/ppermute | solution.py:69
  26.6 6.8 %collective-permute-done.1 = bf16[128,1024]{0,1:T(8,128)(2,1)} collective-permute-done((bf16[128,1024]{0,1:T(8,128)(2,1)S(1)}, bf16[128,1024]{0,1:T(8,128)(2,1)}, u32[]{:S(2)}, u32[]{:S(2)}) %collective-permute-start.1) | collective-permute-done | bytes 262176 | tf_op jit(solution)/shard_map/ppermute | solution.py:69
  33.4 30.3 %all-gather.3.cloned.1.call-done = bf16[1024,1280]{0,1:T(8,128)(2,1)} async-done(((bf16[128,1280]{0,1:T(8,128)(2,1)}), bf16[1024,1280]{0,1:T(8,128)(2,1)}) %all-gather.3.cloned.1.call-update) | async-done | bytes 2621456 | tf_op jit(solution)/shard_map/all_gather | solution.py:119
  63.6 3.6 %fusion.45 = (bf16[512,1280]{1,0:T(8,128)(2,1)S(1)}, f32[512,1280]{1,0:T(8,128)S(1)}) fusion(bf16[1024,1280]{0,1:T(8,128)(2,1)} %all-gather.3.cloned.1.call-done, bf16[128,1024]{0,1:T(8,128)(2,1)} %collective-permute-done.2, bf16[128,1024]{0,1:T(8,128)(2,1)} %collective-permute-done.1, bf16[128,1024]{0,1:T(8,128)(2,1)} %collective-permute-done, ...), kind=kOutput, calls=%fused_computation.75 | convolution fusion | flops 1347026944 | bytes 7602176 | tf_op jit(solution)/shard_map/dot_general | solution.py:22
  67.3 2.8 %collective-permute-start.3 = (bf16[128,1280]{1,0:T(8,128)(2,1)S(1)}, bf16[128,1280]{1,0:T(8,128)(2,1)S(1)}, u32[]{:S(2)}, u32[]{:S(2)}) collective-permute-start(bf16[128,1280]{1,0:T(8,128)(2,1)S(1)} %get-tuple-element.5), channel_id=1, source_target_pairs={{0,3},{1,0},{2,1},{3,2},{4,7},{5,4},{6,5},{7,6},{8,11},{9,8},{10,9... | collective-permute-start | bytes 983048 | tf_op jit(solution)/shard_map/ppermute | solution.py:69
  71.8 4.7 %fusion.4.grad_ref = bf16[128,1024]{1,0:T(8,128)(2,1)S(1)} fusion(bf16[128,4096]{1,0:T(8,128)(2,1)S(1)} %copy-done.1, bf16[1,4096,1024]{2,1,0:T(8,128)(2,1)} %param.13), kind=kOutput, calls=%fused_computation.9 | convolution fusion | flops 1073872896 | bytes 9699328 | tf_op jit(solution)/shard_map/dot_general | solution.py:22
  76.6 3.8 %collective-permute-done.3 = bf16[128,1280]{1,0:T(8,128)(2,1)S(1)} collective-permute-done((bf16[128,1280]{1,0:T(8,128)(2,1)S(1)}, bf16[128,1280]{1,0:T(8,128)(2,1)S(1)}, u32[]{:S(2)}, u32[]{:S(2)}) %collective-permute-start.3) | collective-permute-done | bytes 327712 | tf_op jit(solution)/shard_map/ppermute | solution.py:69
  80.6 3.4 %collective-permute-done.5 = bf16[128,1280]{1,0:T(8,128)(2,1)S(1)} collective-permute-done((bf16[128,1280]{1,0:T(8,128)(2,1)S(1)}, bf16[128,1280]{1,0:T(8,128)(2,1)S(1)}, u32[]{:S(2)}, u32[]{:S(2)}) %collective-permute-start.5) | collective-permute-done | bytes 327712 | tf_op jit(solution)/shard_map/ppermute | solution.py:69
  87.4 1.4 collective-permute-start.8
  88.8 1.9 %constant_dynamic-slice_fusion = f32[1,32,4096]{1,2,0:T(8,128)} fusion(f32[1,128,4096]{1,2,0:T(8,128)S(1)} %convert_element_type.127, s32[]{:T(128)S(6)} %select_n.38), kind=kLoop, calls=%fused_computation.64 | loop fusion | bytes 1048580 | tf_op jit(solution)/shard_map/dynamic_slice | solution.py:150
  91.3 2.2 %copy.23 = f32[1,32,4096]{2,1,0:T(8,128)S(1)} copy(f32[1,32,4096]{1,2,0:T(8,128)} %constant_dynamic-slice_fusion) | data formatting | bytes 1048576 | tf_op jit(solution)/shard_map/dynamic_slice | solution.py:150
  95.4 2.9 %fusion.46 = (bf16[512,1024]{1,0:T(8,128)(2,1)S(1)}, f32[512,1024]{1,0:T(8,128)}) fusion(bf16[512,1280]{1,0:T(8,128)(2,1)S(1)} %bitcast.86, bf16[1024,1280]{0,1:T(8,128)(2,1)S(1)} %copy-done.5), kind=kOutput, calls=%fused_computation.76 | convolution fusion | flops 1342701568 | bytes 7077888 | tf_op jit(solution)/shard_map/dot_general | solution.py:26
  100.3 1.4 collective-permute-start.9
  101.7 13.6 %all-gather.5.cloned.1.call-done = bf16[1024,1280]{0,1:T(8,128)(2,1)} async-done(((bf16[128,1280]{0,1:T(8,128)(2,1)}), bf16[1024,1280]{0,1:T(8,128)(2,1)}) %all-gather.5.cloned.1.call-update) | async-done | bytes 2621456 | tf_op jit(solution)/shard_map/all_gather | solution.py:120
  115.3 5.2 %fusion.44 = (bf16[512,1280]{1,0:T(8,128)(2,1)S(1)}, f32[512,1280]{1,0:T(8,128)}) fusion(bf16[1024,1280]{0,1:T(8,128)(2,1)} %all-gather.5.cloned.1.call-done, bf16[128,1024]{0,1:T(8,128)(2,1)} %collective-permute-done.2, bf16[128,1024]{0,1:T(8,128)(2,1)} %collective-permute-done.1, bf16[128,1024]{0,1:T(8,128)(2,1)} %collective-permute-done, ...), kind=kOutput, calls=%fused_computation.74 | convolution fusion | flops 1347026944 | bytes 7602176 | tf_op jit(solution)/shard_map/dot_general | solution.py:22
  132.1 2.8 %collective-permute-start.19 = (bf16[128,1280]{1,0:T(8,128)(2,1)S(1)}, bf16[128,1280]{1,0:T(8,128)(2,1)S(1)}, u32[]{:S(2)}, u32[]{:S(2)}) collective-permute-start(bf16[128,1280]{1,0:T(8,128)(2,1)S(1)} %get-tuple-element.8), channel_id=1, source_target_pairs={{0,3},{1,0},{2,1},{3,2},{4,7},{5,4},{6,5},{7,6},{8,11},{9,8},{10,9... | collective-permute-start | bytes 983048 | tf_op jit(solution)/shard_map/ppermute | solution.py:69
  134.9 2.6 %collective-permute-done.15 = bf16[32,4096]{1,0:T(8,128)(2,1)S(1)} collective-permute-done((bf16[32,4096]{1,0:T(8,128)(2,1)S(1)}, bf16[32,4096]{1,0:T(8,128)(2,1)S(1)}, u32[]{:S(2)}, u32[]{:S(2)}) %collective-permute-start.15) | collective-permute-done | bytes 262176 | tf_op jit(solution)/shard_map/ppermute | solution.py:85
  137.5 2.0 %collective-permute-start.20 = (bf16[128,1280]{1,0:T(8,128)(2,1)S(1)}, bf16[128,1280]{1,0:T(8,128)(2,1)S(1)}, u32[]{:S(2)}, u32[]{:S(2)}) collective-permute-start(bf16[128,1280]{1,0:T(8,128)(2,1)S(1)} %get-tuple-element.10), channel_id=1, source_target_pairs={{0,2},{1,3},{2,0},{3,1},{4,6},{5,7},{6,4},{7,5},{8,10},{9,11},{10,... | collective-permute-start | bytes 983048 | tf_op jit(solution)/shard_map/ppermute | solution.py:69
  139.5 2.2 %collective-permute-done.16 = bf16[32,4096]{1,0:T(8,128)(2,1)S(1)} collective-permute-done((bf16[32,4096]{1,0:T(8,128)(2,1)S(1)}, bf16[32,4096]{1,0:T(8,128)(2,1)S(1)}, u32[]{:S(2)}, u32[]{:S(2)}) %collective-permute-start.16) | collective-permute-done | bytes 262176 | tf_op jit(solution)/shard_map/ppermute | solution.py:85
  141.7 5.1 %collective-permute-done.17 = bf16[32,4096]{1,0:T(8,128)(2,1)S(1)} collective-permute-done((bf16[32,4096]{1,0:T(8,128)(2,1)S(1)}, bf16[32,4096]{1,0:T(8,128)(2,1)S(1)}, u32[]{:S(2)}, u32[]{:S(2)}) %collective-permute-start.17) | collective-permute-done | bytes 262176 | tf_op jit(solution)/shard_map/ppermute | solution.py:85
  147.7 4.7 %fusion.7 = bf16[128,1024]{1,0:T(8,128)(2,1)S(1)} fusion(bf16[1,4096,1024]{2,1,0:T(8,128)(2,1)} %param.13, bf16[32,4096]{1,0:T(8,128)(2,1)S(1)} %collective-permute-done.18, bf16[32,4096]{1,0:T(8,128)(2,1)S(1)} %collective-permute-done.17, bf16[32,4096]{1,0:T(8,128)(2,1)S(1)} %collective-permute-done.16, bf16[32,4096]{1,0:T(8,128)(2,1)S(1)} %collective-permute-done.15), kind=kOutput, calls=%fused_computation.10 | convolution fusion | flops 1078067200 | bytes 9699328 | tf_op jit(solution)/shard_map/dot_general | solution.py:22
  153.5 3.1 %collective-permute-done.21 = bf16[128,1280]{1,0:T(8,128)(2,1)S(1)} collective-permute-done((bf16[128,1280]{1,0:T(8,128)(2,1)S(1)}, bf16[128,1280]{1,0:T(8,128)(2,1)S(1)}, u32[]{:S(2)}, u32[]{:S(2)}) %collective-permute-start.21) | collective-permute-done | bytes 327712 | tf_op jit(solution)/shard_map/ppermute | solution.py:69
  156.6 1.3 fusion.22
  157.9 7.8 %psum.14 = f32[1280]{0:T(1024)S(1)} all-reduce(f32[1280]{0:T(1024)S(1)} %broadcast_multiply_fusion), channel_id=1, replica_groups=mesh['pipe'=2,'tensor'=4,'z'=8,'y'=4] {'y'}, use_global_device_ids=true, to_apply=%region_3.4 | all-reduce | flops 1280 | bytes 10240 | tf_op jit(solution)/shard_map/psum | solution.py:168
  165.8 15.1 %psum.15 = f32[1,1280]{1,0:T(1,128)} all-reduce(f32[1,1280]{1,0:T(1,128)S(1)} %broadcast_in_dim.2), channel_id=1, replica_groups=mesh['pipe'=2,'tensor'=4,'z'=8,'y'=4] {'z'}, use_global_device_ids=true, to_apply=%region_4.5 | all-reduce | flops 1280 | bytes 10240 | tf_op jit(solution)/shard_map/psum | solution.py:168
  (81 shorter events, 27.3 us)
Async XLA Ops:
  6.5 3.6 %copy-start.2 = (bf16[1,128,4096]{2,1,0:T(8,128)(2,1)S(1)}, bf16[1,128,4096]{2,1,0:T(8,128)(2,1)}, u32[]{:S(2)}) copy-start(bf16[1,128,4096]{2,1,0:T(8,128)(2,1)} %param.7) | copy-start | bytes 3145732
  6.5 57.1 %all-gather.3.cloned.1.call-start = ((), (), s32[]{:S(2)}) async-start(), calls=%async_computation | async-start | bytes 2949120 | tf_op jit(solution)/shard_map/all_gather | solution.py:119
  9.4 105.9 %all-gather.5.cloned.1.call-start = ((), (), s32[]{:S(2)}) async-start(), calls=%async_computation.1 | async-start | bytes 2949120 | tf_op jit(solution)/shard_map/all_gather | solution.py:120
  11.5 1.5 copy-start
  11.5 2.1 %copy-start.4 = (f32[1,4096]{1,0:T(1,128)S(1)}, f32[1,4096]{1,0:T(1,128)}, u32[]{:S(2)}) copy-start(f32[1,4096]{1,0:T(1,128)} %param.8) | copy-start | bytes 49156
  17.1 50.2 %copy-start.3 = (bf16[128,1024]{0,1:T(8,128)(2,1)}, bf16[128,1024]{0,1:T(8,128)(2,1)S(1)}, u32[]{:S(2)}) copy-start(bf16[128,1024]{0,1:T(8,128)(2,1)S(1)} %get-tuple-element.14) | copy-start | bytes 786436
  17.1 9.5 %collective-permute-start = (bf16[128,1024]{0,1:T(8,128)(2,1)S(1)}, bf16[128,1024]{0,1:T(8,128)(2,1)}, u32[]{:S(2)}, u32[]{:S(2)}) collective-permute-start(bf16[128,1024]{0,1:T(8,128)(2,1)S(1)} %get-tuple-element.16), channel_id=1, source_target_pairs={{0,1},{1,2},{2,3},{3,0},{4,5},{5,6},{6,7},{7,4},{8,9},{9,10},{10,1... | collective-permute-start | bytes 786440 | tf_op jit(solution)/shard_map/ppermute | solution.py:69
  18.7 14.7 %collective-permute-start.1 = (bf16[128,1024]{0,1:T(8,128)(2,1)S(1)}, bf16[128,1024]{0,1:T(8,128)(2,1)}, u32[]{:S(2)}, u32[]{:S(2)}) collective-permute-start(bf16[128,1024]{0,1:T(8,128)(2,1)S(1)} %get-tuple-element.15), channel_id=1, source_target_pairs={{0,2},{1,3},{2,0},{3,1},{4,6},{5,7},{6,4},{7,5},{8,10},{9,11},{10,... | collective-permute-start | bytes 786440 | tf_op jit(solution)/shard_map/ppermute | solution.py:69
  21.6 11.7 %collective-permute-start.2 = (bf16[128,1024]{0,1:T(8,128)(2,1)S(1)}, bf16[128,1024]{0,1:T(8,128)(2,1)}, u32[]{:S(2)}, u32[]{:S(2)}) collective-permute-start(bf16[128,1024]{0,1:T(8,128)(2,1)S(1)} %get-tuple-element.17), channel_id=1, source_target_pairs={{0,3},{1,0},{2,1},{3,2},{4,7},{5,4},{6,5},{7,6},{8,11},{9,8},{10,9... | collective-permute-start | bytes 786440 | tf_op jit(solution)/shard_map/ppermute | solution.py:69
  67.2 4.6 %copy-start.1 = (bf16[128,4096]{1,0:T(8,128)(2,1)S(1)}, bf16[128,4096]{1,0:T(8,128)(2,1)}, u32[]{:S(2)}) copy-start(bf16[128,4096]{1,0:T(8,128)(2,1)} %param.9) | copy-start | bytes 3145732
  67.3 13.0 %collective-permute-start.3 = (bf16[128,1280]{1,0:T(8,128)(2,1)S(1)}, bf16[128,1280]{1,0:T(8,128)(2,1)S(1)}, u32[]{:S(2)}, u32[]{:S(2)}) collective-permute-start(bf16[128,1280]{1,0:T(8,128)(2,1)S(1)} %get-tuple-element.5), channel_id=1, source_target_pairs={{0,3},{1,0},{2,1},{3,2},{4,7},{5,4},{6,5},{7,6},{8,11},{9,8},{10,9... | collective-permute-start | bytes 983048 | tf_op jit(solution)/shard_map/ppermute | solution.py:69
  70.1 10.5 %collective-permute-start.4 = (bf16[128,1280]{1,0:T(8,128)(2,1)S(1)}, bf16[128,1280]{1,0:T(8,128)(2,1)S(1)}, u32[]{:S(2)}, u32[]{:S(2)}) collective-permute-start(bf16[128,1280]{1,0:T(8,128)(2,1)S(1)} %get-tuple-element.7), channel_id=1, source_target_pairs={{0,2},{1,3},{2,0},{3,1},{4,6},{5,7},{6,4},{7,5},{8,10},{9,11},{10,... | collective-permute-start | bytes 983048 | tf_op jit(solution)/shard_map/ppermute | solution.py:69
  71.0 13.0 %collective-permute-start.5 = (bf16[128,1280]{1,0:T(8,128)(2,1)S(1)}, bf16[128,1280]{1,0:T(8,128)(2,1)S(1)}, u32[]{:S(2)}, u32[]{:S(2)}) collective-permute-start(bf16[128,1280]{1,0:T(8,128)(2,1)S(1)} %get-tuple-element.6), channel_id=1, source_target_pairs={{0,1},{1,2},{2,3},{3,0},{4,5},{5,6},{6,7},{7,4},{8,9},{9,10},{10,1... | collective-permute-start | bytes 983048 | tf_op jit(solution)/shard_map/ppermute | solution.py:69
  86.0 7.6 %collective-permute-start.6 = (bf16[4,32,1280]{2,1,0:T(8,128)(2,1)}, bf16[4,32,1280]{2,1,0:T(8,128)(2,1)S(1)}, u32[]{:S(2)}, u32[]{:S(2)}) collective-permute-start(bf16[4,32,1280]{2,1,0:T(8,128)(2,1)} %fusion.31), channel_id=1, source_target_pairs={{128,129},{129,130},{130,131},{131,128},{132,133},{133,134},{134,1... | collective-permute-start | bytes 983048 | tf_op jit(solution)/shard_map/ppermute | solution.py:73
  86.7 7.0 %collective-permute-start.7 = (bf16[4,32,1280]{2,1,0:T(8,128)(2,1)}, bf16[4,32,1280]{2,1,0:T(8,128)(2,1)S(1)}, u32[]{:S(2)}, u32[]{:S(2)}) collective-permute-start(bf16[4,32,1280]{2,1,0:T(8,128)(2,1)} %fusion.31), channel_id=1, source_target_pairs={{128,130},{129,131},{130,128},{131,129},{132,134},{133,135},{134,1... | collective-permute-start | bytes 983048 | tf_op jit(solution)/shard_map/ppermute | solution.py:73
  87.4 6.3 %collective-permute-start.8 = (bf16[4,32,1280]{2,1,0:T(8,128)(2,1)}, bf16[4,32,1280]{2,1,0:T(8,128)(2,1)}, u32[]{:S(2)}, u32[]{:S(2)}) collective-permute-start(bf16[4,32,1280]{2,1,0:T(8,128)(2,1)} %fusion.31), channel_id=1, source_target_pairs={{128,131},{129,128},{130,129},{131,130},{132,135},{133,132},{134,1... | collective-permute-start | bytes 983048 | tf_op jit(solution)/shard_map/ppermute | solution.py:73
  93.5 1.8 copy-start.5
  99.0 21.5 %collective-permute-start.10 = (bf16[128,1024]{1,0:T(8,128)(2,1)}, bf16[128,1024]{1,0:T(8,128)(2,1)S(1)}, u32[]{:S(2)}, u32[]{:S(2)}) collective-permute-start(bf16[128,1024]{1,0:T(8,128)(2,1)} %get-tuple-element.13), channel_id=1, source_target_pairs={{128,192},{160,224},{192,128},{224,160},{129,193},{161,225},{193,1... | collective-permute-start | bytes 786440 | tf_op jit(solution)/shard_map/ppermute | solution.py:79
  99.6 20.9 %collective-permute-start.11 = (bf16[128,1024]{1,0:T(8,128)(2,1)S(1)}, bf16[128,1024]{1,0:T(8,128)(2,1)S(1)}, u32[]{:S(2)}, u32[]{:S(2)}) collective-permute-start(bf16[128,1024]{1,0:T(8,128)(2,1)S(1)} %get-tuple-element.12), channel_id=1, source_target_pairs={{128,224},{160,128},{192,160},{224,192},{129,225},{161,129},{193,1... | collective-permute-start | bytes 786440 | tf_op jit(solution)/shard_map/ppermute | solution.py:79
  100.3 20.2 %collective-permute-start.9 = (bf16[128,1024]{1,0:T(8,128)(2,1)S(1)}, bf16[128,1024]{1,0:T(8,128)(2,1)}, u32[]{:S(2)}, u32[]{:S(2)}) collective-permute-start(bf16[128,1024]{1,0:T(8,128)(2,1)S(1)} %get-tuple-element.11), channel_id=1, source_target_pairs={{128,160},{160,192},{192,224},{224,128},{129,161},{161,193},{193,2... | collective-permute-start | bytes 786440 | tf_op jit(solution)/shard_map/ppermute | solution.py:79
  121.8 2.0 %collective-permute-start.12 = (bf16[32,1024]{1,0:T(8,128)(2,1)S(1)}, bf16[32,1024]{1,0:T(8,128)(2,1)S(1)}, u32[]{:S(2)}, u32[]{:S(2)}) collective-permute-start(bf16[32,1024]{1,0:T(8,128)(2,1)S(1)} %get-tuple-element.20), channel_id=1, source_target_pairs={{128,131},{129,128},{130,129},{131,130},{132,135},{133,132},{134,1... | collective-permute-start | bytes 196616 | tf_op jit(solution)/shard_map/ppermute | solution.py:73
  122.5 1.4 collective-permute-start.13
  123.1 0.7 collective-permute-start.14
  126.8 10.7 %collective-permute-start.15 = (bf16[32,4096]{1,0:T(8,128)(2,1)S(1)}, bf16[32,4096]{1,0:T(8,128)(2,1)S(1)}, u32[]{:S(2)}, u32[]{:S(2)}) collective-permute-start(bf16[32,4096]{1,0:T(8,128)(2,1)S(1)} %add_convert_fusion), channel_id=1, source_target_pairs={{128,0},{160,32},{192,64},{224,96},{129,1},{161,33},{193,65},{225,... | collective-permute-start | bytes 786440 | tf_op jit(solution)/shard_map/ppermute | solution.py:85
  128.1 13.6 %collective-permute-start.16 = (bf16[32,4096]{1,0:T(8,128)(2,1)S(1)}, bf16[32,4096]{1,0:T(8,128)(2,1)S(1)}, u32[]{:S(2)}, u32[]{:S(2)}) collective-permute-start(bf16[32,4096]{1,0:T(8,128)(2,1)S(1)} %add_convert_fusion), channel_id=1, source_target_pairs={{128,96},{160,0},{192,32},{224,64},{129,97},{161,1},{193,33},{225,... | collective-permute-start | bytes 786440 | tf_op jit(solution)/shard_map/ppermute | solution.py:85
  129.4 17.5 %collective-permute-start.17 = (bf16[32,4096]{1,0:T(8,128)(2,1)S(1)}, bf16[32,4096]{1,0:T(8,128)(2,1)S(1)}, u32[]{:S(2)}, u32[]{:S(2)}) collective-permute-start(bf16[32,4096]{1,0:T(8,128)(2,1)S(1)} %add_convert_fusion), channel_id=1, source_target_pairs={{128,64},{160,96},{192,0},{224,32},{129,65},{161,97},{193,1},{225,... | collective-permute-start | bytes 786440 | tf_op jit(solution)/shard_map/ppermute | solution.py:85
  130.7 17.0 %collective-permute-start.18 = (bf16[32,4096]{1,0:T(8,128)(2,1)S(1)}, bf16[32,4096]{1,0:T(8,128)(2,1)S(1)}, u32[]{:S(2)}, u32[]{:S(2)}) collective-permute-start(bf16[32,4096]{1,0:T(8,128)(2,1)S(1)} %add_convert_fusion), channel_id=1, source_target_pairs={{128,32},{160,64},{192,96},{224,0},{129,33},{161,65},{193,97},{225... | collective-permute-start | bytes 786440 | tf_op jit(solution)/shard_map/ppermute | solution.py:85
  132.1 21.4 %collective-permute-start.19 = (bf16[128,1280]{1,0:T(8,128)(2,1)S(1)}, bf16[128,1280]{1,0:T(8,128)(2,1)S(1)}, u32[]{:S(2)}, u32[]{:S(2)}) collective-permute-start(bf16[128,1280]{1,0:T(8,128)(2,1)S(1)} %get-tuple-element.8), channel_id=1, source_target_pairs={{0,3},{1,0},{2,1},{3,2},{4,7},{5,4},{6,5},{7,6},{8,11},{9,8},{10,9... | collective-permute-start | bytes 983048 | tf_op jit(solution)/shard_map/ppermute | solution.py:69
  137.5 16.0 %collective-permute-start.20 = (bf16[128,1280]{1,0:T(8,128)(2,1)S(1)}, bf16[128,1280]{1,0:T(8,128)(2,1)S(1)}, u32[]{:S(2)}, u32[]{:S(2)}) collective-permute-start(bf16[128,1280]{1,0:T(8,128)(2,1)S(1)} %get-tuple-element.10), channel_id=1, source_target_pairs={{0,2},{1,3},{2,0},{3,1},{4,6},{5,7},{6,4},{7,5},{8,10},{9,11},{10,... | collective-permute-start | bytes 983048 | tf_op jit(solution)/shard_map/ppermute | solution.py:69
  141.7 14.8 %collective-permute-start.21 = (bf16[128,1280]{1,0:T(8,128)(2,1)S(1)}, bf16[128,1280]{1,0:T(8,128)(2,1)S(1)}, u32[]{:S(2)}, u32[]{:S(2)}) collective-permute-start(bf16[128,1280]{1,0:T(8,128)(2,1)S(1)} %get-tuple-element.9), channel_id=1, source_target_pairs={{0,1},{1,2},{2,3},{3,0},{4,5},{5,6},{6,7},{7,4},{8,9},{9,10},{10,1... | collective-permute-start | bytes 983048 | tf_op jit(solution)/shard_map/ppermute | solution.py:69
Sparse Core Ops, SparseCore 0:
  9.5 54.0 all-gather.2
  65.4 49.8 all-gather.4

commit v2 on v1

v2 whole, which is shorter than its diff:
```python
import functools
import math

import jax
import jax.numpy as jnp
from jax import lax
from jax.experimental import pallas as pl
from jax.experimental.pallas import tpu as pltpu
from jax.sharding import Mesh
from jax.sharding import PartitionSpec as P

HD = 128
QH = 8
NY = 4
NX = 4
NZ = 8
ORDER = (0, 7, 1, 6, 2, 5, 3, 4)

F32 = jnp.float32
BF16 = jnp.bfloat16
VMEM = pl.BlockSpec(memory_space=pltpu.VMEM)


def dot_nn(a, b):
    return lax.dot_general(a, b, (((1,), (0,)), ((), ())), preferred_element_type=F32)


def dot_nt(a, b):
    return lax.dot_general(a, b, (((1,), (1,)), ((), ())), preferred_element_type=F32)


def dot_tn(a, b):
    return lax.dot_general(a, b, (((0,), (0,)), ((), ())), preferred_element_type=F32)


def call(kernel, outs, args, flops, vmem=40):
    return pl.pallas_call(
        kernel,
        out_shape=outs,
        in_specs=[VMEM] * len(args),
        out_specs=jax.tree.map(lambda _: VMEM, outs),
        compiler_params=pltpu.CompilerParams(vmem_limit_bytes=vmem * 1024 * 1024),
        cost_estimate=pl.CostEstimate(flops=flops, bytes_accessed=100000, transcendentals=0),
    )(*args)


def block_column(z_index, y_index, y_step, z_step):
    block = ((z_index + z_step) % NZ) * NY + (y_index + y_step) % NY
    return pl.multiple_of(block * HD, HD)


def norm_kernel(inputs_ref, gain_ref, hidden_ref):
    z_index, y_index = lax.axis_index("z"), lax.axis_index("y")
    values = inputs_ref[...].astype(F32)
    factor = lax.rsqrt(jnp.mean(values * values, axis=-1, keepdims=True) + 1e-05)
    for k in range(NY):
        for p, z_step in enumerate(ORDER):
            columns = pl.ds(block_column(z_index, y_index, k, z_step), HD)
            block = inputs_ref[:, columns].astype(F32) * factor * gain_ref[:, columns]
            hidden_ref[k, :, p * HD : (p + 1) * HD] = block.astype(BF16)


def attention_back(packed_of, grads_of):
    factor = 1.0 / math.sqrt(HD)
    queries = jnp.concatenate([packed_of(h) for h in range(QH)], axis=0)
    grads = jnp.concatenate([grads_of(h) for h in range(QH)], axis=0)
    keys, values = packed_of(QH), packed_of(QH + 1)
    length = keys.shape[0]
    scores = dot_nt(queries, keys) * factor
    rows = lax.broadcasted_iota(jnp.int32, scores.shape, 0) % length
    cols = lax.broadcasted_iota(jnp.int32, scores.shape, 1)
    scores = jnp.where(cols <= rows, scores, -1000000000.0)
    top = jnp.max(scores, axis=-1, keepdims=True)
    raised = jnp.exp(scores - top)
    weights = raised / jnp.sum(raised, axis=-1, keepdims=True)
    grad_weights = dot_nt(grads, values)
    inner = jnp.sum(grad_weights * weights, axis=-1, keepdims=True)
    grad_scores = (weights * (grad_weights - inner) * factor).astype(BF16)
    grad_queries = dot_nn(grad_scores, keys)
    heads = [grad_queries[h * length : (h + 1) * length] for h in range(QH)]
    return heads + [dot_tn(grad_scores, queries), dot_tn(weights.astype(BF16), grads)]


def whole_block(halves):
    return jnp.concatenate([ref[...] if at is None else ref[at] for ref, at in halves], axis=0)


def pairs_of(layout, refs):
    blocks = [[(refs[i], at) for i, at in halves] for halves in layout]
    for p in range(0, len(blocks), 2):
        yield p, functools.partial(
            lambda a, b: jnp.concatenate([whole_block(a), whole_block(b)], axis=1), blocks[p], blocks[p + 1]
        )


def upper_kernel(layouts, hidden_ref, grad_ref, *refs):
    *pieces, packed_acc, grad_packed_ref, back_ref = refs[:-3] + (refs[-1], refs[-3], refs[-2])
    x_index = lax.axis_index("tensor")
    length = grad_ref.shape[0]
    chunk = length // NX
    first = True
    for k, layout in enumerate(layouts):
        for p, pair in pairs_of(layout, pieces):
            term = dot_nt(hidden_ref[k, :, p * HD : (p + 2) * HD], pair())
            packed_acc[...] = term if first else packed_acc[...] + term
            first = False
    columns = attention_back(
        lambda h: packed_acc[:, h * HD : (h + 1) * HD].astype(BF16),
        lambda h: grad_ref[:, h * HD : (h + 1) * HD],
    )
    for h, column in enumerate(columns):
        grad_packed_ref[:, h * HD : (h + 1) * HD] = column.astype(BF16)
    for k, layout in enumerate(layouts):
        for p, pair in pairs_of(layout, pieces):
            term = dot_nn(grad_packed_ref[...], pair()).astype(BF16)
            start = (k * NZ + p) * HD
            for c in range(NX):
                back_ref[(c - x_index + NX) % NX, :, start : start + 2 * HD] = term[c * chunk : (c + 1) * chunk]


def slab_kernel(layout, *refs):
    hidden, pieces, out_ref = refs[:NY], refs[NY:-1], refs[-1]
    for k in range(NY):
        total = None
        for p, pair in pairs_of(layout, pieces):
            term = dot_nt(hidden[k][:, p * HD : (p + 2) * HD], pair())
            total = term if total is None else total + term
        out_ref[k] = total.astype(BF16)


def sign_kernel(*refs):
    hidden, sign_ref, out_ref = refs[:NY], refs[NY], refs[-1]
    z_index = lax.axis_index("z")
    for k in range(NY):
        total = None
        for p in range(0, NZ, 2):
            pair = jnp.concatenate([sign_ref[(z_index + ORDER[q]) % NZ] for q in (p, p + 1)], axis=1)
            term = dot_nt(hidden[k][:, p * HD : (p + 2) * HD], pair)
            total = term if total is None else total + term
        out_ref[k] = total.astype(BF16)


def norm_back_kernel(inputs_ref, gain_ref, cotangent_ref, own_ref, *refs):
    others, out_ref = refs[:-1], refs[-1]
    x_index = lax.axis_index("tensor")
    z_index, y_index = lax.axis_index("z"), lax.axis_index("y")
    chunk = out_ref.shape[0]
    rows = pl.ds(pl.multiple_of(x_index * chunk, chunk), chunk)
    values = inputs_ref[rows, :].astype(F32)
    width = values.shape[1]
    factor = lax.rsqrt(jnp.mean(values * values, axis=-1, keepdims=True) + 1e-05)
    grads, columns = [], []
    inner = jnp.zeros((chunk, HD), F32)
    for k in range(NY):
        for p, z_step in enumerate(ORDER):
            at = (k * NZ + p) * HD
            column = pl.ds(block_column(z_index, y_index, k, z_step), HD)
            grad = own_ref[0, :, at : at + HD].astype(F32)
            for other in others:
                grad = grad + other[:, at : at + HD].astype(F32)
            grad = grad * gain_ref[:, column]
            inner = inner + grad * (inputs_ref[rows, column].astype(F32) * factor)
            grads.append(grad)
            columns.append(column)
    mean = jnp.sum(inner, axis=-1, keepdims=True) * (1.0 / width)
    for grad, column in zip(grads, columns):
        normed = inputs_ref[rows, column].astype(F32) * factor
        kept = cotangent_ref[rows, column].astype(F32)
        out_ref[:, column] = (kept + factor * (grad - normed * mean)).astype(BF16)


def lower_kernel(count, packed_ref, weight_ref, upper_ref, *refs):
    arrived, projected, out_ref, rows_ref, mixed_ref = refs[:NX], refs[NX:-3], refs[-3], refs[-2], refs[-1]
    x_index = lax.axis_index("tensor")
    pipe_index = lax.axis_index("pipe")
    chunk = arrived[0].shape[0]
    for j in range(NX):
        place = pl.multiple_of(((x_index - j + NX) % NX) * chunk, chunk)
        rows_ref[pl.ds(place, chunk), :] = arrived[j][...]
    mixed_ref[...] = jnp.zeros_like(mixed_ref)
    depth = 512

    def step(i, _):
        at = pl.ds(pl.multiple_of(i * depth, depth), depth)
        mixed_ref[...] += dot_nn(rows_ref[:, at], weight_ref[at, :])
        return 0

    lax.fori_loop(0, rows_ref.shape[1] // depth, step, 0)
    columns = attention_back(
        lambda h: packed_ref[:, h * HD : (h + 1) * HD],
        lambda h: mixed_ref[:, h * HD : (h + 1) * HD].astype(BF16),
    )
    for h, column in enumerate(columns):
        at = slice(h * HD, (h + 1) * HD)
        lower = column.astype(BF16).astype(F32)
        kept = jnp.where(pipe_index == 1, upper_ref[:, at].astype(F32), lower)
        product = projected[0][0, :, at].astype(F32)
        for other in projected[1:]:
            product = product + other[:, at].astype(F32)
        out_ref[:, at] = jnp.sum(kept * product, axis=0, keepdims=True) * (1.0 / count)


def send_z(value, steps):
    return lax.ppermute(value, "z", [(i, (i + steps) % NZ) for i in range(NZ)])


def send_y(value, steps, pipes=(0, 1)):
    pairs = [(NY * p + i, NY * p + (i + steps) % NY) for p in pipes for i in range(NY)]
    return lax.ppermute(value, ("pipe", "y"), pairs)


def send_x_upper(value, steps):
    pairs = [(NX + i, NX + (i + steps) % NX) for i in range(NX)]
    return lax.ppermute(value, ("pipe", "tensor"), pairs)


def send_down(value, steps):
    return lax.ppermute(value, ("pipe", "tensor"), [(NX + i, (i + steps) % NX) for i in range(NX)])


def local(section_input, norm_gain, cotangent, qkv_base, qkv_sign, qkv_scale, out_base):
    inputs = section_input[0]
    tokens, width = inputs.shape
    chunk = tokens // NX
    weight_out = out_base[0]
    sign = qkv_sign[0]
    rows = sign.shape[0]
    half = rows // 2
    weight = (qkv_base[0].astype(F32) + qkv_scale[0][:, None] * sign.astype(F32)).astype(BF16)

    above, below = [weight], [weight]
    for _ in range(3):
        below.append(send_z(below[-1], 1))
        above.append(send_z(above[-1], -1))
    far_first, far_second = send_z(below[3][:half], 1), send_z(above[3][half:], -1)
    sign_slab = lax.all_gather(sign, "z", axis=0, tiled=True).reshape(NZ, rows, -1)

    single = lambda i: [[(i, None)]]
    split = lambda i: [[(i, None), (i + 1, None)]]
    pair = lambda i: [[(i, 0)], [(i, 1)]]
    groups = [weight] + [jnp.stack([below[i], above[i]]) for i in (1, 2, 3)]
    groups += [jnp.concatenate([far_first, far_second], axis=0)]
    pieces, layouts = [], []
    sides = [[], [], [], []]
    for group in groups:
        from_below, from_above = send_y(group, 1, (1,)), send_y(group, -1, (1,))
        if group.ndim == 3:
            parts = (from_below[0], from_above[1])
        else:
            parts = (from_below[:half], from_above[half:])
        sides[0].append([group])
        sides[1].append([from_above])
        sides[2].append([send_y(parts[0], 1, (1,)), send_y(parts[1], -1, (1,))])
        sides[3].append([from_below])
    for side in sides:
        layout = []
        for arrays in side:
            at = len(pieces)
            pieces += arrays
            if len(arrays) == 1:
                layout += pair(at) if arrays[0].ndim == 3 else single(at)
            else:
                layout += split(at) if arrays[0].shape[0] == half else single(at) + single(at + 1)
        layouts.append(layout)

    hidden = call(
        norm_kernel, jax.ShapeDtypeStruct((NY, tokens, NZ * HD), BF16), (inputs, norm_gain), 10**7
    )
    hidden_slab = [hidden[0]] + [send_y(hidden[k], k) for k in range(1, NY)]
    grad_mixed = dot_nn(cotangent, weight_out).astype(BF16)

    flops = 2 * tokens * rows * width
    upper = pl.pallas_call(
        functools.partial(upper_kernel, layouts),
        out_shape=(
            jax.ShapeDtypeStruct((tokens, rows), BF16),
            jax.ShapeDtypeStruct((NX, chunk, width), BF16),
        ),
        in_specs=[VMEM] * (2 + len(pieces)),
        out_specs=(VMEM, VMEM),
        scratch_shapes=[pltpu.VMEM((tokens, rows), F32)],
        compiler_params=pltpu.CompilerParams(vmem_limit_bytes=40 * 1024 * 1024),
        cost_estimate=pl.CostEstimate(flops=2 * flops, bytes_accessed=100000, transcendentals=131072),
    )
    grad_upper, back = upper(hidden, grad_mixed, *pieces)

    own = pieces[: len(groups)]
    partial = call(
        functools.partial(slab_kernel, layouts[0]),
        jax.ShapeDtypeStruct((NY, tokens, rows), BF16),
        (*hidden_slab, *own),
        flops,
    )
    packed = partial[0].astype(F32)
    for k in range(1, NY):
        packed = packed + send_y(partial[k], -k, (0,)).astype(F32)
    packed = packed.astype(BF16)

    signed = call(
        sign_kernel, jax.ShapeDtypeStruct((NY, tokens, rows), BF16), (*hidden_slab, sign_slab), flops
    )
    projected = [signed] + [send_y(signed[k], -k) for k in range(1, NY)]

    received = [send_x_upper(back[j], j) for j in range(1, NX)]
    backward = call(
        norm_back_kernel,
        jax.ShapeDtypeStruct((chunk, width), BF16),
        (inputs, norm_gain, cotangent, back, *received),
        10**6,
    )
    arrived = [send_down(backward, j) for j in range(NX)]
    args = (packed, weight_out, grad_upper, *arrived, *projected)
    result = pl.pallas_call(
        functools.partial(lower_kernel, tokens * NZ * NY),
        out_shape=jax.ShapeDtypeStruct((1, rows), F32),
        in_specs=[VMEM] * len(args),
        out_specs=VMEM,
        scratch_shapes=[pltpu.VMEM((tokens, width), BF16), pltpu.VMEM((tokens, QH * HD), F32)],
        compiler_params=pltpu.CompilerParams(vmem_limit_bytes=40 * 1024 * 1024),
        cost_estimate=pl.CostEstimate(flops=flops, bytes_accessed=100000, transcendentals=131072),
    )(*args)
    return lax.psum(lax.psum(result, "y"), "z")


def solution(mesh):
    sizes = mesh.devices.shape
    fine = Mesh(mesh.devices.reshape(sizes[0], sizes[1], NZ, NY), ("pipe", "tensor", "z", "y"))
    dp = ("z", "y")
    placed = (
        P("pipe", dp, None),
        P("pipe", None),
        P(dp, None),
        P("pipe", "tensor", dp),
        P("pipe", "tensor", dp),
        P("pipe", "tensor"),
        P("pipe", None, "tensor"),
    )
    return jax.shard_map(
        local, mesh=fine, in_specs=placed, out_specs=P("pipe", "tensor"), check_vma=False
    )
```

time: 190 us -> 208 us (1.095)
  starting transfers between devices: 27.9 us -> 55.7 us
  matrix products: 21 us -> 1.34 us
  Pallas kernels: 1.98 us -> 18.9 us
  other arithmetic: 14.4 us -> 5.92 us
  blocking collectives: 23 us -> 26.4 us
  local copies, waits for them, and re-layouts: 9.27 us -> 6.61 us
    all_gather x2 -> x1, waiting for transfers between devices: 43.9 us -> 0.02 us  [local(): lax.all_gather(sign, 'z', axis=0, tiled=True).reshape(NZ, rows, -1)]
    ppermute x4, waiting for transfers between devices: 10.8 us -> 50 us  [send_down(): lax.ppermute(value, ('pipe', 'tensor'), [(NX + i, (i + steps) % NX) for i...]
    ppermute x18 -> x40, starting transfers between devices: 22.7 us -> 50.5 us  [the longest x29 32.5 us: send_y(): return lax.ppermute(value, ('pipe', 'y'), pairs)]
    pallas_call x2 -> x6, Pallas kernels: 1.98 us -> 18.9 us  [the longest x4 8.69 us: call(): pl.pallas_call(kernel, out_shape=outs, in_specs=[VMEM] * len(args), out_s...]
    dot_general x4 -> x1, matrix products: 18.2 us -> 1.34 us  [dot_nn(): lax.dot_general(a, b, (((1,), (0,)), ((), ())), preferred_element_type=F32)]
    ppermute x18 -> x40, waiting for transfers between devices: 20.9 us -> 27.3 us  [the longest x8 20 us: send_z(): return lax.ppermute(value, 'z', [(i, (i + steps) % NZ) for i in range(NZ)])]
    dynamic_slice x2 -> x0, local copies, waits for them, and re-layouts: 4.11 us -> none  [local(): rows = lax.dynamic_slice_in_dim(values, x_index * chunk, chunk, 0)]
    psum x2, blocking collectives: 23 us -> 26.4 us  [local(): return lax.psum(lax.psum(result, 'y'), 'z')]
  transfers between devices with their start and end apart: 24 -> 45, of which waited for: 12 -> 11; matrix products, arithmetic and copies ran while one was open for 19% -> 3% of each run, Pallas kernels for 1% -> 7%
where the time goes in v2:
time: 208 us; the launch traced here: 206 us
  waiting for transfers between devices  77.3 us (37%)
  starting transfers between devices  55.7 us (27%)
  blocking collectives  26.4 us (13%)
  Pallas kernels  18.9 us (9%)
  between operations  14.4 us (7%)
  local copies, waits for them, and re-layouts  6.61 us (3%)
  other arithmetic  5.92 us (3%)
    ppermute x4, waiting for transfers between devices, send_down(): lax.ppermute(value, ('pipe', 'tensor'), [(NX + i, (i + steps) % NX) for i...  50 us
    ppermute x29, starting transfers between devices, send_y(): return lax.ppermute(value, ('pipe', 'y'), pairs)  32.5 us
    psum x2, blocking collectives, local(): return lax.psum(lax.psum(result, 'y'), 'z')  26.4 us
    ppermute x8, waiting for transfers between devices, send_z(): return lax.ppermute(value, 'z', [(i, (i + steps) % NZ) for i in range(NZ)])  20 us
    ppermute x8, starting transfers between devices, send_z(): return lax.ppermute(value, 'z', [(i, (i + steps) % NZ) for i in range(NZ)])  15.9 us
    pallas_call x4, Pallas kernels, call(): pl.pallas_call(kernel, out_shape=outs, in_specs=[VMEM] * len(args), out_s...  8.69 us
    ppermute x29, waiting for transfers between devices, send_y(): return lax.ppermute(value, ('pipe', 'y'), pairs)  7.28 us
    pallas_call x1, Pallas kernels, local(): grad_upper, back = upper(hidden, grad_mixed, *pieces)  6.54 us
  transfers between devices with their start and end apart: 45, of which 11 were waited for; matrix products, arithmetic and copies ran while one was open for 3% of the time, Pallas kernels for 7%

profile of v2, /device:TPU:2, one launch (start us, length us, event | category | flops | bytes accessed | tf_op | source)
XLA Modules:
  0.0 206.4 jit_solution(1406597029087949993)
XLA Ops:
  7.3 1.3 fusion.4.refs_4_.refs_0_
  8.7 2.0 collective-permute-start.3
  10.7 4.0 %collective-permute-start.4 = (bf16[1280,128]{1,0:T(8,128)(2,1)S(1)}, bf16[1280,128]{1,0:T(8,128)(2,1)}, u32[]{:S(2)}, u32[]{:S(2)}) collective-permute-start(bf16[1280,128]{1,0:T(8,128)(2,1)S(1)} %fusion.4.refs_4_.refs_0_), channel_id=1, source_target_pairs={{0,28},{4,0},{8,4},{12,8},{16,12},{20,16},{24,20},{28,24},{1,29},{... | collective-permute-start | bytes 983048 | tf_op jit(solution)/shard_map/ppermute | solution.py:204
  14.7 7.7 %collective-permute-done.3 = bf16[1280,128]{1,0:T(8,128)(2,1)} collective-permute-done((bf16[1280,128]{1,0:T(8,128)(2,1)S(1)}, bf16[1280,128]{1,0:T(8,128)(2,1)}, u32[]{:S(2)}, u32[]{:S(2)}) %collective-permute-start.3) | collective-permute-done | bytes 327712 | tf_op jit(solution)/shard_map/ppermute | solution.py:204
  22.4 3.2 %collective-permute-start.6 = (bf16[1280,128]{1,0:T(8,128)(2,1)}, bf16[1280,128]{1,0:T(8,128)(2,1)}, u32[]{:S(2)}, u32[]{:S(2)}) collective-permute-start(bf16[1280,128]{1,0:T(8,128)(2,1)} %collective-permute-done.4), channel_id=1, source_target_pairs={{0,28},{4,0},{8,4},{12,8},{16,12},{20,16},{24,20},{28,24},{1,29},{... | collective-permute-start | bytes 983048 | tf_op jit(solution)/shard_map/ppermute | solution.py:204
  29.5 3.3 %collective-permute-done.5 = bf16[1280,128]{1,0:T(8,128)(2,1)} collective-permute-done((bf16[1280,128]{1,0:T(8,128)(2,1)}, bf16[1280,128]{1,0:T(8,128)(2,1)}, u32[]{:S(2)}, u32[]{:S(2)}) %collective-permute-start.5) | collective-permute-done | bytes 327712 | tf_op jit(solution)/shard_map/ppermute | solution.py:204
  32.8 3.2 %collective-permute-start.8 = (bf16[1280,128]{1,0:T(8,128)(2,1)}, bf16[1280,128]{1,0:T(8,128)(2,1)S(1)}, u32[]{:S(2)}, u32[]{:S(2)}) collective-permute-start(bf16[1280,128]{1,0:T(8,128)(2,1)} %collective-permute-done.6), channel_id=1, source_target_pairs={{0,28},{4,0},{8,4},{12,8},{16,12},{20,16},{24,20},{28,24},{1,29},{... | collective-permute-start | bytes 983048 | tf_op jit(solution)/shard_map/ppermute | solution.py:204
  36.2 1.7 collective-permute-start
  39.9 2.7 %collective-permute-done.7 = bf16[1280,128]{1,0:T(8,128)(2,1)S(1)} collective-permute-done((bf16[1280,128]{1,0:T(8,128)(2,1)}, bf16[1280,128]{1,0:T(8,128)(2,1)S(1)}, u32[]{:S(2)}, u32[]{:S(2)}) %collective-permute-start.7) | collective-permute-done | bytes 327712 | tf_op jit(solution)/shard_map/ppermute | solution.py:204
  44.2 3.3 %collective-permute-start.10 = (bf16[640,128]{1,0:T(8,128)(2,1)S(1)}, bf16[640,128]{1,0:T(8,128)(2,1)S(1)}, u32[]{:S(2)}, u32[]{:S(2)}) collective-permute-start(bf16[640,128]{1,0:T(8,128)(2,1)S(1)} %slice.109), channel_id=1, source_target_pairs={{0,28},{4,0},{8,4},{12,8},{16,12},{20,16},{24,20},{28,24},{1,29},{... | collective-permute-start | bytes 491528 | tf_op jit(solution)/shard_map/ppermute | solution.py:204
  47.6 6.2 %collective-permute-done.9 = bf16[640,128]{1,0:T(8,128)(2,1)S(1)} collective-permute-done((bf16[640,128]{1,0:T(8,128)(2,1)S(1)}, bf16[640,128]{1,0:T(8,128)(2,1)S(1)}, u32[]{:S(2)}, u32[]{:S(2)}) %collective-permute-start.9) | collective-permute-done | bytes 163872 | tf_op jit(solution)/shard_map/ppermute | solution.py:204
  56.8 5.4 %collective-permute-start.1 = (bf16[128,1024]{1,0:T(8,128)(2,1)S(1)}, bf16[128,1024]{1,0:T(8,128)(2,1)S(1)}, u32[]{:S(2)}, u32[]{:S(2)}) collective-permute-start(bf16[128,1024]{1,0:T(8,128)(2,1)S(1)} %get-tuple-element.19), channel_id=1, source_target_pairs={{0,2},{1,3},{2,0},{3,1},{128,130},{129,131},{130,128},{131,129},{4... | collective-permute-start | bytes 786440 | tf_op jit(solution)/shard_map/ppermute | solution.py:209
  64.3 2.2 %collective-permute-done.1.refs_2_ = bf16[128,1024]{1,0:T(8,128)(2,1)S(1)} collective-permute-done((bf16[128,1024]{1,0:T(8,128)(2,1)S(1)}, bf16[128,1024]{1,0:T(8,128)(2,1)S(1)}, u32[]{:S(2)}, u32[]{:S(2)}) %collective-permute-start.1) | collective-permute-done | bytes 262176 | tf_op jit(solution)/shard_map/ppermute | solution.py:209
  67.2 2.9 %collective-permute-done.2.refs_3_ = bf16[128,1024]{1,0:T(8,128)(2,1)S(1)} collective-permute-done((bf16[128,1024]{1,0:T(8,128)(2,1)S(1)}, bf16[128,1024]{1,0:T(8,128)(2,1)S(1)}, u32[]{:S(2)}, u32[]{:S(2)}) %collective-permute-start.2) | collective-permute-done | bytes 262176 | tf_op jit(solution)/shard_map/ppermute | solution.py:209
  75.2 1.3 convolution_convert_fusion.grad_ref
  76.6 3.5 %shard_map.74 = bf16[4,128,1280]{2,1,0:T(8,128)(2,1)S(1)} custom-call(bf16[128,1024]{1,0:T(8,128)(2,1)S(1)} %get-tuple-element.21.refs_0_, bf16[128,1024]{1,0:T(8,128)(2,1)S(1)} %collective-permute-done.refs_1_, bf16[128,1024]{1,0:T(8,128)(2,1)S(1)} %collective-permute-done.1.refs_2_, bf16[128,1024]{1,0:T(8,128)(2,1)S(1)} %collective-permute-done.2.refs_3_, ...), custom_call_target="tpu_custom_call" | custom-call | flops 1342177280 | bytes 100000 | tf_op jit(solution)/shard_map/pallas_call | solution.py:37
  80.1 6.5 %shard_map.75 = (bf16[128,1280]{1,0:T(8,128)(2,1)S(1)}, bf16[4,32,4096]{2,1,0:T(8,128)(2,1)S(1)}) custom-call(bf16[4,128,1024]{2,1,0:T(8,128)(2,1)S(1)} %shard_map.73.hidden_ref, bf16[128,1024]{1,0:T(8,128)(2,1)S(1)} %convolution_convert_fusion.grad_ref, bf16[1280,128]{1,0:T(8,128)(2,1)S(1)} %fusion.4.refs_4_.refs_0_, ...), custom_call_target="tpu_custom_call" | custom-call | flops 2684354560 | bytes 100000 | tf_op jit(solution)/shard_map/pallas_call | solution.py:285
  90.0 4.5 %collective-permute-start.11 = (bf16[128,1280]{1,0:T(8,128)(2,1)}, bf16[128,1280]{1,0:T(8,128)(2,1)}, u32[]{:S(2)}, u32[]{:S(2)}) collective-permute-start(bf16[128,1280]{1,0:T(8,128)(2,1)} %get-tuple-element.12), channel_id=1, source_target_pairs={{0,3},{1,0},{2,1},{3,2},{4,7},{5,4},{6,5},{7,6},{8,11},{9,8},{10,9... | collective-permute-start | bytes 983048 | tf_op jit(solution)/shard_map/ppermute | solution.py:209
  94.5 2.1 collective-permute-start.12
  96.6 2.6 %collective-permute-start.13 = (bf16[128,1280]{1,0:T(8,128)(2,1)}, bf16[128,1280]{1,0:T(8,128)(2,1)}, u32[]{:S(2)}, u32[]{:S(2)}) collective-permute-start(bf16[128,1280]{1,0:T(8,128)(2,1)} %get-tuple-element.13), channel_id=1, source_target_pairs={{0,1},{1,2},{2,3},{3,0},{4,5},{5,6},{6,7},{7,4},{8,9},{9,10},{10,1... | collective-permute-start | bytes 983048 | tf_op jit(solution)/shard_map/ppermute | solution.py:209
  103.1 1.7 copy-done.4
  104.9 3.4 %shard_map.77.refs_4_ = bf16[4,128,1280]{2,1,0:T(8,128)(2,1)S(1)} custom-call(bf16[128,1024]{1,0:T(8,128)(2,1)S(1)} %copy-done.6, bf16[128,1024]{1,0:T(8,128)(2,1)S(1)} %copy-done.10, bf16[128,1024]{1,0:T(8,128)(2,1)S(1)} %copy-done.12, bf16[128,1024]{1,0:T(8,128)(2,1)S(1)} %copy-done.14, bf16[8,1280,128]{2,1,0:T(8,128)(2,1)S(1)} %bitcast.64), custom_call_target="tpu_custom_call" | custom-call | flops 1342177280 | bytes 100000 | tf_op jit(solution)/shard_map/pallas_call | solution.py:37
  111.0 2.1 %collective-permute-done.13 = bf16[128,1280]{1,0:T(8,128)(2,1)} collective-permute-done((bf16[128,1280]{1,0:T(8,128)(2,1)}, bf16[128,1280]{1,0:T(8,128)(2,1)}, u32[]{:S(2)}, u32[]{:S(2)}) %collective-permute-start.13) | collective-permute-done | bytes 327712 | tf_op jit(solution)/shard_map/ppermute | solution.py:209
  114.0 37.2 %collective-permute-done.37.refs_0_ = bf16[32,4096]{1,0:T(8,128)(2,1)S(1)} collective-permute-done((bf16[32,4096]{1,0:T(8,128)(2,1)}, bf16[32,4096]{1,0:T(8,128)(2,1)S(1)}, u32[]{:S(2)}, u32[]{:S(2)}) %collective-permute-start.37) | collective-permute-done | bytes 262176 | tf_op jit(solution)/shard_map/ppermute | solution.py:218
  152.1 4.6 %collective-permute-done.38.refs_1_ = bf16[32,4096]{1,0:T(8,128)(2,1)S(1)} collective-permute-done((bf16[32,4096]{1,0:T(8,128)(2,1)}, bf16[32,4096]{1,0:T(8,128)(2,1)S(1)}, u32[]{:S(2)}, u32[]{:S(2)}) %collective-permute-start.38) | collective-permute-done | bytes 262176 | tf_op jit(solution)/shard_map/ppermute | solution.py:218
  156.7 1.3 fusion.2.packed_ref
  158.0 5.8 %collective-permute-done.39.refs_2_ = bf16[32,4096]{1,0:T(8,128)(2,1)S(1)} collective-permute-done((bf16[32,4096]{1,0:T(8,128)(2,1)}, bf16[32,4096]{1,0:T(8,128)(2,1)S(1)}, u32[]{:S(2)}, u32[]{:S(2)}) %collective-permute-start.39) | collective-permute-done | bytes 262176 | tf_op jit(solution)/shard_map/ppermute | solution.py:218
  163.8 2.4 %collective-permute-done.40.refs_3_ = bf16[32,4096]{1,0:T(8,128)(2,1)S(1)} collective-permute-done((bf16[32,4096]{1,0:T(8,128)(2,1)}, bf16[32,4096]{1,0:T(8,128)(2,1)S(1)}, u32[]{:S(2)}, u32[]{:S(2)}) %collective-permute-start.40) | collective-permute-done | bytes 262176 | tf_op jit(solution)/shard_map/ppermute | solution.py:218
  166.2 3.4 %copy-done.1 = bf16[1,4096,1024]{2,1,0:T(8,128)(2,1)S(1)} copy-done((bf16[1,4096,1024]{2,1,0:T(8,128)(2,1)S(1)}, bf16[1,4096,1024]{2,1,0:T(8,128)(2,1)}, u32[]{:S(2)}) %copy-start.1) | copy-done | bytes 8388632
  169.5 3.6 %shard_map.78 = f32[1,1280]{1,0:T(1,128)S(1)} custom-call(bf16[128,1280]{1,0:T(8,128)(2,1)S(1)} %fusion.2.packed_ref, bf16[4096,1024]{1,0:T(8,128)(2,1)S(1)} %bitcast.61, bf16[128,1280]{1,0:T(8,128)(2,1)S(1)} %copy-done.20, bf16[32,4096]{1,0:T(8,128)(2,1)S(1)} %collective-permute-done.37.refs_0_, bf16[32,4096]{1,0:T(8,128)(2,1)S(1)} %collective-permute-done.38.refs_1_, ...), custom_call_target="tpu_custom_call" | custom-call | flops 1342177280 | bytes 100000 | tf_op jit(solution)/shard_map/pallas_call | solution.py:313
  173.2 10.1 %psum.14 = f32[1,1280]{1,0:T(1,128)S(1)} all-reduce(f32[1,1280]{1,0:T(1,128)S(1)} %shard_map.78), channel_id=1, replica_groups=mesh['pipe'=2,'tensor'=4,'z'=8,'y'=4] {'y'}, use_global_device_ids=true, to_apply=%region_0.0 | all-reduce | flops 1280 | bytes 10240 | tf_op jit(solution)/shard_map/psum | solution.py:322
  183.3 16.3 %psum.15 = f32[1,1280]{1,0:T(1,128)} all-reduce(f32[1,1280]{1,0:T(1,128)S(1)} %psum.14), channel_id=1, replica_groups=mesh['pipe'=2,'tensor'=4,'z'=8,'y'=4] {'z'}, use_global_device_ids=true, to_apply=%region_1.0 | all-reduce | flops 1280 | bytes 10240 | tf_op jit(solution)/shard_map/psum | solution.py:322
  (136 shorter events, 30.3 us)
Async XLA Ops:
  6.5 96.5 %all-gather.3.cloned.1.call-start = ((), (), s32[]{:S(2)}) async-start(), calls=%async_computation | async-start | bytes 2949120 | tf_op jit(solution)/shard_map/all_gather | solution.py:236
  8.7 13.7 %collective-permute-start.3 = (bf16[1280,128]{1,0:T(8,128)(2,1)S(1)}, bf16[1280,128]{1,0:T(8,128)(2,1)}, u32[]{:S(2)}, u32[]{:S(2)}) collective-permute-start(bf16[1280,128]{1,0:T(8,128)(2,1)S(1)} %fusion.4.refs_4_.refs_0_), channel_id=1, source_target_pairs={{0,4},{4,8},{8,12},{12,16},{16,20},{20,24},{24,28},{28,0},{1,5},{5... | collective-permute-start | bytes 983048 | tf_op jit(solution)/shard_map/ppermute | solution.py:204
  10.7 11.8 %collective-permute-start.4 = (bf16[1280,128]{1,0:T(8,128)(2,1)S(1)}, bf16[1280,128]{1,0:T(8,128)(2,1)}, u32[]{:S(2)}, u32[]{:S(2)}) collective-permute-start(bf16[1280,128]{1,0:T(8,128)(2,1)S(1)} %fusion.4.refs_4_.refs_0_), channel_id=1, source_target_pairs={{0,28},{4,0},{8,4},{12,8},{16,12},{20,16},{24,20},{28,24},{1,29},{... | collective-permute-start | bytes 983048 | tf_op jit(solution)/shard_map/ppermute | solution.py:204
  22.4 10.4 %collective-permute-start.5 = (bf16[1280,128]{1,0:T(8,128)(2,1)}, bf16[1280,128]{1,0:T(8,128)(2,1)}, u32[]{:S(2)}, u32[]{:S(2)}) collective-permute-start(bf16[1280,128]{1,0:T(8,128)(2,1)} %collective-permute-done.3), channel_id=1, source_target_pairs={{0,4},{4,8},{8,12},{12,16},{16,20},{20,24},{24,28},{28,0},{1,5},{5... | collective-permute-start | bytes 983048 | tf_op jit(solution)/shard_map/ppermute | solution.py:204
  22.4 10.4 %collective-permute-start.6 = (bf16[1280,128]{1,0:T(8,128)(2,1)}, bf16[1280,128]{1,0:T(8,128)(2,1)}, u32[]{:S(2)}, u32[]{:S(2)}) collective-permute-start(bf16[1280,128]{1,0:T(8,128)(2,1)} %collective-permute-done.4), channel_id=1, source_target_pairs={{0,28},{4,0},{8,4},{12,8},{16,12},{20,16},{24,20},{28,24},{1,29},{... | collective-permute-start | bytes 983048 | tf_op jit(solution)/shard_map/ppermute | solution.py:204
  26.8 17.3 %collective-permute-start.22 = (bf16[2,1280,128]{2,1,0:T(8,128)(2,1)S(1)}, bf16[2,1280,128]{2,1,0:T(8,128)(2,1)S(1)}, u32[]{:S(2)}, u32[]{:S(2)}) collective-permute-start(bf16[2,1280,128]{2,1,0:T(8,128)(2,1)S(1)} %pad_maximum_fusion.refs_5_.refs_1_), channel_id=1, source_target_pairs={{128,129},{129,130},{130,131},{131,128},{132,133},{133,134},{134,1... | collective-permute-start | bytes 1966088 | tf_op jit(solution)/shard_map/ppermute | solution.py:209
  27.5 8.7 %collective-permute-start.19 = (bf16[1280,128]{1,0:T(8,128)(2,1)S(1)}, bf16[1280,128]{1,0:T(8,128)(2,1)S(1)}, u32[]{:S(2)}, u32[]{:S(2)}) collective-permute-start(bf16[1280,128]{1,0:T(8,128)(2,1)S(1)} %fusion.4.refs_4_.refs_0_), channel_id=1, source_target_pairs={{128,129},{129,130},{130,131},{131,128},{132,133},{133,134},{134,1... | collective-permute-start | bytes 983048 | tf_op jit(solution)/shard_map/ppermute | solution.py:209
  28.2 9.7 %collective-permute-start.14 = (bf16[1280,128]{1,0:T(8,128)(2,1)S(1)}, bf16[1280,128]{1,0:T(8,128)(2,1)S(1)}, u32[]{:S(2)}, u32[]{:S(2)}) collective-permute-start(bf16[1280,128]{1,0:T(8,128)(2,1)S(1)} %fusion.4.refs_4_.refs_0_), channel_id=1, source_target_pairs={{128,131},{129,128},{130,129},{131,130},{132,135},{133,132},{134,1... | collective-permute-start | bytes 983048 | tf_op jit(solution)/shard_map/ppermute | solution.py:209
  32.8 9.8 %collective-permute-start.7 = (bf16[1280,128]{1,0:T(8,128)(2,1)}, bf16[1280,128]{1,0:T(8,128)(2,1)S(1)}, u32[]{:S(2)}, u32[]{:S(2)}) collective-permute-start(bf16[1280,128]{1,0:T(8,128)(2,1)} %collective-permute-done.5), channel_id=1, source_target_pairs={{0,4},{4,8},{8,12},{12,16},{16,20},{20,24},{24,28},{28,0},{1,5},{5... | collective-permute-start | bytes 983048 | tf_op jit(solution)/shard_map/ppermute | solution.py:204
  32.8 10.5 %collective-permute-start.8 = (bf16[1280,128]{1,0:T(8,128)(2,1)}, bf16[1280,128]{1,0:T(8,128)(2,1)S(1)}, u32[]{:S(2)}, u32[]{:S(2)}) collective-permute-start(bf16[1280,128]{1,0:T(8,128)(2,1)} %collective-permute-done.6), channel_id=1, source_target_pairs={{0,28},{4,0},{8,4},{12,8},{16,12},{20,16},{24,20},{28,24},{1,29},{... | collective-permute-start | bytes 983048 | tf_op jit(solution)/shard_map/ppermute | solution.py:204
  36.2 27.4 %collective-permute-start = (bf16[128,1024]{1,0:T(8,128)(2,1)S(1)}, bf16[128,1024]{1,0:T(8,128)(2,1)S(1)}, u32[]{:S(2)}, u32[]{:S(2)}) collective-permute-start(bf16[128,1024]{1,0:T(8,128)(2,1)S(1)} %get-tuple-element.20), channel_id=1, source_target_pairs={{0,1},{1,2},{2,3},{3,0},{128,129},{129,130},{130,131},{131,128},{4... | collective-permute-start | bytes 786440 | tf_op jit(solution)/shard_map/ppermute | solution.py:209
  42.6 12.7 %collective-permute-start.25 = (bf16[2,1280,128]{2,1,0:T(8,128)(2,1)S(1)}, bf16[2,1280,128]{2,1,0:T(8,128)(2,1)S(1)}, u32[]{:S(2)}, u32[]{:S(2)}) collective-permute-start(bf16[2,1280,128]{2,1,0:T(8,128)(2,1)S(1)} %pad_maximum_fusion.1.refs_6_.refs_2_), channel_id=1, source_target_pairs={{128,129},{129,130},{130,131},{131,128},{132,133},{133,134},{134,1... | collective-permute-start | bytes 1966088 | tf_op jit(solution)/shard_map/ppermute | solution.py:209
  43.3 12.7 %collective-permute-start.16 = (bf16[2,1280,128]{2,1,0:T(8,128)(2,1)S(1)}, bf16[2,1280,128]{2,1,0:T(8,128)(2,1)S(1)}, u32[]{:S(2)}, u32[]{:S(2)}) collective-permute-start(bf16[2,1280,128]{2,1,0:T(8,128)(2,1)S(1)} %pad_maximum_fusion.1.refs_6_.refs_2_), channel_id=1, source_target_pairs={{128,131},{129,128},{130,129},{131,130},{132,135},{133,132},{134,1... | collective-permute-start | bytes 1966088 | tf_op jit(solution)/shard_map/ppermute | solution.py:209
  44.1 9.7 %collective-permute-start.9 = (bf16[640,128]{1,0:T(8,128)(2,1)S(1)}, bf16[640,128]{1,0:T(8,128)(2,1)S(1)}, u32[]{:S(2)}, u32[]{:S(2)}) collective-permute-start(bf16[640,128]{1,0:T(8,128)(2,1)S(1)} %slice.108), channel_id=1, source_target_pairs={{0,4},{4,8},{8,12},{12,16},{16,20},{20,24},{24,28},{28,0},{1,5},{5... | collective-permute-start | bytes 491528 | tf_op jit(solution)/shard_map/ppermute | solution.py:204
  44.2 10.3 %collective-permute-start.10 = (bf16[640,128]{1,0:T(8,128)(2,1)S(1)}, bf16[640,128]{1,0:T(8,128)(2,1)S(1)}, u32[]{:S(2)}, u32[]{:S(2)}) collective-permute-start(bf16[640,128]{1,0:T(8,128)(2,1)S(1)} %slice.109), channel_id=1, source_target_pairs={{0,28},{4,0},{8,4},{12,8},{16,12},{20,16},{24,20},{28,24},{1,29},{... | collective-permute-start | bytes 491528 | tf_op jit(solution)/shard_map/ppermute | solution.py:204
  53.8 9.1 %collective-permute-start.28 = (bf16[2,1280,128]{2,1,0:T(8,128)(2,1)S(1)}, bf16[2,1280,128]{2,1,0:T(8,128)(2,1)S(1)}, u32[]{:S(2)}, u32[]{:S(2)}) collective-permute-start(bf16[2,1280,128]{2,1,0:T(8,128)(2,1)S(1)} %pad_maximum_fusion.2.refs_7_.refs_3_), channel_id=1, source_target_pairs={{128,129},{129,130},{130,131},{131,128},{132,133},{133,134},{134,1... | collective-permute-start | bytes 1966088 | tf_op jit(solution)/shard_map/ppermute | solution.py:209
  54.6 16.2 %collective-permute-start.17 = (bf16[2,1280,128]{2,1,0:T(8,128)(2,1)S(1)}, bf16[2,1280,128]{2,1,0:T(8,128)(2,1)S(1)}, u32[]{:S(2)}, u32[]{:S(2)}) collective-permute-start(bf16[2,1280,128]{2,1,0:T(8,128)(2,1)S(1)} %pad_maximum_fusion.2.refs_7_.refs_3_), channel_id=1, source_target_pairs={{128,131},{129,128},{130,129},{131,130},{132,135},{133,132},{134,1... | collective-permute-start | bytes 1966088 | tf_op jit(solution)/shard_map/ppermute | solution.py:209
  56.8 9.7 %collective-permute-start.1 = (bf16[128,1024]{1,0:T(8,128)(2,1)S(1)}, bf16[128,1024]{1,0:T(8,128)(2,1)S(1)}, u32[]{:S(2)}, u32[]{:S(2)}) collective-permute-start(bf16[128,1024]{1,0:T(8,128)(2,1)S(1)} %get-tuple-element.19), channel_id=1, source_target_pairs={{0,2},{1,3},{2,0},{3,1},{128,130},{129,131},{130,128},{131,129},{4... | collective-permute-start | bytes 786440 | tf_op jit(solution)/shard_map/ppermute | solution.py:209
  62.9 8.6 %collective-permute-start.20 = (bf16[640,128]{1,0:T(8,128)(2,1)S(1)}, bf16[640,128]{1,0:T(8,128)(2,1)S(1)}, u32[]{:S(2)}, u32[]{:S(2)}) collective-permute-start(bf16[640,128]{1,0:T(8,128)(2,1)S(1)} %slice.114), channel_id=1, source_target_pairs={{128,129},{129,130},{130,131},{131,128},{132,133},{133,134},{134,1... | collective-permute-start | bytes 491528 | tf_op jit(solution)/shard_map/ppermute | solution.py:209
  86.8 9.8 %collective-permute-start.34 = (bf16[32,4096]{1,0:T(8,128)(2,1)S(1)}, bf16[32,4096]{1,0:T(8,128)(2,1)S(1)}, u32[]{:S(2)}, u32[]{:S(2)}) collective-permute-start(bf16[32,4096]{1,0:T(8,128)(2,1)S(1)} %get-tuple-element.17), channel_id=1, source_target_pairs={{128,160},{160,192},{192,224},{224,128},{129,161},{161,193},{193,2... | collective-permute-start | bytes 786440 | tf_op jit(solution)/shard_map/ppermute | solution.py:214
  87.4 11.8 %collective-permute-start.35 = (bf16[32,4096]{1,0:T(8,128)(2,1)S(1)}, bf16[32,4096]{1,0:T(8,128)(2,1)S(1)}, u32[]{:S(2)}, u32[]{:S(2)}) collective-permute-start(bf16[32,4096]{1,0:T(8,128)(2,1)S(1)} %get-tuple-element.16), channel_id=1, source_target_pairs={{128,192},{160,224},{192,128},{224,160},{129,193},{161,225},{193,1... | collective-permute-start | bytes 786440 | tf_op jit(solution)/shard_map/ppermute | solution.py:214
  88.2 11.1 %collective-permute-start.36 = (bf16[32,4096]{1,0:T(8,128)(2,1)S(1)}, bf16[32,4096]{1,0:T(8,128)(2,1)S(1)}, u32[]{:S(2)}, u32[]{:S(2)}) collective-permute-start(bf16[32,4096]{1,0:T(8,128)(2,1)S(1)} %get-tuple-element.15), channel_id=1, source_target_pairs={{128,224},{160,128},{192,160},{224,192},{129,225},{161,129},{193,1... | collective-permute-start | bytes 786440 | tf_op jit(solution)/shard_map/ppermute | solution.py:214
  90.0 18.4 %collective-permute-start.11 = (bf16[128,1280]{1,0:T(8,128)(2,1)}, bf16[128,1280]{1,0:T(8,128)(2,1)}, u32[]{:S(2)}, u32[]{:S(2)}) collective-permute-start(bf16[128,1280]{1,0:T(8,128)(2,1)} %get-tuple-element.12), channel_id=1, source_target_pairs={{0,3},{1,0},{2,1},{3,2},{4,7},{5,4},{6,5},{7,6},{8,11},{9,8},{10,9... | collective-permute-start | bytes 983048 | tf_op jit(solution)/shard_map/ppermute | solution.py:209
  94.5 15.2 %collective-permute-start.12 = (bf16[128,1280]{1,0:T(8,128)(2,1)}, bf16[128,1280]{1,0:T(8,128)(2,1)}, u32[]{:S(2)}, u32[]{:S(2)}) collective-permute-start(bf16[128,1280]{1,0:T(8,128)(2,1)} %get-tuple-element.14), channel_id=1, source_target_pairs={{0,2},{1,3},{2,0},{3,1},{4,6},{5,7},{6,4},{7,5},{8,10},{9,11},{10,... | collective-permute-start | bytes 983048 | tf_op jit(solution)/shard_map/ppermute | solution.py:209
  96.6 16.5 %collective-permute-start.13 = (bf16[128,1280]{1,0:T(8,128)(2,1)}, bf16[128,1280]{1,0:T(8,128)(2,1)}, u32[]{:S(2)}, u32[]{:S(2)}) collective-permute-start(bf16[128,1280]{1,0:T(8,128)(2,1)} %get-tuple-element.13), channel_id=1, source_target_pairs={{0,1},{1,2},{2,3},{3,0},{4,5},{5,6},{6,7},{7,4},{8,9},{9,10},{10,1... | collective-permute-start | bytes 983048 | tf_op jit(solution)/shard_map/ppermute | solution.py:209
  100.5 50.8 %collective-permute-start.37 = (bf16[32,4096]{1,0:T(8,128)(2,1)}, bf16[32,4096]{1,0:T(8,128)(2,1)S(1)}, u32[]{:S(2)}, u32[]{:S(2)}) collective-permute-start(bf16[32,4096]{1,0:T(8,128)(2,1)} %shard_map.76), channel_id=1, source_target_pairs={{128,0},{160,32},{192,64},{224,96},{129,1},{161,33},{193,65},{225,... | collective-permute-start | bytes 786440 | tf_op jit(solution)/shard_map/ppermute | solution.py:218
  101.8 54.9 %collective-permute-start.38 = (bf16[32,4096]{1,0:T(8,128)(2,1)}, bf16[32,4096]{1,0:T(8,128)(2,1)S(1)}, u32[]{:S(2)}, u32[]{:S(2)}) collective-permute-start(bf16[32,4096]{1,0:T(8,128)(2,1)} %shard_map.76), channel_id=1, source_target_pairs={{128,32},{160,64},{192,96},{224,0},{129,33},{161,65},{193,97},{225... | collective-permute-start | bytes 786440 | tf_op jit(solution)/shard_map/ppermute | solution.py:218
  108.4 55.4 %collective-permute-start.39 = (bf16[32,4096]{1,0:T(8,128)(2,1)}, bf16[32,4096]{1,0:T(8,128)(2,1)S(1)}, u32[]{:S(2)}, u32[]{:S(2)}) collective-permute-start(bf16[32,4096]{1,0:T(8,128)(2,1)} %shard_map.76), channel_id=1, source_target_pairs={{128,64},{160,96},{192,0},{224,32},{129,65},{161,97},{193,1},{225,... | collective-permute-start | bytes 786440 | tf_op jit(solution)/shard_map/ppermute | solution.py:218
  109.7 56.4 %collective-permute-start.40 = (bf16[32,4096]{1,0:T(8,128)(2,1)}, bf16[32,4096]{1,0:T(8,128)(2,1)S(1)}, u32[]{:S(2)}, u32[]{:S(2)}) collective-permute-start(bf16[32,4096]{1,0:T(8,128)(2,1)} %shard_map.76), channel_id=1, source_target_pairs={{128,96},{160,0},{192,32},{224,64},{129,97},{161,1},{193,33},{225,... | collective-permute-start | bytes 786440 | tf_op jit(solution)/shard_map/ppermute | solution.py:218
  113.1 53.0 %collective-permute-start.41 = (bf16[128,1280]{1,0:T(8,128)(2,1)S(1)}, bf16[128,1280]{1,0:T(8,128)(2,1)S(1)}, u32[]{:S(2)}, u32[]{:S(2)}) collective-permute-start(bf16[128,1280]{1,0:T(8,128)(2,1)S(1)} %get-tuple-element.11), channel_id=1, source_target_pairs={{0,3},{1,0},{2,1},{3,2},{128,131},{129,128},{130,129},{131,130},{4... | collective-permute-start | bytes 983048 | tf_op jit(solution)/shard_map/ppermute | solution.py:209
  151.3 14.8 %collective-permute-start.42 = (bf16[128,1280]{1,0:T(8,128)(2,1)S(1)}, bf16[128,1280]{1,0:T(8,128)(2,1)S(1)}, u32[]{:S(2)}, u32[]{:S(2)}) collective-permute-start(bf16[128,1280]{1,0:T(8,128)(2,1)S(1)} %get-tuple-element.10), channel_id=1, source_target_pairs={{0,2},{1,3},{2,0},{3,1},{128,130},{129,131},{130,128},{131,129},{4... | collective-permute-start | bytes 983048 | tf_op jit(solution)/shard_map/ppermute | solution.py:209
  156.7 9.5 %collective-permute-start.43 = (bf16[128,1280]{1,0:T(8,128)(2,1)S(1)}, bf16[128,1280]{1,0:T(8,128)(2,1)S(1)}, u32[]{:S(2)}, u32[]{:S(2)}) collective-permute-start(bf16[128,1280]{1,0:T(8,128)(2,1)S(1)} %get-tuple-element.9), channel_id=1, source_target_pairs={{0,1},{1,2},{2,3},{3,0},{128,129},{129,130},{130,131},{131,128},{4... | collective-permute-start | bytes 983048 | tf_op jit(solution)/shard_map/ppermute | solution.py:209
  (35 other events, 464.3 us)
Sparse Core Ops, SparseCore 0:
  29.0 49.3 all-gather.2

commit v3 on v2

v3 whole, which is shorter than its diff:
```python
import functools
import math

import jax
import jax.numpy as jnp
from jax import lax
from jax.experimental import pallas as pl
from jax.experimental.pallas import tpu as pltpu
from jax.sharding import Mesh
from jax.sharding import PartitionSpec as P

HD = 128
QH = 8
NY = 4
NX = 4
NZ = 8

F32 = jnp.float32
BF16 = jnp.bfloat16
VMEM = pl.BlockSpec(memory_space=pltpu.VMEM)


def dot_nn(a, b):
    return lax.dot_general(a, b, (((1,), (0,)), ((), ())), preferred_element_type=F32)


def dot_nt(a, b):
    return lax.dot_general(a, b, (((1,), (1,)), ((), ())), preferred_element_type=F32)


def dot_tn(a, b):
    return lax.dot_general(a, b, (((0,), (0,)), ((), ())), preferred_element_type=F32)


def call(kernel, outs, args, flops, vmem=20):
    return pl.pallas_call(
        kernel,
        out_shape=outs,
        in_specs=[VMEM] * len(args),
        out_specs=jax.tree.map(lambda _: VMEM, outs),
        compiler_params=pltpu.CompilerParams(vmem_limit_bytes=vmem * 1024 * 1024),
        cost_estimate=pl.CostEstimate(flops=flops, bytes_accessed=100000, transcendentals=0),
    )(*args)


def norm_kernel(inputs_ref, gain_ref, hidden_ref):
    y_index = lax.axis_index("y")
    values = inputs_ref[...].astype(F32)
    factor = lax.rsqrt(jnp.mean(values * values, axis=-1, keepdims=True) + 1e-05)
    hidden = (values * factor * gain_ref[...]).astype(BF16)
    for y in range(NY):
        for z in range(NZ):
            block = hidden[:, (z * NY + y) * HD : (z * NY + y + 1) * HD]
            hidden_ref[(y - y_index + NY) % NY, :, z * HD : (z + 1) * HD] = block


def attention_back(packed_of, grads_of):
    factor = 1.0 / math.sqrt(HD)
    queries = jnp.concatenate([packed_of(h) for h in range(QH)], axis=0)
    grads = jnp.concatenate([grads_of(h) for h in range(QH)], axis=0)
    keys, values = packed_of(QH), packed_of(QH + 1)
    length = keys.shape[0]
    scores = dot_nt(queries, keys) * factor
    rows = lax.broadcasted_iota(jnp.int32, scores.shape, 0) % length
    cols = lax.broadcasted_iota(jnp.int32, scores.shape, 1)
    scores = jnp.where(cols <= rows, scores, -1000000000.0)
    top = jnp.max(scores, axis=-1, keepdims=True)
    raised = jnp.exp(scores - top)
    weights = raised / jnp.sum(raised, axis=-1, keepdims=True)
    grad_weights = dot_nt(grads, values)
    inner = jnp.sum(grad_weights * weights, axis=-1, keepdims=True)
    grad_scores = (weights * (grad_weights - inner) * factor).astype(BF16)
    grad_queries = dot_nn(grad_scores, keys)
    heads = [grad_queries[h * length : (h + 1) * length] for h in range(QH)]
    return heads + [dot_tn(grad_scores, queries), dot_tn(weights.astype(BF16), grads)]


def slab_product(hidden_ref, slab_ref):
    total = None
    for z in range(0, NZ, 2):
        pair = jnp.concatenate([slab_ref[z], slab_ref[z + 1]], axis=1)
        term = dot_nt(hidden_ref[:, z * HD : (z + 2) * HD], pair)
        total = term if total is None else total + term
    return total.astype(BF16)


def packed_kernel(*refs):
    hidden, slab_ref, out_ref = refs[:NY], refs[NY], refs[-1]
    for k in range(NY):
        out_ref[k] = slab_product(hidden[k], slab_ref)


def sign_kernel(*refs):
    hidden, slab_ref, out_ref = refs[:NY], refs[NY], refs[-1]
    y_index = lax.axis_index("y")
    for k in range(NY):
        out_ref[(y_index - k + NY) % NY] = slab_product(hidden[k], slab_ref)


def upper_kernel(grad_ref, *refs):
    parts, packed_ref, grad_packed_ref = refs[:-2], refs[-2], refs[-1]
    packed = parts[0][...].astype(F32)
    for part in parts[1:]:
        packed = packed + part[...].astype(F32)
    packed_ref[...] = packed.astype(BF16)
    columns = attention_back(
        lambda h: packed_ref[:, h * HD : (h + 1) * HD],
        lambda h: grad_ref[:, h * HD : (h + 1) * HD],
    )
    for h, column in enumerate(columns):
        grad_packed_ref[:, h * HD : (h + 1) * HD] = column.astype(BF16)


def back_kernel(*refs):
    rows, slab_ref, out_ref = refs[:NY], refs[NY], refs[-1]
    y_index = lax.axis_index("y")
    chunk = out_ref.shape[1]
    for k in range(NY):
        for z in range(0, NZ, 2):
            pair = jnp.concatenate([slab_ref[z], slab_ref[z + 1]], axis=1)
            term = dot_nn(rows[k][...], pair).astype(BF16)
            for c in range(NX):
                place = c * NY + (y_index - k + NY) % NY
                out_ref[place, :, z * HD : (z + 2) * HD] = term[c * chunk : (c + 1) * chunk]


def norm_back_kernel(inputs_ref, gain_ref, cotangent_ref, terms_ref, out_ref):
    x_index = lax.axis_index("tensor")
    chunk, width = out_ref.shape
    rows = pl.ds(pl.multiple_of(x_index * chunk, chunk), chunk)
    values = inputs_ref[rows, :].astype(F32)
    factor = lax.rsqrt(jnp.mean(values * values, axis=-1, keepdims=True) + 1e-05)
    normed = values * factor
    blocks = []
    for z in range(NZ):
        for y in range(NY):
            at = slice(z * HD, (z + 1) * HD)
            block = terms_ref[y, :, at].astype(F32)
            for x in range(1, NX):
                block = block + terms_ref[x * NY + y, :, at].astype(F32)
            blocks.append(block)
    grad = jnp.concatenate(blocks, axis=1) * gain_ref[...]
    mean = jnp.sum(grad * normed, axis=-1, keepdims=True) * (1.0 / width)
    out_ref[...] = (cotangent_ref[rows, :].astype(F32) + factor * (grad - normed * mean)).astype(BF16)


def lower_kernel(count, packed_ref, weight_ref, upper_ref, *refs):
    *arrived, projected_ref, out_ref, rows_ref, mixed_ref = refs
    x_index = lax.axis_index("tensor")
    pipe_index = lax.axis_index("pipe")
    chunk = arrived[0].shape[0]
    for j in range(NX):
        place = pl.multiple_of(((x_index - j + NX) % NX) * chunk, chunk)
        rows_ref[pl.ds(place, chunk), :] = arrived[j][...]
    mixed_ref[...] = jnp.zeros_like(mixed_ref)
    depth = 512

    def step(i, _):
        at = pl.ds(pl.multiple_of(i * depth, depth), depth)
        mixed_ref[...] += dot_nn(rows_ref[:, at], weight_ref[at, :])
        return 0

    lax.fori_loop(0, rows_ref.shape[1] // depth, step, 0)
    columns = attention_back(
        lambda h: packed_ref[:, h * HD : (h + 1) * HD],
        lambda h: mixed_ref[:, h * HD : (h + 1) * HD].astype(BF16),
    )
    for h, column in enumerate(columns):
        at = slice(h * HD, (h + 1) * HD)
        lower = column.astype(BF16).astype(F32)
        kept = jnp.where(pipe_index == 1, upper_ref[:, at].astype(F32), lower)
        product = projected_ref[:, at].astype(F32)
        out_ref[:, at] = jnp.sum(kept * product, axis=0, keepdims=True) * (1.0 / count)


def send_y(value, steps, pipes=(0, 1)):
    pairs = [(NY * p + i, NY * p + (i + steps) % NY) for p in pipes for i in range(NY)]
    return lax.ppermute(value, ("pipe", "y"), pairs)


def send_down(value, steps):
    return lax.ppermute(value, ("pipe", "tensor"), [(NX + i, (i + steps) % NX) for i in range(NX)])


def local(section_input, norm_gain, cotangent, qkv_base, qkv_sign, qkv_scale, out_base):
    inputs = section_input[0]
    tokens, width = inputs.shape
    chunk = tokens // NX
    weight_out = out_base[0]
    sign = qkv_sign[0]
    rows = sign.shape[0]
    weight = (qkv_base[0].astype(F32) + qkv_scale[0][:, None] * sign.astype(F32)).astype(BF16)
    weight_slab = lax.all_gather(weight, "z", axis=0, tiled=False)
    sign_slab = lax.all_gather(sign, "z", axis=0, tiled=False)

    hidden = call(
        norm_kernel, jax.ShapeDtypeStruct((NY, tokens, NZ * HD), BF16), (inputs, norm_gain), 10**7
    )
    hidden_slab = [hidden[0]] + [send_y(hidden[k], k) for k in range(1, NY)]
    grad_mixed = dot_nn(cotangent, weight_out).astype(BF16)

    flops = 2 * tokens * rows * width
    by_y = jax.ShapeDtypeStruct((NY, tokens, rows), BF16)
    packed_rows = jax.ShapeDtypeStruct((tokens, rows), BF16)
    partial = call(packed_kernel, by_y, (*hidden_slab, weight_slab), flops)
    parts = [partial[0]] + [send_y(partial[k], -k) for k in range(1, NY)]
    packed, grad_upper = call(upper_kernel, (packed_rows, packed_rows), (grad_mixed, *parts), 10**8)

    signed = call(sign_kernel, by_y, (*hidden_slab, sign_slab), flops)
    projected = lax.psum_scatter(signed, "y", scatter_dimension=0)

    slab_rows = [grad_upper] + [send_y(grad_upper, k, (1,)) for k in range(1, NY)]
    back = call(
        back_kernel,
        jax.ShapeDtypeStruct((NX * NY, chunk, NZ * HD), BF16),
        (*slab_rows, weight_slab),
        flops,
    )
    terms = lax.all_to_all(back, ("tensor", "y"), 0, 0)
    backward = call(
        norm_back_kernel,
        jax.ShapeDtypeStruct((chunk, width), BF16),
        (inputs, norm_gain, cotangent, terms),
        10**6,
    )
    arrived = [send_down(backward, j) for j in range(NX)]
    args = (packed, weight_out, grad_upper, *arrived, projected)
    result = pl.pallas_call(
        functools.partial(lower_kernel, tokens * NZ * NY),
        out_shape=jax.ShapeDtypeStruct((1, rows), F32),
        in_specs=[VMEM] * len(args),
        out_specs=VMEM,
        scratch_shapes=[pltpu.VMEM((tokens, width), BF16), pltpu.VMEM((tokens, QH * HD), F32)],
        compiler_params=pltpu.CompilerParams(vmem_limit_bytes=28 * 1024 * 1024),
        cost_estimate=pl.CostEstimate(flops=flops, bytes_accessed=100000, transcendentals=131072),
    )(*args)
    return lax.psum(lax.psum(result, "y"), "z")


def solution(mesh):
    sizes = mesh.devices.shape
    fine = Mesh(mesh.devices.reshape(sizes[0], sizes[1], NZ, NY), ("pipe", "tensor", "z", "y"))
    dp = ("z", "y")
    placed = (
        P("pipe", dp, None),
        P("pipe", None),
        P(dp, None),
        P("pipe", "tensor", dp),
        P("pipe", "tensor", dp),
        P("pipe", "tensor"),
        P("pipe", None, "tensor"),
    )
    return jax.shard_map(
        local, mesh=fine, in_specs=placed, out_specs=P("pipe", "tensor"), check_vma=False
    )
```

time: 208 us -> 209 us (level)
  starting transfers between devices: 55.7 us -> 18 us
  waiting for transfers between devices: 77.3 us -> 98.1 us
  blocking collectives: 26.4 us -> 46.3 us
  matrix products: 1.34 us -> 4.85 us
  Pallas kernels: 18.9 us -> 15.4 us
  local copies, waits for them, and re-layouts: 6.61 us -> 9.96 us
  other arithmetic: 5.92 us -> 2.75 us
    all_gather x1 -> x2, waiting for transfers between devices: 0.02 us -> 61.8 us  [the longest x1 36.4 us: local(): weight_slab = lax.all_gather(weight, 'z', axis=0, tiled=False)]
    ppermute x4, waiting for transfers between devices: 50 us -> 11 us  [send_down(): lax.ppermute(value, ('pipe', 'tensor'), [(NX + i, (i + steps) % NX) for i...]
    all_to_all x0 -> x1, blocking collectives: none -> 21.3 us  [local(): terms = lax.all_to_all(back, ('tensor', 'y'), 0, 0)]
    ppermute x11 -> x0, waiting for transfers between devices: 20 us -> none  [the longest x8 20 us: send_z(): return lax.ppermute(value, 'z', [(i, (i + steps) % NZ) for i in range(NZ)])]
    ppermute x29 -> x9, starting transfers between devices: 32.5 us -> 12.8 us  [send_y(): return lax.ppermute(value, ('pipe', 'y'), pairs)]
    ppermute x11 -> x0, starting transfers between devices: 18 us -> none  [the longest x8 15.9 us: send_z(): return lax.ppermute(value, 'z', [(i, (i + steps) % NZ) for i in range(NZ)])]
    ppermute x29 -> x9, waiting for transfers between devices: 7.28 us -> 24.5 us  [send_y(): return lax.ppermute(value, ('pipe', 'y'), pairs)]
    pallas_call x1 -> x0, Pallas kernels: 6.54 us -> none  [local(): grad_upper, back = upper(hidden, grad_mixed, *pieces)]
  transfers between devices with their start and end apart: 45 -> 16, of which waited for: 11 -> 10; matrix products, arithmetic and copies ran while one was open for 3% -> 4% of each run, Pallas kernels for 7% -> 6%
where the time goes in v3:
time: 209 us
  waiting for transfers between devices  98.1 us (47%)
  blocking collectives  46.3 us (22%)
  starting transfers between devices  18 us (9%)
  Pallas kernels  15.4 us (7%)
  between operations  13.3 us (6%)
  local copies, waits for them, and re-layouts  9.96 us (5%)
  matrix products  4.85 us (2%)
  other arithmetic  2.75 us (1%)
    all_gather x1, waiting for transfers between devices, local(): weight_slab = lax.all_gather(weight, 'z', axis=0, tiled=False)  36.4 us
    all_gather x1, waiting for transfers between devices, local(): sign_slab = lax.all_gather(sign, 'z', axis=0, tiled=False)  25.4 us
    psum x2, blocking collectives, local(): return lax.psum(lax.psum(result, 'y'), 'z')  25 us
    ppermute x9, waiting for transfers between devices, send_y(): return lax.ppermute(value, ('pipe', 'y'), pairs)  24.5 us
    all_to_all x1, blocking collectives, local(): terms = lax.all_to_all(back, ('tensor', 'y'), 0, 0)  21.3 us
    ppermute x9, starting transfers between devices, send_y(): return lax.ppermute(value, ('pipe', 'y'), pairs)  12.8 us
    pallas_call x6, Pallas kernels, call(): pl.pallas_call(kernel, out_shape=outs, in_specs=[VMEM] * len(args), out_s...  11.8 us
    ppermute x4, waiting for transfers between devices, send_down(): lax.ppermute(value, ('pipe', 'tensor'), [(NX + i, (i + steps) % NX) for i...  11 us
  transfers between devices with their start and end apart: 16, of which 10 were waited for; matrix products, arithmetic and copies ran while one was open for 4% of the time, Pallas kernels for 6%

profile of v3, /device:TPU:2, one launch (start us, length us, event | category | flops | bytes accessed | tf_op | source)
XLA Modules:
  0.0 208.7 jit_solution(4732396346265748734)
XLA Ops:
  8.0 2.0 add_convert_fusion
  10.1 1.2 copy-done.4
  12.9 1.7 collective-permute-start
  14.5 2.9 %collective-permute-start.1 = (bf16[128,1024]{1,0:T(8,128)(2,1)S(1)}, bf16[128,1024]{1,0:T(8,128)(2,1)S(1)}, u32[]{:S(2)}, u32[]{:S(2)}) collective-permute-start(bf16[128,1024]{1,0:T(8,128)(2,1)S(1)} %get-tuple-element.14), channel_id=1, source_target_pairs={{0,2},{1,3},{2,0},{3,1},{128,130},{129,131},{130,128},{131,129},{4... | collective-permute-start | bytes 786440 | tf_op jit(solution)/shard_map/ppermute | solution.py:178
  17.4 1.3 collective-permute-start.2
  18.8 3.5 %collective-permute-done.refs_1_ = bf16[128,1024]{1,0:T(8,128)(2,1)S(1)} collective-permute-done((bf16[128,1024]{1,0:T(8,128)(2,1)S(1)}, bf16[128,1024]{1,0:T(8,128)(2,1)S(1)}, u32[]{:S(2)}, u32[]{:S(2)}) %collective-permute-start) | collective-permute-done | bytes 262176 | tf_op jit(solution)/shard_map/ppermute | solution.py:178
  22.3 6.8 %collective-permute-done.1.refs_2_ = bf16[128,1024]{1,0:T(8,128)(2,1)S(1)} collective-permute-done((bf16[128,1024]{1,0:T(8,128)(2,1)S(1)}, bf16[128,1024]{1,0:T(8,128)(2,1)S(1)}, u32[]{:S(2)}, u32[]{:S(2)}) %collective-permute-start.1) | collective-permute-done | bytes 262176 | tf_op jit(solution)/shard_map/ppermute | solution.py:178
  29.1 25.4 %all-gather.5.cloned.1.call-done.refs_4_ = bf16[8,1280,128]{2,1,0:T(8,128)(2,1)} async-done(((bf16[1,1280,128]{2,1,0:T(8,128)(2,1)}), bf16[8,1280,128]{2,1,0:T(8,128)(2,1)}) %all-gather.5.cloned.1.call-update) | async-done | bytes 2621456 | tf_op jit(solution)/shard_map/all_gather | solution.py:194
  54.4 1.7 copy-done.6
  56.2 4.5 %shard_map.81 = bf16[4,128,1280]{2,1,0:T(8,128)(2,1)} custom-call(bf16[128,1024]{1,0:T(8,128)(2,1)S(1)} %get-tuple-element.16.refs_0_, bf16[128,1024]{1,0:T(8,128)(2,1)S(1)} %collective-permute-done.refs_1_, bf16[128,1024]{1,0:T(8,128)(2,1)S(1)} %collective-permute-done.1.refs_2_, bf16[128,1024]{1,0:T(8,128)(2,1)S(1)} %collective-permute-done.2.refs_3_, ...), custom_call_target="tpu_custom_call" | custom-call | flops 1342177280 | bytes 100000 | tf_op jit(solution)/shard_map/pallas_call | solution.py:36
  60.7 36.4 %all-gather.3.cloned.1.call-done.refs_4_ = bf16[8,1280,128]{2,1,0:T(8,128)(2,1)} async-done(((bf16[1,1280,128]{2,1,0:T(8,128)(2,1)}), bf16[8,1280,128]{2,1,0:T(8,128)(2,1)}) %all-gather.3.cloned.1.call-update) | async-done | bytes 2621456 | tf_op jit(solution)/shard_map/all_gather | solution.py:193
  97.2 1.7 copy-done.1
  98.9 3.5 %shard_map.77 = bf16[4,128,1280]{2,1,0:T(8,128)(2,1)S(1)} custom-call(bf16[128,1024]{1,0:T(8,128)(2,1)S(1)} %get-tuple-element.16.refs_0_, bf16[128,1024]{1,0:T(8,128)(2,1)S(1)} %collective-permute-done.refs_1_, bf16[128,1024]{1,0:T(8,128)(2,1)S(1)} %collective-permute-done.1.refs_2_, bf16[128,1024]{1,0:T(8,128)(2,1)S(1)} %collective-permute-done.2.refs_3_, ...), custom_call_target="tpu_custom_call" | custom-call | flops 1342177280 | bytes 100000 | tf_op jit(solution)/shard_map/pallas_call | solution.py:36
  102.5 2.8 %collective-permute-start.3 = (bf16[128,1280]{1,0:T(8,128)(2,1)S(1)}, bf16[128,1280]{1,0:T(8,128)(2,1)S(1)}, u32[]{:S(2)}, u32[]{:S(2)}) collective-permute-start(bf16[128,1280]{1,0:T(8,128)(2,1)S(1)} %get-tuple-element.11), channel_id=1, source_target_pairs={{0,3},{1,0},{2,1},{3,2},{128,131},{129,128},{130,129},{131,130},{4... | collective-permute-start | bytes 983048 | tf_op jit(solution)/shard_map/ppermute | solution.py:178
  107.0 4.9 %convolution_convert_fusion.grad_ref = bf16[128,1024]{1,0:T(8,128)(2,1)S(1)} fusion(bf16[128,4096]{1,0:T(8,128)(2,1)S(1)} %copy-done.3, bf16[1,4096,1024]{2,1,0:T(8,128)(2,1)} %param.13), kind=kOutput, calls=%fused_computation | convolution fusion | flops 1073872896 | bytes 9699328 | tf_op jit(solution)/shard_map/dot_general | solution.py:24
  111.8 7.6 %collective-permute-done.3.refs_1_ = bf16[128,1280]{1,0:T(8,128)(2,1)S(1)} collective-permute-done((bf16[128,1280]{1,0:T(8,128)(2,1)S(1)}, bf16[128,1280]{1,0:T(8,128)(2,1)S(1)}, u32[]{:S(2)}, u32[]{:S(2)}) %collective-permute-start.3) | collective-permute-done | bytes 327712 | tf_op jit(solution)/shard_map/ppermute | solution.py:178
  119.4 1.5 collective-permute-done.4.refs_2_
  120.9 5.2 %collective-permute-done.5.refs_3_ = bf16[128,1280]{1,0:T(8,128)(2,1)S(1)} collective-permute-done((bf16[128,1280]{1,0:T(8,128)(2,1)S(1)}, bf16[128,1280]{1,0:T(8,128)(2,1)S(1)}, u32[]{:S(2)}, u32[]{:S(2)}) %collective-permute-start.5) | collective-permute-done | bytes 327712 | tf_op jit(solution)/shard_map/ppermute | solution.py:178
  126.1 1.1 shard_map.78
  129.6 1.6 shard_map.79
  131.2 21.3 %all_to_all.5.terms_ref = bf16[16,32,1024]{2,1,0:T(8,128)(2,1)S(1)} all-to-all(bf16[16,32,1024]{2,1,0:T(8,128)(2,1)S(1)} %shard_map.79), channel_id=1, replica_groups=mesh['pipe'=2,'tensor'=4,'z'=8,'y'=4] {'tensor','y'}, dimensions={0} | all-to-all | bytes 2097152 | tf_op jit(solution)/shard_map/all_to_all | solution.py:219
  152.9 1.3 collective-permute-start.10
  154.2 1.3 collective-permute-start.11
  155.5 1.3 collective-permute-start.12
  156.8 1.3 collective-permute-start.9
  158.1 6.9 %collective-permute-done.10.refs_1_ = bf16[32,4096]{1,0:T(8,128)(2,1)S(1)} collective-permute-done((bf16[32,4096]{1,0:T(8,128)(2,1)S(1)}, bf16[32,4096]{1,0:T(8,128)(2,1)S(1)}, u32[]{:S(2)}, u32[]{:S(2)}) %collective-permute-start.10) | collective-permute-done | bytes 262176 | tf_op jit(solution)/shard_map/ppermute | solution.py:182
  165.1 1.4 collective-permute-done.11.refs_2_
  166.4 2.7 %collective-permute-done.12.refs_3_ = bf16[32,4096]{1,0:T(8,128)(2,1)S(1)} collective-permute-done((bf16[32,4096]{1,0:T(8,128)(2,1)S(1)}, bf16[32,4096]{1,0:T(8,128)(2,1)S(1)}, u32[]{:S(2)}, u32[]{:S(2)}) %collective-permute-start.12) | collective-permute-done | bytes 262176 | tf_op jit(solution)/shard_map/ppermute | solution.py:182
  169.1 3.4 %copy-done = bf16[1,4096,1024]{2,1,0:T(8,128)(2,1)S(1)} copy-done((bf16[1,4096,1024]{2,1,0:T(8,128)(2,1)S(1)}, bf16[1,4096,1024]{2,1,0:T(8,128)(2,1)}, u32[]{:S(2)}) %copy-start) | copy-done | bytes 8388632
  173.5 3.6 %shard_map.82 = f32[1,1280]{1,0:T(1,128)S(1)} custom-call(bf16[128,1280]{1,0:T(8,128)(2,1)S(1)} %get-tuple-element.7.packed_ref, bf16[4096,1024]{1,0:T(8,128)(2,1)S(1)} %bitcast.22, bf16[128,1280]{1,0:T(8,128)(2,1)S(1)} %get-tuple-element.8.refs_0_.upper_ref, bf16[32,4096]{1,0:T(8,128)(2,1)S(1)} %collective-permute-done.9.refs_0_, ...), custom_call_target="tpu_custom_call" | custom-call | flops 1342177280 | bytes 100000 | tf_op jit(solution)/shard_map/pallas_call | solution.py:228
  177.1 8.5 %psum.14 = f32[1,1280]{1,0:T(1,128)S(1)} all-reduce(f32[1,1280]{1,0:T(1,128)S(1)} %shard_map.82), channel_id=1, replica_groups=mesh['pipe'=2,'tensor'=4,'z'=8,'y'=4] {'y'}, use_global_device_ids=true, to_apply=%region_1.0 | all-reduce | flops 1280 | bytes 10240 | tf_op jit(solution)/shard_map/psum | solution.py:237
  185.6 16.5 %psum.15 = f32[1,1280]{1,0:T(1,128)} all-reduce(f32[1,1280]{1,0:T(1,128)S(1)} %psum.14), channel_id=1, replica_groups=mesh['pipe'=2,'tensor'=4,'z'=8,'y'=4] {'z'}, use_global_device_ids=true, to_apply=%region_2.0 | all-reduce | flops 1280 | bytes 10240 | tf_op jit(solution)/shard_map/psum | solution.py:237
  (38 shorter events, 8.6 us)
Async XLA Ops:
  6.5 47.9 %all-gather.5.cloned.1.call-start = ((), (), s32[]{:S(2)}) async-start(), calls=%async_computation.3 | async-start | bytes 2949120 | tf_op jit(solution)/shard_map/all_gather | solution.py:194
  7.3 89.9 %all-gather.3.cloned.1.call-start = ((), (), s32[]{:S(2)}) async-start(), calls=%async_computation.2 | async-start | bytes 2949120 | tf_op jit(solution)/shard_map/all_gather | solution.py:193
  10.1 159.0 %reduce-scatter.2.cloned.1.call-start = ((), (), s32[]{:S(2)}) async-start(), calls=%async_computation.4 | async-start | bytes 1638400 | tf_op jit(solution)/shard_map/reduce_scatter | solution.py:210
  10.1 1.2 copy-start.4
  11.4 0.7 copy-start.8
  12.9 9.4 %collective-permute-start = (bf16[128,1024]{1,0:T(8,128)(2,1)S(1)}, bf16[128,1024]{1,0:T(8,128)(2,1)S(1)}, u32[]{:S(2)}, u32[]{:S(2)}) collective-permute-start(bf16[128,1024]{1,0:T(8,128)(2,1)S(1)} %get-tuple-element.15), channel_id=1, source_target_pairs={{0,1},{1,2},{2,3},{3,0},{128,129},{129,130},{130,131},{131,128},{4... | collective-permute-start | bytes 786440 | tf_op jit(solution)/shard_map/ppermute | solution.py:178
  14.5 14.5 %collective-permute-start.1 = (bf16[128,1024]{1,0:T(8,128)(2,1)S(1)}, bf16[128,1024]{1,0:T(8,128)(2,1)S(1)}, u32[]{:S(2)}, u32[]{:S(2)}) collective-permute-start(bf16[128,1024]{1,0:T(8,128)(2,1)S(1)} %get-tuple-element.14), channel_id=1, source_target_pairs={{0,2},{1,3},{2,0},{3,1},{128,130},{129,131},{130,128},{131,129},{4... | collective-permute-start | bytes 786440 | tf_op jit(solution)/shard_map/ppermute | solution.py:178
  17.4 11.6 %collective-permute-start.2 = (bf16[128,1024]{1,0:T(8,128)(2,1)S(1)}, bf16[128,1024]{1,0:T(8,128)(2,1)S(1)}, u32[]{:S(2)}, u32[]{:S(2)}) collective-permute-start(bf16[128,1024]{1,0:T(8,128)(2,1)S(1)} %get-tuple-element.13), channel_id=1, source_target_pairs={{0,3},{1,0},{2,1},{3,2},{128,131},{129,128},{130,129},{131,130},{4... | collective-permute-start | bytes 786440 | tf_op jit(solution)/shard_map/ppermute | solution.py:178
  54.4 1.7 copy-start.6
  97.1 1.7 copy-start.1
  98.9 8.1 %copy-start.3 = (bf16[128,4096]{1,0:T(8,128)(2,1)S(1)}, bf16[128,4096]{1,0:T(8,128)(2,1)}, u32[]{:S(2)}) copy-start(bf16[128,4096]{1,0:T(8,128)(2,1)} %cotangent_ref.1) | copy-start | bytes 3145732
  102.5 17.0 %collective-permute-start.3 = (bf16[128,1280]{1,0:T(8,128)(2,1)S(1)}, bf16[128,1280]{1,0:T(8,128)(2,1)S(1)}, u32[]{:S(2)}, u32[]{:S(2)}) collective-permute-start(bf16[128,1280]{1,0:T(8,128)(2,1)S(1)} %get-tuple-element.11), channel_id=1, source_target_pairs={{0,3},{1,0},{2,1},{3,2},{128,131},{129,128},{130,129},{131,130},{4... | collective-permute-start | bytes 983048 | tf_op jit(solution)/shard_map/ppermute | solution.py:178
  105.3 15.6 %collective-permute-start.4 = (bf16[128,1280]{1,0:T(8,128)(2,1)S(1)}, bf16[128,1280]{1,0:T(8,128)(2,1)S(1)}, u32[]{:S(2)}, u32[]{:S(2)}) collective-permute-start(bf16[128,1280]{1,0:T(8,128)(2,1)S(1)} %get-tuple-element.10), channel_id=1, source_target_pairs={{0,2},{1,3},{2,0},{3,1},{128,130},{129,131},{130,128},{131,129},{4... | collective-permute-start | bytes 983048 | tf_op jit(solution)/shard_map/ppermute | solution.py:178
  106.1 23.5 %copy-start.2 = (bf16[8,1280,128]{2,1,0:T(8,128)(2,1)S(1)}, bf16[8,1280,128]{2,1,0:T(8,128)(2,1)}, u32[]{:S(2)}) copy-start(bf16[8,1280,128]{2,1,0:T(8,128)(2,1)} %all-gather.3.cloned.1.call-done.refs_4_) | copy-start | bytes 7864324
  106.1 20.0 %collective-permute-start.5 = (bf16[128,1280]{1,0:T(8,128)(2,1)S(1)}, bf16[128,1280]{1,0:T(8,128)(2,1)S(1)}, u32[]{:S(2)}, u32[]{:S(2)}) collective-permute-start(bf16[128,1280]{1,0:T(8,128)(2,1)S(1)} %get-tuple-element.9), channel_id=1, source_target_pairs={{0,1},{1,2},{2,3},{3,0},{128,129},{129,130},{130,131},{131,128},{4... | collective-permute-start | bytes 983048 | tf_op jit(solution)/shard_map/ppermute | solution.py:178
  127.1 25.3 %copy-start.5 = (bf16[1,128,4096]{2,1,0:T(8,128)(2,1)S(1)}, bf16[1,128,4096]{2,1,0:T(8,128)(2,1)}, u32[]{:S(2)}) copy-start(bf16[1,128,4096]{2,1,0:T(8,128)(2,1)} %param.7) | copy-start | bytes 3145732
  127.1 25.3 %copy-start.9 = (f32[1,4096]{1,0:T(1,128)S(1)}, f32[1,4096]{1,0:T(1,128)}, u32[]{:S(2)}) copy-start(f32[1,4096]{1,0:T(1,128)} %gain_ref.3) | copy-start | bytes 49156
  127.1 2.4 %collective-permute-start.6 = (bf16[128,1280]{1,0:T(8,128)(2,1)S(1)}, bf16[128,1280]{1,0:T(8,128)(2,1)S(1)}, u32[]{:S(2)}, u32[]{:S(2)}) collective-permute-start(bf16[128,1280]{1,0:T(8,128)(2,1)S(1)} %get-tuple-element.8.refs_0_.upper_ref), channel_id=1, source_target_pairs={{128,129},{129,130},{130,131},{131,128},{132,133},{133,134},{134,1... | collective-permute-start | bytes 983048 | tf_op jit(solution)/shard_map/ppermute | solution.py:178
  128.0 1.6 collective-permute-start.7
  128.7 0.9 collective-permute-start.8
  152.9 12.1 %collective-permute-start.10 = (bf16[32,4096]{1,0:T(8,128)(2,1)S(1)}, bf16[32,4096]{1,0:T(8,128)(2,1)S(1)}, u32[]{:S(2)}, u32[]{:S(2)}) collective-permute-start(bf16[32,4096]{1,0:T(8,128)(2,1)S(1)} %shard_map.80), channel_id=1, source_target_pairs={{128,32},{160,64},{192,96},{224,0},{129,33},{161,65},{193,97},{225... | collective-permute-start | bytes 786440 | tf_op jit(solution)/shard_map/ppermute | solution.py:182
  154.2 12.2 %collective-permute-start.11 = (bf16[32,4096]{1,0:T(8,128)(2,1)S(1)}, bf16[32,4096]{1,0:T(8,128)(2,1)S(1)}, u32[]{:S(2)}, u32[]{:S(2)}) collective-permute-start(bf16[32,4096]{1,0:T(8,128)(2,1)S(1)} %shard_map.80), channel_id=1, source_target_pairs={{128,64},{160,96},{192,0},{224,32},{129,65},{161,97},{193,1},{225,... | collective-permute-start | bytes 786440 | tf_op jit(solution)/shard_map/ppermute | solution.py:182
  155.5 13.6 %collective-permute-start.12 = (bf16[32,4096]{1,0:T(8,128)(2,1)S(1)}, bf16[32,4096]{1,0:T(8,128)(2,1)S(1)}, u32[]{:S(2)}, u32[]{:S(2)}) collective-permute-start(bf16[32,4096]{1,0:T(8,128)(2,1)S(1)} %shard_map.80), channel_id=1, source_target_pairs={{128,96},{160,0},{192,32},{224,64},{129,97},{161,1},{193,33},{225,... | collective-permute-start | bytes 786440 | tf_op jit(solution)/shard_map/ppermute | solution.py:182
  156.8 12.3 %collective-permute-start.9 = (bf16[32,4096]{1,0:T(8,128)(2,1)S(1)}, bf16[32,4096]{1,0:T(8,128)(2,1)S(1)}, u32[]{:S(2)}, u32[]{:S(2)}) collective-permute-start(bf16[32,4096]{1,0:T(8,128)(2,1)S(1)} %shard_map.80), channel_id=1, source_target_pairs={{128,0},{160,32},{192,64},{224,96},{129,1},{161,33},{193,65},{225,... | collective-permute-start | bytes 786440 | tf_op jit(solution)/shard_map/ppermute | solution.py:182
  169.1 3.4 %copy-start = (bf16[1,4096,1024]{2,1,0:T(8,128)(2,1)S(1)}, bf16[1,4096,1024]{2,1,0:T(8,128)(2,1)}, u32[]{:S(2)}) copy-start(bf16[1,4096,1024]{2,1,0:T(8,128)(2,1)} %param.13) | copy-start | bytes 25165828
  172.5 1.0 copy-start.7
Sparse Core Ops, SparseCore 0:
  9.1 45.2 all-gather.4
  56.2 40.9 all-gather.2
  99.7 32.1 reduce-scatter.1

commit v4 on v3

--- a/solution.py
+++ b/solution.py
@@ -18,6 +18,8 @@
 F32 = jnp.float32
 BF16 = jnp.bfloat16
 VMEM = pl.BlockSpec(memory_space=pltpu.VMEM)
+HBM = pl.BlockSpec(memory_space=pltpu.HBM)
+ANY = pl.BlockSpec(memory_space=pl.ANY)
 
 
 def dot_nn(a, b):
@@ -32,18 +34,20 @@
     return lax.dot_general(a, b, (((0,), (0,)), ((), ())), preferred_element_type=F32)
 
 
-def call(kernel, outs, args, flops, vmem=20):
+def call(kernel, outs, args, flops, vmem=14, unread=0, scratch=(), far=()):
     return pl.pallas_call(
         kernel,
         out_shape=outs,
-        in_specs=[VMEM] * len(args),
+        in_specs=[HBM if i in far else VMEM for i in range(len(args) - unread)] + [ANY] * unread,
         out_specs=jax.tree.map(lambda _: VMEM, outs),
+        scratch_shapes=scratch,
         compiler_params=pltpu.CompilerParams(vmem_limit_bytes=vmem * 1024 * 1024),
         cost_estimate=pl.CostEstimate(flops=flops, bytes_accessed=100000, transcendentals=0),
     )(*args)
 
 
-def norm_kernel(inputs_ref, gain_ref, hidden_ref):
+def norm_kernel(inputs_ref, gain_ref, *refs):
+    turned_ref = refs[-1]
     y_index = lax.axis_index("y")
     values = inputs_ref[...].astype(F32)
     factor = lax.rsqrt(jnp.mean(values * values, axis=-1, keepdims=True) + 1e-05)
@@ -51,7 +55,9 @@
     for y in range(NY):
         for z in range(NZ):
             block = hidden[:, (z * NY + y) * HD : (z * NY + y + 1) * HD]
-            hidden_ref[(y - y_index + NY) % NY, :, z * HD : (z + 1) * HD] = block
+            turned_ref[(y - y_index + NY) % NY, :, z * HD : (z + 1) * HD] = block
+    for k in range(NY):
+        refs[k][...] = turned_ref[k]
 
 
 def attention_back(packed_of, grads_of):
@@ -75,36 +81,53 @@
     return heads + [dot_tn(grad_scores, queries), dot_tn(weights.astype(BF16), grads)]
 
 
-def slab_product(hidden_ref, slab_ref):
-    total = None
-    for z in range(0, NZ, 2):
-        pair = jnp.concatenate([slab_ref[z], slab_ref[z + 1]], axis=1)
-        term = dot_nt(hidden_ref[:, z * HD : (z + 2) * HD], pair)
-        total = term if total is None else total + term
+def slab_products(hidden, slab_ref, held_ref, sems):
+    copies = [
+        pltpu.make_async_copy(slab_ref.at[pl.ds(z, 2)], held_ref.at[pl.ds(z, 2)], sems.at[z // 2])
+        for z in range(0, NZ, 2)
+    ]
+    for copy in copies:
+        copy.start()
+    for k in range(NY):
+        total = None
+        for z in range(0, NZ, 2):
+            if k == 0:
+                copies[z // 2].wait()
+            pair = jnp.concatenate([held_ref[z], held_ref[z + 1]], axis=1)
+            term = dot_nt(hidden[k][:, z * HD : (z + 2) * HD], pair)
+            total = term if total is None else total + term
+        yield k, total
+
+
+def packed_kernel(*refs):
+    hidden, slab_ref, outs, (held_ref, sems) = refs[:NY], refs[NY], refs[NY + 1 : -2], refs[-2:]
+    for k, total in slab_products(hidden, slab_ref, held_ref, sems):
+        outs[k][...] = total.astype(BF16)
+
+
+def sign_kernel(*refs):
+    hidden, slab_ref, rows = refs[:NY], refs[NY], refs[NY + 1 : 2 * NY + 1]
+    *outs, upper_ref, held_ref, sems = refs[2 * NY + 2 :]
+    upper = None
+    for k, total in slab_products(hidden, slab_ref, held_ref, sems):
+        outs[k][...] = total.astype(BF16)
+        term = jnp.sum(rows[k][...].astype(F32) * total, axis=0, keepdims=True)
+        upper = term if upper is None else upper + term
+    upper_ref[...] = upper
+
+
+def summed(parts, h):
+    at = slice(h * HD, (h + 1) * HD)
+    total = parts[0][:, at].astype(F32)
+    for part in parts[1:]:
+        total = total + part[:, at].astype(F32)
     return total.astype(BF16)
 
 
-def packed_kernel(*refs):
-    hidden, slab_ref, out_ref = refs[:NY], refs[NY], refs[-1]
-    for k in range(NY):
-        out_ref[k] = slab_product(hidden[k], slab_ref)
-
-
-def sign_kernel(*refs):
-    hidden, slab_ref, out_ref = refs[:NY], refs[NY], refs[-1]
-    y_index = lax.axis_index("y")
-    for k in range(NY):
-        out_ref[(y_index - k + NY) % NY] = slab_product(hidden[k], slab_ref)
-
-
 def upper_kernel(grad_ref, *refs):
-    parts, packed_ref, grad_packed_ref = refs[:-2], refs[-2], refs[-1]
-    packed = parts[0][...].astype(F32)
-    for part in parts[1:]:
-        packed = packed + part[...].astype(F32)
-    packed_ref[...] = packed.astype(BF16)
+    parts, grad_packed_ref = refs[:-1], refs[-1]
     columns = attention_back(
-        lambda h: packed_ref[:, h * HD : (h + 1) * HD],
+        lambda h: summed(parts, h),
         lambda h: grad_ref[:, h * HD : (h + 1) * HD],
     )
     for h, column in enumerate(columns):
@@ -124,8 +147,9 @@
                 out_ref[place, :, z * HD : (z + 2) * HD] = term[c * chunk : (c + 1) * chunk]
 
 
-def norm_back_kernel(inputs_ref, gain_ref, cotangent_ref, terms_ref, out_ref):
+def norm_back_kernel(inputs_ref, gain_ref, cotangent_ref, terms_ref, *refs):
     x_index = lax.axis_index("tensor")
+    out_ref = refs[-1]
     chunk, width = out_ref.shape
     rows = pl.ds(pl.multiple_of(x_index * chunk, chunk), chunk)
     values = inputs_ref[rows, :].astype(F32)
@@ -144,33 +168,38 @@
     out_ref[...] = (cotangent_ref[rows, :].astype(F32) + factor * (grad - normed * mean)).astype(BF16)
 
 
-def lower_kernel(count, packed_ref, weight_ref, upper_ref, *refs):
-    *arrived, projected_ref, out_ref, rows_ref, mixed_ref = refs
+def lower_kernel(count, *refs):
+    parts, arrived, projected = refs[:NY], refs[NY : NY + NX], refs[NY + NX : 2 * NY + NX]
+    upper_ref, weight_ref, out_ref, rows_ref, mixed_ref, held_ref, sems = refs[2 * NY + NX :]
     x_index = lax.axis_index("tensor")
     pipe_index = lax.axis_index("pipe")
     chunk = arrived[0].shape[0]
+    depth = held_ref.shape[1]
+    steps = held_ref.shape[0]
+    copies = [
+        pltpu.make_async_copy(weight_ref.at[pl.ds(i * depth, depth)], held_ref.at[i], sems.at[i])
+        for i in range(steps)
+    ]
+    for copy in copies:
+        copy.start()
     for j in range(NX):
         place = pl.multiple_of(((x_index - j + NX) % NX) * chunk, chunk)
         rows_ref[pl.ds(place, chunk), :] = arrived[j][...]
-    mixed_ref[...] = jnp.zeros_like(mixed_ref)
-    depth = 512
-
-    def step(i, _):
-        at = pl.ds(pl.multiple_of(i * depth, depth), depth)
-        mixed_ref[...] += dot_nn(rows_ref[:, at], weight_ref[at, :])
-        return 0
-
-    lax.fori_loop(0, rows_ref.shape[1] // depth, step, 0)
+    for i, copy in enumerate(copies):
+        copy.wait()
+        term = dot_nn(rows_ref[:, i * depth : (i + 1) * depth], held_ref[i])
+        mixed_ref[...] = term if i == 0 else mixed_ref[...] + term
     columns = attention_back(
-        lambda h: packed_ref[:, h * HD : (h + 1) * HD],
+        lambda h: summed(parts, h),
         lambda h: mixed_ref[:, h * HD : (h + 1) * HD].astype(BF16),
     )
     for h, column in enumerate(columns):
         at = slice(h * HD, (h + 1) * HD)
-        lower = column.astype(BF16).astype(F32)
-        kept = jnp.where(pipe_index == 1, upper_ref[:, at].astype(F32), lower)
-        product = projected_ref[:, at].astype(F32)
-        out_ref[:, at] = jnp.sum(kept * product, axis=0, keepdims=True) * (1.0 / count)
+        product = projected[0][:, at].astype(F32)
+        for other in projected[1:]:
+            product = product + other[:, at].astype(F32)
+        lower = jnp.sum(column.astype(BF16).astype(F32) * product, axis=0, keepdims=True)
+        out_ref[:, at] = jnp.where(pipe_index == 1, upper_ref[:, at], lower) * (1.0 / count)
 
 
 def send_y(value, steps, pipes=(0, 1)):
@@ -191,47 +220,66 @@
     rows = sign.shape[0]
     weight = (qkv_base[0].astype(F32) + qkv_scale[0][:, None] * sign.astype(F32)).astype(BF16)
     weight_slab = lax.all_gather(weight, "z", axis=0, tiled=False)
-    sign_slab = lax.all_gather(sign, "z", axis=0, tiled=False)
-
-    hidden = call(
-        norm_kernel, jax.ShapeDtypeStruct((NY, tokens, NZ * HD), BF16), (inputs, norm_gain), 10**7
-    )
+
+    slab = jax.ShapeDtypeStruct((tokens, NZ * HD), BF16)
+    hidden = call(norm_kernel, (slab,) * NY, (inputs, norm_gain), 10**7, scratch=[pltpu.VMEM((NY, *slab.shape), BF16)])
     hidden_slab = [hidden[0]] + [send_y(hidden[k], k) for k in range(1, NY)]
+    later_sign = lax.optimization_barrier((sign, weight_slab, *hidden_slab))[0]
+    sign_slab = lax.all_gather(later_sign, "z", axis=0, tiled=False)
     grad_mixed = dot_nn(cotangent, weight_out).astype(BF16)
 
     flops = 2 * tokens * rows * width
-    by_y = jax.ShapeDtypeStruct((NY, tokens, rows), BF16)
+    slab_scratch = [pltpu.VMEM((NZ, rows, HD), BF16), pltpu.SemaphoreType.DMA((NZ // 2,))]
     packed_rows = jax.ShapeDtypeStruct((tokens, rows), BF16)
-    partial = call(packed_kernel, by_y, (*hidden_slab, weight_slab), flops)
-    parts = [partial[0]] + [send_y(partial[k], -k) for k in range(1, NY)]
-    packed, grad_upper = call(upper_kernel, (packed_rows, packed_rows), (grad_mixed, *parts), 10**8)
-
-    signed = call(sign_kernel, by_y, (*hidden_slab, sign_slab), flops)
-    projected = lax.psum_scatter(signed, "y", scatter_dimension=0)
+    partial = call(
+        packed_kernel, (packed_rows,) * NY, (*hidden_slab, weight_slab), flops, scratch=slab_scratch, far=(NY,), vmem=60
+    )
+    parts = [partial[0]] + [send_y(partial[k], -k, (1,)) for k in range(1, NY)]
+    grad_upper = call(upper_kernel, packed_rows, (grad_mixed, *parts), 10**8)
 
     slab_rows = [grad_upper] + [send_y(grad_upper, k, (1,)) for k in range(1, NY)]
+    later = lax.optimization_barrier((*partial, grad_upper))
+    parts = [partial[0]] + [send_y(later[k], -k, (0,)) for k in range(1, NY)]
     back = call(
         back_kernel,
         jax.ShapeDtypeStruct((NX * NY, chunk, NZ * HD), BF16),
         (*slab_rows, weight_slab),
         flops,
     )
+    *signed, upper_total = call(
+        sign_kernel,
+        (packed_rows,) * NY + (jax.ShapeDtypeStruct((1, rows), F32),),
+        (*hidden_slab, sign_slab, *slab_rows, back),
+        flops,
+        unread=1,
+        scratch=slab_scratch,
+        far=(NY,),
+        vmem=44,
+    )
+    projected = [signed[0]] + [send_y(signed[k], -k, (0,)) for k in range(1, NY)]
     terms = lax.all_to_all(back, ("tensor", "y"), 0, 0)
     backward = call(
         norm_back_kernel,
         jax.ShapeDtypeStruct((chunk, width), BF16),
-        (inputs, norm_gain, cotangent, terms),
+        (inputs, norm_gain, cotangent, terms, upper_total, *parts[1:]),
         10**6,
+        unread=NY,
     )
     arrived = [send_down(backward, j) for j in range(NX)]
-    args = (packed, weight_out, grad_upper, *arrived, projected)
+    args = (*parts, *arrived, *projected, upper_total, weight_out)
+    depth = width // 8
     result = pl.pallas_call(
         functools.partial(lower_kernel, tokens * NZ * NY),
         out_shape=jax.ShapeDtypeStruct((1, rows), F32),
-        in_specs=[VMEM] * len(args),
+        in_specs=[VMEM] * (len(args) - 1) + [HBM],
         out_specs=VMEM,
-        scratch_shapes=[pltpu.VMEM((tokens, width), BF16), pltpu.VMEM((tokens, QH * HD), F32)],
-        compiler_params=pltpu.CompilerParams(vmem_limit_bytes=28 * 1024 * 1024),
+        scratch_shapes=[
+            pltpu.VMEM((tokens, width), BF16),
+            pltpu.VMEM((tokens, QH * HD), F32),
+            pltpu.VMEM((8, depth, QH * HD), BF16),
+            pltpu.SemaphoreType.DMA((8,)),
+        ],
+        compiler_params=pltpu.CompilerParams(vmem_limit_bytes=56 * 1024 * 1024),
         cost_estimate=pl.CostEstimate(flops=flops, bytes_accessed=100000, transcendentals=131072),
     )(*args)
     return lax.psum(lax.psum(result, "y"), "z")

time: 209 us -> 191 us (0.914)
  waiting for transfers between devices: 98.1 us -> 55.1 us
  starting transfers between devices: 18 us -> 43.3 us
  blocking collectives: 46.3 us -> 27.9 us
  Pallas kernels: 15.4 us -> 24.6 us
  local copies, waits for them, and re-layouts: 9.96 us -> 16.5 us
    all_gather x1, waiting for transfers between devices: 25.4 us -> 3.26 us  [local(): sign_slab = lax.all_gather(later_sign, 'z', axis=0, tiled=False)]
    all_to_all x1 -> x0, blocking collectives: 21.3 us -> none  [local(): terms = lax.all_to_all(back, ('tensor', 'y'), 0, 0)]
    ppermute x9 -> x15, starting transfers between devices: 12.8 us -> 30.8 us  [send_y(): return lax.ppermute(value, ('pipe', 'y'), pairs)]
    ppermute x9 -> x15, waiting for transfers between devices: 24.5 us -> 10.3 us  [send_y(): return lax.ppermute(value, ('pipe', 'y'), pairs)]
    all_gather x1, waiting for transfers between devices: 36.4 us -> 25.8 us  [local(): weight_slab = lax.all_gather(weight, 'z', axis=0, tiled=False)]
    all_to_all x0 -> x1, starting transfers between devices: none -> 7.29 us  [local(): terms = lax.all_to_all(back, ('tensor', 'y'), 0, 0)]
    unnamed x20 -> x68, local copies, waits for them, and re-layouts: 9.79 us -> 16.5 us
    pallas_call x6, Pallas kernels: 11.8 us -> 17.4 us  [call(): pl.pallas_call(kernel, out_shape=outs, in_specs=[HBM if i in far else VME...]
  transfers between devices with their start and end apart: 16 -> 22, of which waited for: 10 -> 8; matrix products, arithmetic and copies ran while one was open for 4% -> 3% of each run, Pallas kernels for 6% -> 9%
where the time goes in v4:
time: 191 us; the launch traced here: 189 us
  waiting for transfers between devices  55.1 us (29%)
  starting transfers between devices  43.3 us (23%)
  blocking collectives  27.9 us (15%)
  Pallas kernels  24.6 us (13%)
  local copies, waits for them, and re-layouts  16.5 us (9%)
  between operations  13.9 us (7%)
  matrix products  4.75 us (2%)
  other arithmetic  2.83 us (1%)
    ppermute x15, starting transfers between devices, send_y(): return lax.ppermute(value, ('pipe', 'y'), pairs)  30.8 us
    psum x2, blocking collectives, local(): return lax.psum(lax.psum(result, 'y'), 'z')  27.9 us
    all_gather x1, waiting for transfers between devices, local(): weight_slab = lax.all_gather(weight, 'z', axis=0, tiled=False)  25.8 us
    pallas_call x6, Pallas kernels, call(): pl.pallas_call(kernel, out_shape=outs, in_specs=[HBM if i in far else VME...  17.4 us
    unnamed x68, local copies, waits for them, and re-layouts  16.5 us
    ppermute x4, waiting for transfers between devices, send_down(): lax.ppermute(value, ('pipe', 'tensor'), [(NX + i, (i + steps) % NX) for i...  15.7 us
    ppermute x15, waiting for transfers between devices, send_y(): return lax.ppermute(value, ('pipe', 'y'), pairs)  10.3 us
    all_to_all x1, starting transfers between devices, local(): terms = lax.all_to_all(back, ('tensor', 'y'), 0, 0)  7.29 us
  transfers between devices with their start and end apart: 22, of which 8 were waited for; matrix products, arithmetic and copies ran while one was open for 3% of the time, Pallas kernels for 9%

profile of v4, /device:TPU:2, one launch (start us, length us, event | category | flops | bytes accessed | tf_op | source)
XLA Modules:
  0.0 188.8 jit_solution(4394664038456460590)
XLA Ops:
  7.3 2.0 %add_convert_fusion = bf16[1,1280,128]{2,1,0:T(8,128)(2,1)} fusion(bf16[1,1280,128]{2,1,0:T(8,128)(2,1)} %param.11, bf16[1,1280,128]{2,1,0:T(8,128)(2,1)} %param.10, f32[1280]{0:T(1024)S(1)} %reduce), kind=kLoop, calls=%fused_computation.1 | loop fusion | flops 819200 | bytes 988160 | tf_op jit(solution)/shard_map/convert_element_type | solution.py:221
  9.5 1.2 copy-done.1
  12.9 1.6 collective-permute-start
  14.5 2.9 %collective-permute-start.1 = (bf16[128,1024]{1,0:T(8,128)(2,1)S(1)}, bf16[128,1024]{1,0:T(8,128)(2,1)S(1)}, u32[]{:S(2)}, u32[]{:S(2)}) collective-permute-start(bf16[128,1024]{1,0:T(8,128)(2,1)S(1)} %get-tuple-element.24), channel_id=1, source_target_pairs={{0,2},{1,3},{2,0},{3,1},{128,130},{129,131},{130,128},{131,129},{4... | collective-permute-start | bytes 786440 | tf_op jit(solution)/shard_map/ppermute | solution.py:207
  17.4 1.3 collective-permute-start.2
  18.7 3.5 %collective-permute-done.refs_1_ = bf16[128,1024]{1,0:T(8,128)(2,1)S(1)} collective-permute-done((bf16[128,1024]{1,0:T(8,128)(2,1)S(1)}, bf16[128,1024]{1,0:T(8,128)(2,1)S(1)}, u32[]{:S(2)}, u32[]{:S(2)}) %collective-permute-start) | collective-permute-done | bytes 262176 | tf_op jit(solution)/shard_map/ppermute | solution.py:207
  22.2 6.8 %collective-permute-done.1.refs_2_ = bf16[128,1024]{1,0:T(8,128)(2,1)S(1)} collective-permute-done((bf16[128,1024]{1,0:T(8,128)(2,1)S(1)}, bf16[128,1024]{1,0:T(8,128)(2,1)S(1)}, u32[]{:S(2)}, u32[]{:S(2)}) %collective-permute-start.1) | collective-permute-done | bytes 262176 | tf_op jit(solution)/shard_map/ppermute | solution.py:207
  29.0 25.8 %all-gather.4.cloned.1.call-done.refs_4_ = bf16[8,1280,128]{2,1,0:T(8,128)(2,1)} async-done(((bf16[1,1280,128]{2,1,0:T(8,128)(2,1)}), bf16[8,1280,128]{2,1,0:T(8,128)(2,1)}) %all-gather.4.cloned.1.call-update) | async-done | bytes 2621456 | tf_op jit(solution)/shard_map/all_gather | solution.py:222
  54.8 7.4 %shard_map.77 = (bf16[128,1280]{1,0:T(8,128)(2,1)}, bf16[128,1280]{1,0:T(8,128)(2,1)}, bf16[128,1280]{1,0:T(8,128)(2,1)}, bf16[128,1280]{1,0:T(8,128)(2,1)}) custom-call(bf16[128,1024]{1,0:T(8,128)(2,1)} %copy-done.13, bf16[128,1024]{1,0:T(8,128)(2,1)} %copy-done.15, bf16[128,1024]{1,0:T(8,128)(2,1)} %copy-done.17, bf16[128,1024]{1,0:T(8,128)(2,1)} %copy-done.19, ...), custom_call_target="tpu_custom_call" | custom-call | flops 1342177280 | bytes 100000 | tf_op jit(solution)/shard_map/pallas_call | solution.py:38
  64.7 4.8 %convolution_convert_fusion.grad_ref = bf16[128,1024]{1,0:T(8,128)(2,1)S(1)} fusion(bf16[128,4096]{1,0:T(8,128)(2,1)S(1)} %copy-done, bf16[1,4096,1024]{2,1,0:T(8,128)(2,1)} %param.13), kind=kOutput, calls=%fused_computation | convolution fusion | flops 1073872896 | bytes 9699328 | tf_op jit(solution)/shard_map/dot_general | solution.py:26
  72.6 2.6 %shard_map.79.refs_9_ = bf16[16,32,1024]{2,1,0:T(8,128)(2,1)} custom-call(bf16[128,1280]{1,0:T(8,128)(2,1)S(1)} %shard_map.78.refs_0_.refs_5_, bf16[128,1280]{1,0:T(8,128)(2,1)S(1)} %collective-permute-done.9.refs_1_.refs_6_, bf16[128,1280]{1,0:T(8,128)(2,1)S(1)} %collective-permute-done.10.refs_2_.refs_7_, ...), custom_call_target="tpu_custom_call" | custom-call | flops 1342177280 | bytes 100000 | tf_op jit(solution)/shard_map/pallas_call | solution.py:38
  76.7 7.3 %all-to-all-start = ((bf16[16,32,1024]{2,1,0:T(8,128)(2,1)}), bf16[16,32,1024]{2,1,0:T(8,128)(2,1)S(1)}, u32[]{:S(2)}, u32[]{:S(2)}) async-start(bf16[16,32,1024]{2,1,0:T(8,128)(2,1)} %shard_map.79.refs_9_), calls=%async_computation | async-start | bytes 2097152 | tf_op jit(solution)/shard_map/all_to_all | solution.py:260
  84.0 4.6 %collective-permute-start.6 = (bf16[128,1280]{1,0:T(8,128)(2,1)}, bf16[128,1280]{1,0:T(8,128)(2,1)}, u32[]{:S(2)}, u32[]{:S(2)}) collective-permute-start(bf16[128,1280]{1,0:T(8,128)(2,1)} %get-tuple-element.30), channel_id=1, source_target_pairs={{0,3},{1,0},{2,1},{3,2},{4,7},{5,4},{6,5},{7,6},{8,11},{9,8},{10,9... | collective-permute-start | bytes 983048 | tf_op jit(solution)/shard_map/ppermute | solution.py:207
  88.5 2.8 %collective-permute-start.7 = (bf16[128,1280]{1,0:T(8,128)(2,1)}, bf16[128,1280]{1,0:T(8,128)(2,1)}, u32[]{:S(2)}, u32[]{:S(2)}) collective-permute-start(bf16[128,1280]{1,0:T(8,128)(2,1)} %get-tuple-element.31), channel_id=1, source_target_pairs={{0,2},{1,3},{2,0},{3,1},{4,6},{5,7},{6,4},{7,5},{8,10},{9,11},{10,... | collective-permute-start | bytes 983048 | tf_op jit(solution)/shard_map/ppermute | solution.py:207
  91.3 2.9 %collective-permute-start.8 = (bf16[128,1280]{1,0:T(8,128)(2,1)}, bf16[128,1280]{1,0:T(8,128)(2,1)}, u32[]{:S(2)}, u32[]{:S(2)}) collective-permute-start(bf16[128,1280]{1,0:T(8,128)(2,1)} %get-tuple-element.32), channel_id=1, source_target_pairs={{0,1},{1,2},{2,3},{3,0},{4,5},{5,6},{6,7},{7,4},{8,9},{9,10},{10,1... | collective-permute-start | bytes 983048 | tf_op jit(solution)/shard_map/ppermute | solution.py:207
  94.3 3.3 %all-gather.6.cloned.1.call-done = bf16[10240,128]{1,0:T(8,128)(2,1)} async-done(((bf16[1280,128]{1,0:T(8,128)(2,1)}), bf16[10240,128]{1,0:T(8,128)(2,1)}) %all-gather.6.cloned.1.call-update) | async-done | bytes 2621456 | tf_op jit(solution)/shard_map/all_gather | solution.py:228
  97.5 1.7 copy-done.4
  106.0 5.1 %shard_map.80 = (bf16[128,1280]{1,0:T(8,128)(2,1)S(1)}, bf16[128,1280]{1,0:T(8,128)(2,1)S(1)}, bf16[128,1280]{1,0:T(8,128)(2,1)S(1)}, bf16[128,1280]{1,0:T(8,128)(2,1)S(1)}, f32[1,1280]{1,0:T(1,128)S(1)}) custom-call(bf16[128,1024]{1,0:T(8,128)(2,1)S(1)} %copy-done.14, bf16[128,1024]{1,0:T(8,128)(2,1)S(1)} %copy-done.16, bf16[128,1024]{1,0:T(8,128)(2,1)S(1)} %copy-done.18, ...), custom_call_target="tpu_custom_call" | custom-call | flops 1342177280 | bytes 100000 | tf_op jit(solution)/shard_map/pallas_call | solution.py:38
  114.6 1.3 collective-permute-start.12
  115.9 1.3 collective-permute-start.13
  117.2 4.7 %collective-permute-start.16 = (bf16[128,1280]{1,0:T(8,128)(2,1)}, bf16[128,1280]{1,0:T(8,128)(2,1)S(1)}, u32[]{:S(2)}, u32[]{:S(2)}) collective-permute-start(bf16[128,1280]{1,0:T(8,128)(2,1)} %copy-done.26), channel_id=1, source_target_pairs={{0,3},{1,0},{2,1},{3,2},{4,7},{5,4},{6,5},{7,6},{8,11},{9,8},{10,9... | collective-permute-start | bytes 983048 | tf_op jit(solution)/shard_map/ppermute | solution.py:207
  121.8 2.7 %collective-permute-start.17 = (bf16[128,1280]{1,0:T(8,128)(2,1)}, bf16[128,1280]{1,0:T(8,128)(2,1)S(1)}, u32[]{:S(2)}, u32[]{:S(2)}) collective-permute-start(bf16[128,1280]{1,0:T(8,128)(2,1)} %copy-done.25), channel_id=1, source_target_pairs={{0,2},{1,3},{2,0},{3,1},{4,6},{5,7},{6,4},{7,5},{8,10},{9,11},{10,... | collective-permute-start | bytes 983048 | tf_op jit(solution)/shard_map/ppermute | solution.py:207
  124.5 3.0 %collective-permute-start.18 = (bf16[128,1280]{1,0:T(8,128)(2,1)}, bf16[128,1280]{1,0:T(8,128)(2,1)S(1)}, u32[]{:S(2)}, u32[]{:S(2)}) collective-permute-start(bf16[128,1280]{1,0:T(8,128)(2,1)} %copy-done.24), channel_id=1, source_target_pairs={{0,1},{1,2},{2,3},{3,0},{4,5},{5,6},{6,7},{7,4},{8,9},{9,10},{10,1... | collective-permute-start | bytes 983048 | tf_op jit(solution)/shard_map/ppermute | solution.py:207
  127.5 6.0 %collective-permute-done.12.refs_4_ = bf16[32,4096]{1,0:T(8,128)(2,1)S(1)} collective-permute-done((bf16[32,4096]{1,0:T(8,128)(2,1)S(1)}, bf16[32,4096]{1,0:T(8,128)(2,1)S(1)}, u32[]{:S(2)}, u32[]{:S(2)}) %collective-permute-start.12) | collective-permute-done | bytes 262176 | tf_op jit(solution)/shard_map/ppermute | solution.py:211
  133.5 1.3 collective-permute-start.14
  134.8 3.0 %collective-permute-done.13.refs_5_ = bf16[32,4096]{1,0:T(8,128)(2,1)S(1)} collective-permute-done((bf16[32,4096]{1,0:T(8,128)(2,1)S(1)}, bf16[32,4096]{1,0:T(8,128)(2,1)S(1)}, u32[]{:S(2)}, u32[]{:S(2)}) %collective-permute-start.13) | collective-permute-done | bytes 262176 | tf_op jit(solution)/shard_map/ppermute | solution.py:211
  137.9 1.3 collective-permute-start.15
  139.2 3.8 %collective-permute-done.14.refs_6_ = bf16[32,4096]{1,0:T(8,128)(2,1)S(1)} collective-permute-done((bf16[32,4096]{1,0:T(8,128)(2,1)S(1)}, bf16[32,4096]{1,0:T(8,128)(2,1)S(1)}, u32[]{:S(2)}, u32[]{:S(2)}) %collective-permute-start.14) | collective-permute-done | bytes 262176 | tf_op jit(solution)/shard_map/ppermute | solution.py:211
  143.0 2.8 %collective-permute-done.15.refs_7_ = bf16[32,4096]{1,0:T(8,128)(2,1)S(1)} collective-permute-done((bf16[32,4096]{1,0:T(8,128)(2,1)S(1)}, bf16[32,4096]{1,0:T(8,128)(2,1)S(1)}, u32[]{:S(2)}, u32[]{:S(2)}) %collective-permute-start.15) | collective-permute-done | bytes 262176 | tf_op jit(solution)/shard_map/ppermute | solution.py:211
  146.8 7.2 %shard_map.82 = f32[1,1280]{1,0:T(1,128)} custom-call(bf16[128,1280]{1,0:T(8,128)(2,1)} %get-tuple-element.26.refs_0_, bf16[128,1280]{1,0:T(8,128)(2,1)} %collective-permute-done.6.refs_1_, bf16[128,1280]{1,0:T(8,128)(2,1)} %collective-permute-done.7.refs_2_, bf16[128,1280]{1,0:T(8,128)(2,1)} %collective-permute-done.8.refs_3_, bf16[32,4096]{1,0:T(8,128)(2,1)} %copy-done.30, ...), custom_call_target="tpu_custom_call" | custom-call | flops 1342177280 | bytes 100000 | tf_op jit(solution)/shard_map/pallas_call | solution.py:271
  154.1 10.6 %psum.14 = f32[1,1280]{1,0:T(1,128)S(1)} all-reduce(f32[1,1280]{1,0:T(1,128)} %shard_map.82), channel_id=1, replica_groups=mesh['pipe'=2,'tensor'=4,'z'=8,'y'=4] {'y'}, use_global_device_ids=true, to_apply=%region_0.0 | all-reduce | flops 1280 | bytes 10240 | tf_op jit(solution)/shard_map/psum | solution.py:285
  164.7 17.2 %psum.15 = f32[1,1280]{1,0:T(1,128)} all-reduce(f32[1,1280]{1,0:T(1,128)S(1)} %psum.14), channel_id=1, replica_groups=mesh['pipe'=2,'tensor'=4,'z'=8,'y'=4] {'z'}, use_global_device_ids=true, to_apply=%region_1.0 | all-reduce | flops 1280 | bytes 10240 | tf_op jit(solution)/shard_map/psum | solution.py:285
  (94 shorter events, 21.0 us)
Async XLA Ops:
  6.5 58.1 %copy-start = (bf16[128,4096]{1,0:T(8,128)(2,1)S(1)}, bf16[128,4096]{1,0:T(8,128)(2,1)}, u32[]{:S(2)}) copy-start(bf16[128,4096]{1,0:T(8,128)(2,1)} %cotangent_ref.1) | copy-start | bytes 3145732
  6.5 48.3 %all-gather.4.cloned.1.call-start = ((), (), s32[]{:S(2)}) async-start(), calls=%async_computation.1 | async-start | bytes 2949120 | tf_op jit(solution)/shard_map/all_gather | solution.py:222
  9.4 88.1 %all-gather.6.cloned.1.call-start = ((), (), s32[]{:S(2)}) async-start(), calls=%async_computation.2 | async-start | bytes 2949120 | tf_op jit(solution)/shard_map/all_gather | solution.py:228
  12.9 9.3 %collective-permute-start = (bf16[128,1024]{1,0:T(8,128)(2,1)S(1)}, bf16[128,1024]{1,0:T(8,128)(2,1)S(1)}, u32[]{:S(2)}, u32[]{:S(2)}) collective-permute-start(bf16[128,1024]{1,0:T(8,128)(2,1)S(1)} %get-tuple-element.23), channel_id=1, source_target_pairs={{0,1},{1,2},{2,3},{3,0},{128,129},{129,130},{130,131},{131,128},{4... | collective-permute-start | bytes 786440 | tf_op jit(solution)/shard_map/ppermute | solution.py:207
  14.5 14.5 %collective-permute-start.1 = (bf16[128,1024]{1,0:T(8,128)(2,1)S(1)}, bf16[128,1024]{1,0:T(8,128)(2,1)S(1)}, u32[]{:S(2)}, u32[]{:S(2)}) collective-permute-start(bf16[128,1024]{1,0:T(8,128)(2,1)S(1)} %get-tuple-element.24), channel_id=1, source_target_pairs={{0,2},{1,3},{2,0},{3,1},{128,130},{129,131},{130,128},{131,129},{4... | collective-permute-start | bytes 786440 | tf_op jit(solution)/shard_map/ppermute | solution.py:207
  17.4 11.6 %collective-permute-start.2 = (bf16[128,1024]{1,0:T(8,128)(2,1)S(1)}, bf16[128,1024]{1,0:T(8,128)(2,1)S(1)}, u32[]{:S(2)}, u32[]{:S(2)}) collective-permute-start(bf16[128,1024]{1,0:T(8,128)(2,1)S(1)} %get-tuple-element.25), channel_id=1, source_target_pairs={{0,3},{1,0},{2,1},{3,2},{128,131},{129,128},{130,129},{131,130},{4... | collective-permute-start | bytes 786440 | tf_op jit(solution)/shard_map/ppermute | solution.py:207
  22.2 32.6 %copy-start.15 = (bf16[128,1024]{1,0:T(8,128)(2,1)}, bf16[128,1024]{1,0:T(8,128)(2,1)S(1)}, u32[]{:S(2)}) copy-start(bf16[128,1024]{1,0:T(8,128)(2,1)S(1)} %collective-permute-done.refs_1_) | copy-start | bytes 786436
  29.0 25.8 %copy-start.17 = (bf16[128,1024]{1,0:T(8,128)(2,1)}, bf16[128,1024]{1,0:T(8,128)(2,1)S(1)}, u32[]{:S(2)}) copy-start(bf16[128,1024]{1,0:T(8,128)(2,1)S(1)} %collective-permute-done.1.refs_2_) | copy-start | bytes 786436
  29.0 25.8 %copy-start.19 = (bf16[128,1024]{1,0:T(8,128)(2,1)}, bf16[128,1024]{1,0:T(8,128)(2,1)S(1)}, u32[]{:S(2)}) copy-start(bf16[128,1024]{1,0:T(8,128)(2,1)S(1)} %collective-permute-done.2.refs_3_) | copy-start | bytes 786436
  62.3 7.1 %collective-permute-start.3 = (bf16[128,1280]{1,0:T(8,128)(2,1)}, bf16[128,1280]{1,0:T(8,128)(2,1)S(1)}, u32[]{:S(2)}, u32[]{:S(2)}) collective-permute-start(bf16[128,1280]{1,0:T(8,128)(2,1)} %get-tuple-element.30), channel_id=1, source_target_pairs={{128,131},{129,128},{130,129},{131,130},{132,135},{133,132},{134,1... | collective-permute-start | bytes 983048 | tf_op jit(solution)/shard_map/ppermute | solution.py:207
  63.1 6.3 %collective-permute-start.4 = (bf16[128,1280]{1,0:T(8,128)(2,1)}, bf16[128,1280]{1,0:T(8,128)(2,1)S(1)}, u32[]{:S(2)}, u32[]{:S(2)}) collective-permute-start(bf16[128,1280]{1,0:T(8,128)(2,1)} %get-tuple-element.31), channel_id=1, source_target_pairs={{128,130},{129,131},{130,128},{131,129},{132,134},{133,135},{134,1... | collective-permute-start | bytes 983048 | tf_op jit(solution)/shard_map/ppermute | solution.py:207
  63.8 8.8 %copy-start.3 = (bf16[8,1280,128]{2,1,0:T(8,128)(2,1)S(1)}, bf16[8,1280,128]{2,1,0:T(8,128)(2,1)}, u32[]{:S(2)}) copy-start(bf16[8,1280,128]{2,1,0:T(8,128)(2,1)} %all-gather.4.cloned.1.call-done.refs_4_) | copy-start | bytes 7864324
  63.8 5.6 %collective-permute-start.5 = (bf16[128,1280]{1,0:T(8,128)(2,1)}, bf16[128,1280]{1,0:T(8,128)(2,1)S(1)}, u32[]{:S(2)}, u32[]{:S(2)}) collective-permute-start(bf16[128,1280]{1,0:T(8,128)(2,1)} %get-tuple-element.32), channel_id=1, source_target_pairs={{128,129},{129,130},{130,131},{131,128},{132,133},{133,134},{134,1... | collective-permute-start | bytes 983048 | tf_op jit(solution)/shard_map/ppermute | solution.py:207
  69.4 44.6 %copy-start.2 = (bf16[1,128,4096]{2,1,0:T(8,128)(2,1)S(1)}, bf16[1,128,4096]{2,1,0:T(8,128)(2,1)}, u32[]{:S(2)}) copy-start(bf16[1,128,4096]{2,1,0:T(8,128)(2,1)} %param.7) | copy-start | bytes 3145732
  69.4 44.6 %copy-start.22 = (f32[1,4096]{1,0:T(1,128)S(1)}, f32[1,4096]{1,0:T(1,128)}, u32[]{:S(2)}) copy-start(f32[1,4096]{1,0:T(1,128)} %gain_ref.3) | copy-start | bytes 49156
  70.5 2.1 %collective-permute-start.10 = (bf16[128,1280]{1,0:T(8,128)(2,1)S(1)}, bf16[128,1280]{1,0:T(8,128)(2,1)S(1)}, u32[]{:S(2)}, u32[]{:S(2)}) collective-permute-start(bf16[128,1280]{1,0:T(8,128)(2,1)S(1)} %shard_map.78.refs_0_.refs_5_), channel_id=1, source_target_pairs={{128,130},{129,131},{130,128},{131,129},{132,134},{133,135},{134,1... | collective-permute-start | bytes 983048 | tf_op jit(solution)/shard_map/ppermute | solution.py:207
  71.2 1.4 collective-permute-start.11
  71.9 0.7 collective-permute-start.9
  76.7 37.4 %all-to-all-start = ((bf16[16,32,1024]{2,1,0:T(8,128)(2,1)}), bf16[16,32,1024]{2,1,0:T(8,128)(2,1)S(1)}, u32[]{:S(2)}, u32[]{:S(2)}) async-start(bf16[16,32,1024]{2,1,0:T(8,128)(2,1)} %shard_map.79.refs_9_), calls=%async_computation | async-start | bytes 2097152 | tf_op jit(solution)/shard_map/all_to_all | solution.py:260
  84.0 30.1 %collective-permute-start.6 = (bf16[128,1280]{1,0:T(8,128)(2,1)}, bf16[128,1280]{1,0:T(8,128)(2,1)}, u32[]{:S(2)}, u32[]{:S(2)}) collective-permute-start(bf16[128,1280]{1,0:T(8,128)(2,1)} %get-tuple-element.30), channel_id=1, source_target_pairs={{0,3},{1,0},{2,1},{3,2},{4,7},{5,4},{6,5},{7,6},{8,11},{9,8},{10,9... | collective-permute-start | bytes 983048 | tf_op jit(solution)/shard_map/ppermute | solution.py:207
  88.5 25.5 %collective-permute-start.7 = (bf16[128,1280]{1,0:T(8,128)(2,1)}, bf16[128,1280]{1,0:T(8,128)(2,1)}, u32[]{:S(2)}, u32[]{:S(2)}) collective-permute-start(bf16[128,1280]{1,0:T(8,128)(2,1)} %get-tuple-element.31), channel_id=1, source_target_pairs={{0,2},{1,3},{2,0},{3,1},{4,6},{5,7},{6,4},{7,5},{8,10},{9,11},{10,... | collective-permute-start | bytes 983048 | tf_op jit(solution)/shard_map/ppermute | solution.py:207
  91.3 22.7 %collective-permute-start.8 = (bf16[128,1280]{1,0:T(8,128)(2,1)}, bf16[128,1280]{1,0:T(8,128)(2,1)}, u32[]{:S(2)}, u32[]{:S(2)}) collective-permute-start(bf16[128,1280]{1,0:T(8,128)(2,1)} %get-tuple-element.32), channel_id=1, source_target_pairs={{0,1},{1,2},{2,3},{3,0},{4,5},{5,6},{6,7},{7,4},{8,9},{9,10},{10,1... | collective-permute-start | bytes 983048 | tf_op jit(solution)/shard_map/ppermute | solution.py:207
  114.0 31.8 %copy-start.23 = (f32[1,1280]{1,0:T(1,128)}, f32[1,1280]{1,0:T(1,128)S(1)}, u32[]{:S(2)}) copy-start(f32[1,1280]{1,0:T(1,128)S(1)} %get-tuple-element.34.refs_0_.refs_12_) | copy-start | bytes 15364
  114.6 19.0 %collective-permute-start.12 = (bf16[32,4096]{1,0:T(8,128)(2,1)S(1)}, bf16[32,4096]{1,0:T(8,128)(2,1)S(1)}, u32[]{:S(2)}, u32[]{:S(2)}) collective-permute-start(bf16[32,4096]{1,0:T(8,128)(2,1)S(1)} %shard_map.81), channel_id=1, source_target_pairs={{128,0},{160,32},{192,64},{224,96},{129,1},{161,33},{193,65},{225,... | collective-permute-start | bytes 786440 | tf_op jit(solution)/shard_map/ppermute | solution.py:211
  115.9 22.0 %collective-permute-start.13 = (bf16[32,4096]{1,0:T(8,128)(2,1)S(1)}, bf16[32,4096]{1,0:T(8,128)(2,1)S(1)}, u32[]{:S(2)}, u32[]{:S(2)}) collective-permute-start(bf16[32,4096]{1,0:T(8,128)(2,1)S(1)} %shard_map.81), channel_id=1, source_target_pairs={{128,32},{160,64},{192,96},{224,0},{129,33},{161,65},{193,97},{225... | collective-permute-start | bytes 786440 | tf_op jit(solution)/shard_map/ppermute | solution.py:211
  117.2 28.6 %collective-permute-start.16 = (bf16[128,1280]{1,0:T(8,128)(2,1)}, bf16[128,1280]{1,0:T(8,128)(2,1)S(1)}, u32[]{:S(2)}, u32[]{:S(2)}) collective-permute-start(bf16[128,1280]{1,0:T(8,128)(2,1)} %copy-done.26), channel_id=1, source_target_pairs={{0,3},{1,0},{2,1},{3,2},{4,7},{5,4},{6,5},{7,6},{8,11},{9,8},{10,9... | collective-permute-start | bytes 983048 | tf_op jit(solution)/shard_map/ppermute | solution.py:207
  121.8 24.0 %collective-permute-start.17 = (bf16[128,1280]{1,0:T(8,128)(2,1)}, bf16[128,1280]{1,0:T(8,128)(2,1)S(1)}, u32[]{:S(2)}, u32[]{:S(2)}) collective-permute-start(bf16[128,1280]{1,0:T(8,128)(2,1)} %copy-done.25), channel_id=1, source_target_pairs={{0,2},{1,3},{2,0},{3,1},{4,6},{5,7},{6,4},{7,5},{8,10},{9,11},{10,... | collective-permute-start | bytes 983048 | tf_op jit(solution)/shard_map/ppermute | solution.py:207
  124.5 21.3 %collective-permute-start.18 = (bf16[128,1280]{1,0:T(8,128)(2,1)}, bf16[128,1280]{1,0:T(8,128)(2,1)S(1)}, u32[]{:S(2)}, u32[]{:S(2)}) collective-permute-start(bf16[128,1280]{1,0:T(8,128)(2,1)} %copy-done.24), channel_id=1, source_target_pairs={{0,1},{1,2},{2,3},{3,0},{4,5},{5,6},{6,7},{7,4},{8,9},{9,10},{10,1... | collective-permute-start | bytes 983048 | tf_op jit(solution)/shard_map/ppermute | solution.py:207
  133.5 12.3 %copy-start.30 = (bf16[32,4096]{1,0:T(8,128)(2,1)}, bf16[32,4096]{1,0:T(8,128)(2,1)S(1)}, u32[]{:S(2)}) copy-start(bf16[32,4096]{1,0:T(8,128)(2,1)S(1)} %collective-permute-done.12.refs_4_) | copy-start | bytes 786436
  133.5 9.4 %collective-permute-start.14 = (bf16[32,4096]{1,0:T(8,128)(2,1)S(1)}, bf16[32,4096]{1,0:T(8,128)(2,1)S(1)}, u32[]{:S(2)}, u32[]{:S(2)}) collective-permute-start(bf16[32,4096]{1,0:T(8,128)(2,1)S(1)} %shard_map.81), channel_id=1, source_target_pairs={{128,64},{160,96},{192,0},{224,32},{129,65},{161,97},{193,1},{225,... | collective-permute-start | bytes 786440 | tf_op jit(solution)/shard_map/ppermute | solution.py:211
  137.9 8.0 %copy-start.31 = (bf16[32,4096]{1,0:T(8,128)(2,1)}, bf16[32,4096]{1,0:T(8,128)(2,1)S(1)}, u32[]{:S(2)}) copy-start(bf16[32,4096]{1,0:T(8,128)(2,1)S(1)} %collective-permute-done.13.refs_5_) | copy-start | bytes 786436
  137.9 7.9 %collective-permute-start.15 = (bf16[32,4096]{1,0:T(8,128)(2,1)S(1)}, bf16[32,4096]{1,0:T(8,128)(2,1)S(1)}, u32[]{:S(2)}, u32[]{:S(2)}) collective-permute-start(bf16[32,4096]{1,0:T(8,128)(2,1)S(1)} %shard_map.81), channel_id=1, source_target_pairs={{128,96},{160,0},{192,32},{224,64},{129,97},{161,1},{193,33},{225,... | collective-permute-start | bytes 786440 | tf_op jit(solution)/shard_map/ppermute | solution.py:211
  (24 other events, 33.1 us)
Sparse Core Ops, SparseCore 0:
  9.5 45.2 all-gather.3
  56.6 40.9 all-gather.5

commit v5 on v4

--- a/solution.py
+++ b/solution.py
@@ -18,7 +18,6 @@
 F32 = jnp.float32
 BF16 = jnp.bfloat16
 VMEM = pl.BlockSpec(memory_space=pltpu.VMEM)
-HBM = pl.BlockSpec(memory_space=pltpu.HBM)
 ANY = pl.BlockSpec(memory_space=pl.ANY)
 
 
@@ -34,11 +33,11 @@
     return lax.dot_general(a, b, (((0,), (0,)), ((), ())), preferred_element_type=F32)
 
 
-def call(kernel, outs, args, flops, vmem=14, unread=0, scratch=(), far=()):
+def call(kernel, outs, args, flops, vmem=14, unread=0, scratch=()):
     return pl.pallas_call(
         kernel,
         out_shape=outs,
-        in_specs=[HBM if i in far else VMEM for i in range(len(args) - unread)] + [ANY] * unread,
+        in_specs=[VMEM] * (len(args) - unread) + [ANY] * unread,
         out_specs=jax.tree.map(lambda _: VMEM, outs),
         scratch_shapes=scratch,
         compiler_params=pltpu.CompilerParams(vmem_limit_bytes=vmem * 1024 * 1024),
@@ -81,39 +80,16 @@
     return heads + [dot_tn(grad_scores, queries), dot_tn(weights.astype(BF16), grads)]
 
 
-def slab_products(hidden, slab_ref, held_ref, sems):
-    copies = [
-        pltpu.make_async_copy(slab_ref.at[pl.ds(z, 2)], held_ref.at[pl.ds(z, 2)], sems.at[z // 2])
-        for z in range(0, NZ, 2)
-    ]
-    for copy in copies:
-        copy.start()
+def slab_kernel(*refs):
+    hidden, slab_ref, outs, done_ref = refs[:NY], refs[NY], refs[-NY - 1 : -1], refs[-1]
+    done_ref[...] = jnp.zeros_like(done_ref)
     for k in range(NY):
         total = None
         for z in range(0, NZ, 2):
-            if k == 0:
-                copies[z // 2].wait()
-            pair = jnp.concatenate([held_ref[z], held_ref[z + 1]], axis=1)
+            pair = jnp.concatenate([slab_ref[z], slab_ref[z + 1]], axis=1)
             term = dot_nt(hidden[k][:, z * HD : (z + 2) * HD], pair)
             total = term if total is None else total + term
-        yield k, total
-
-
-def packed_kernel(*refs):
-    hidden, slab_ref, outs, (held_ref, sems) = refs[:NY], refs[NY], refs[NY + 1 : -2], refs[-2:]
-    for k, total in slab_products(hidden, slab_ref, held_ref, sems):
         outs[k][...] = total.astype(BF16)
-
-
-def sign_kernel(*refs):
-    hidden, slab_ref, rows = refs[:NY], refs[NY], refs[NY + 1 : 2 * NY + 1]
-    *outs, upper_ref, held_ref, sems = refs[2 * NY + 2 :]
-    upper = None
-    for k, total in slab_products(hidden, slab_ref, held_ref, sems):
-        outs[k][...] = total.astype(BF16)
-        term = jnp.sum(rows[k][...].astype(F32) * total, axis=0, keepdims=True)
-        upper = term if upper is None else upper + term
-    upper_ref[...] = upper
 
 
 def summed(parts, h):
@@ -135,7 +111,8 @@
 
 
 def back_kernel(*refs):
-    rows, slab_ref, out_ref = refs[:NY], refs[NY], refs[-1]
+    rows, slab_ref, out_ref, done_ref = refs[:NY], refs[NY], refs[-2], refs[-1]
+    done_ref[...] = jnp.zeros_like(done_ref)
     y_index = lax.axis_index("y")
     chunk = out_ref.shape[1]
     for k in range(NY):
@@ -168,38 +145,26 @@
     out_ref[...] = (cotangent_ref[rows, :].astype(F32) + factor * (grad - normed * mean)).astype(BF16)
 
 
-def lower_kernel(count, *refs):
-    parts, arrived, projected = refs[:NY], refs[NY : NY + NX], refs[NY + NX : 2 * NY + NX]
-    upper_ref, weight_ref, out_ref, rows_ref, mixed_ref, held_ref, sems = refs[2 * NY + NX :]
+def lower_kernel(count, mixed_ref, upper_ref, *refs):
+    parts, projected, out_ref, turned_ref = refs[:NY], refs[NY:-2], refs[-2], refs[-1]
+    pipe_index = lax.axis_index("pipe")
     x_index = lax.axis_index("tensor")
-    pipe_index = lax.axis_index("pipe")
-    chunk = arrived[0].shape[0]
-    depth = held_ref.shape[1]
-    steps = held_ref.shape[0]
-    copies = [
-        pltpu.make_async_copy(weight_ref.at[pl.ds(i * depth, depth)], held_ref.at[i], sems.at[i])
-        for i in range(steps)
-    ]
-    for copy in copies:
-        copy.start()
+    chunk = turned_ref.shape[0] // NX
     for j in range(NX):
         place = pl.multiple_of(((x_index - j + NX) % NX) * chunk, chunk)
-        rows_ref[pl.ds(place, chunk), :] = arrived[j][...]
-    for i, copy in enumerate(copies):
-        copy.wait()
-        term = dot_nn(rows_ref[:, i * depth : (i + 1) * depth], held_ref[i])
-        mixed_ref[...] = term if i == 0 else mixed_ref[...] + term
+        turned_ref[pl.ds(place, chunk), :] = mixed_ref[j * chunk : (j + 1) * chunk]
     columns = attention_back(
         lambda h: summed(parts, h),
-        lambda h: mixed_ref[:, h * HD : (h + 1) * HD].astype(BF16),
+        lambda h: turned_ref[:, h * HD : (h + 1) * HD],
     )
     for h, column in enumerate(columns):
         at = slice(h * HD, (h + 1) * HD)
+        lower = column.astype(BF16).astype(F32)
+        kept = jnp.where(pipe_index == 1, upper_ref[:, at].astype(F32), lower)
         product = projected[0][:, at].astype(F32)
         for other in projected[1:]:
             product = product + other[:, at].astype(F32)
-        lower = jnp.sum(column.astype(BF16).astype(F32) * product, axis=0, keepdims=True)
-        out_ref[:, at] = jnp.where(pipe_index == 1, upper_ref[:, at], lower) * (1.0 / count)
+        out_ref[:, at] = jnp.sum(kept * product, axis=0, keepdims=True) * (1.0 / count)
 
 
 def send_y(value, steps, pipes=(0, 1)):
@@ -229,60 +194,41 @@
     grad_mixed = dot_nn(cotangent, weight_out).astype(BF16)
 
     flops = 2 * tokens * rows * width
-    slab_scratch = [pltpu.VMEM((NZ, rows, HD), BF16), pltpu.SemaphoreType.DMA((NZ // 2,))]
     packed_rows = jax.ShapeDtypeStruct((tokens, rows), BF16)
-    partial = call(
-        packed_kernel, (packed_rows,) * NY, (*hidden_slab, weight_slab), flops, scratch=slab_scratch, far=(NY,), vmem=60
-    )
-    parts = [partial[0]] + [send_y(partial[k], -k, (1,)) for k in range(1, NY)]
+    done = jax.ShapeDtypeStruct((8, HD), F32)
+    *partial, _ = call(slab_kernel, (packed_rows,) * NY + (done,), (*hidden_slab, weight_slab), flops)
+    parts = [partial[0]] + [send_y(partial[k], -k) for k in range(1, NY)]
     grad_upper = call(upper_kernel, packed_rows, (grad_mixed, *parts), 10**8)
-
-    slab_rows = [grad_upper] + [send_y(grad_upper, k, (1,)) for k in range(1, NY)]
-    later = lax.optimization_barrier((*partial, grad_upper))
-    parts = [partial[0]] + [send_y(later[k], -k, (0,)) for k in range(1, NY)]
-    back = call(
+    slab_rows = [grad_upper] + [send_y(grad_upper, k) for k in range(1, NY)]
+    back, after_back = call(
         back_kernel,
-        jax.ShapeDtypeStruct((NX * NY, chunk, NZ * HD), BF16),
+        (jax.ShapeDtypeStruct((NX * NY, chunk, NZ * HD), BF16), done),
         (*slab_rows, weight_slab),
         flops,
     )
-    *signed, upper_total = call(
-        sign_kernel,
-        (packed_rows,) * NY + (jax.ShapeDtypeStruct((1, rows), F32),),
-        (*hidden_slab, sign_slab, *slab_rows, back),
-        flops,
-        unread=1,
-        scratch=slab_scratch,
-        far=(NY,),
-        vmem=44,
-    )
-    projected = [signed[0]] + [send_y(signed[k], -k, (0,)) for k in range(1, NY)]
+    *signed, after_signed = call(
+        slab_kernel, (packed_rows,) * NY + (done,), (*hidden_slab, sign_slab, after_back), flops, unread=1
+    )
+    projected = [signed[0]] + [send_y(signed[k], -k) for k in range(1, NY)]
     terms = lax.all_to_all(back, ("tensor", "y"), 0, 0)
     backward = call(
         norm_back_kernel,
         jax.ShapeDtypeStruct((chunk, width), BF16),
-        (inputs, norm_gain, cotangent, terms, upper_total, *parts[1:]),
+        (inputs, norm_gain, cotangent, terms, after_signed),
         10**6,
-        unread=NY,
+        unread=1,
     )
     arrived = [send_down(backward, j) for j in range(NX)]
-    args = (*parts, *arrived, *projected, upper_total, weight_out)
-    depth = width // 8
-    result = pl.pallas_call(
+    grad_mixed_lower = dot_nn(jnp.concatenate(arrived, axis=0), weight_out).astype(BF16)
+    partial_sum = call(
         functools.partial(lower_kernel, tokens * NZ * NY),
-        out_shape=jax.ShapeDtypeStruct((1, rows), F32),
-        in_specs=[VMEM] * (len(args) - 1) + [HBM],
-        out_specs=VMEM,
-        scratch_shapes=[
-            pltpu.VMEM((tokens, width), BF16),
-            pltpu.VMEM((tokens, QH * HD), F32),
-            pltpu.VMEM((8, depth, QH * HD), BF16),
-            pltpu.SemaphoreType.DMA((8,)),
-        ],
-        compiler_params=pltpu.CompilerParams(vmem_limit_bytes=56 * 1024 * 1024),
-        cost_estimate=pl.CostEstimate(flops=flops, bytes_accessed=100000, transcendentals=131072),
-    )(*args)
-    return lax.psum(lax.psum(result, "y"), "z")
+        jax.ShapeDtypeStruct((1, rows), F32),
+        (grad_mixed_lower, grad_upper, *parts, *projected),
+        10**8,
+        scratch=[pltpu.VMEM((tokens, QH * HD), BF16)],
+    )
+    copies = jnp.broadcast_to(partial_sum, (NZ * NY, rows))
+    return jnp.sum(lax.all_to_all(copies, ("z", "y"), 0, 0), axis=0, keepdims=True)
 
 
 def solution(mesh):

time: 191 us -> 175 us (0.916)
  waiting for transfers between devices: 55.1 us -> 74.8 us
  starting transfers between devices: 43.3 us -> 29.8 us
  Pallas kernels: 24.6 us -> 13.3 us
  blocking collectives: 27.9 us -> 17.2 us
  matrix products: 4.75 us -> 9.45 us
  local copies, waits for them, and re-layouts: 16.5 us -> 13 us
    ppermute x15 -> x12, waiting for transfers between devices: 10.3 us -> 41.5 us  [send_y(): return lax.ppermute(value, ('pipe', 'y'), pairs)]
    psum x2 -> x0, blocking collectives: 27.9 us -> none  [local(): return lax.psum(lax.psum(result, 'y'), 'z')]
    all_to_all x0 -> x1, blocking collectives: none -> 17.2 us  [local(): lax.all_to_all(copies, ('z', 'y'), 0, 0)]
    ppermute x15 -> x12, starting transfers between devices: 30.8 us -> 18 us  [send_y(): return lax.ppermute(value, ('pipe', 'y'), pairs)]
    ppermute x4, waiting for transfers between devices: 15.7 us -> 3.89 us  [send_down(): lax.ppermute(value, ('pipe', 'tensor'), [(NX + i, (i + steps) % NX) for i...]
    pallas_call x7, Pallas kernels: 24.6 us -> 13.3 us  [call(): pl.pallas_call(kernel, out_shape=outs, in_specs=[VMEM] * (len(args) - unr...]
    dot_general x1 -> x2, matrix products: 4.75 us -> 9.45 us  [dot_nn(): lax.dot_general(a, b, (((1,), (0,)), ((), ())), preferred_element_type=F32)]
    unnamed x68 -> x64, local copies, waits for them, and re-layouts: 16.5 us -> 12.3 us
  transfers between devices with their start and end apart: 22 -> 19, of which waited for: 8 -> 14; matrix products, arithmetic and copies ran while one was open for 3% -> 5% of each run, Pallas kernels for 9% -> 7%
where the time goes in v5:
time: 175 us; the launch traced here: 174 us
  waiting for transfers between devices  74.8 us (43%)
  starting transfers between devices  29.8 us (17%)
  blocking collectives  17.2 us (10%)
  between operations  13.7 us (8%)
  Pallas kernels  13.3 us (8%)
  local copies, waits for them, and re-layouts  13 us (7%)
  matrix products  9.45 us (5%)
  other arithmetic  2.88 us (2%)
    ppermute x12, waiting for transfers between devices, send_y(): return lax.ppermute(value, ('pipe', 'y'), pairs)  41.5 us
    all_gather x1, waiting for transfers between devices, local(): weight_slab = lax.all_gather(weight, 'z', axis=0, tiled=False)  26.4 us
    ppermute x12, starting transfers between devices, send_y(): return lax.ppermute(value, ('pipe', 'y'), pairs)  18 us
    all_to_all x1, blocking collectives, local(): lax.all_to_all(copies, ('z', 'y'), 0, 0)  17.2 us
    pallas_call x7, Pallas kernels, call(): pl.pallas_call(kernel, out_shape=outs, in_specs=[VMEM] * (len(args) - unr...  13.3 us
    unnamed x64, local copies, waits for them, and re-layouts  12.3 us
    dot_general x2, matrix products, dot_nn(): lax.dot_general(a, b, (((1,), (0,)), ((), ())), preferred_element_type=F32)  9.45 us
    all_to_all x1, starting transfers between devices, local(): terms = lax.all_to_all(back, ('tensor', 'y'), 0, 0)  6.6 us
  transfers between devices with their start and end apart: 19, of which 14 were waited for; matrix products, arithmetic and copies ran while one was open for 5% of the time, Pallas kernels for 7%

profile of v5, /device:TPU:2, one launch (start us, length us, event | category | flops | bytes accessed | tf_op | source)
XLA Modules:
  0.0 174.2 jit_solution(13431792398309852223)
XLA Ops:
  7.2 2.0 %add_convert_fusion = bf16[1,1280,128]{2,1,0:T(8,128)(2,1)} fusion(bf16[1,1280,128]{2,1,0:T(8,128)(2,1)} %param.11, bf16[1,1280,128]{2,1,0:T(8,128)(2,1)} %param.10, f32[1280]{0:T(1024)S(1)} %reduce.1), kind=kLoop, calls=%fused_computation.13 | loop fusion | flops 819200 | bytes 988160 | tf_op jit(solution)/shard_map/convert_element_type | solution.py:186
  12.1 1.7 collective-permute-start
  13.7 2.9 %collective-permute-start.1 = (bf16[128,1024]{1,0:T(8,128)(2,1)S(1)}, bf16[128,1024]{1,0:T(8,128)(2,1)S(1)}, u32[]{:S(2)}, u32[]{:S(2)}) collective-permute-start(bf16[128,1024]{1,0:T(8,128)(2,1)S(1)} %get-tuple-element.23), channel_id=1, source_target_pairs={{0,2},{1,3},{2,0},{3,1},{128,130},{129,131},{130,128},{131,129},{4... | collective-permute-start | bytes 786440 | tf_op jit(solution)/shard_map/ppermute | solution.py:172
  16.6 1.3 collective-permute-start.2
  18.0 3.5 %collective-permute-done.refs_1_ = bf16[128,1024]{1,0:T(8,128)(2,1)S(1)} collective-permute-done((bf16[128,1024]{1,0:T(8,128)(2,1)S(1)}, bf16[128,1024]{1,0:T(8,128)(2,1)S(1)}, u32[]{:S(2)}, u32[]{:S(2)}) %collective-permute-start) | collective-permute-done | bytes 262176 | tf_op jit(solution)/shard_map/ppermute | solution.py:172
  21.5 6.8 %collective-permute-done.1.refs_2_ = bf16[128,1024]{1,0:T(8,128)(2,1)S(1)} collective-permute-done((bf16[128,1024]{1,0:T(8,128)(2,1)S(1)}, bf16[128,1024]{1,0:T(8,128)(2,1)S(1)}, u32[]{:S(2)}, u32[]{:S(2)}) %collective-permute-start.1) | collective-permute-done | bytes 262176 | tf_op jit(solution)/shard_map/ppermute | solution.py:172
  28.3 26.4 %all-gather.4.cloned.1.call-done.refs_4_ = bf16[8,1280,128]{2,1,0:T(8,128)(2,1)} async-done(((bf16[1,1280,128]{2,1,0:T(8,128)(2,1)}), bf16[8,1280,128]{2,1,0:T(8,128)(2,1)}) %all-gather.4.cloned.1.call-update) | async-done | bytes 2621456 | tf_op jit(solution)/shard_map/all_gather | solution.py:187
  54.7 1.8 %copy-done.15 = bf16[8,1280,128]{2,1,0:T(8,128)(2,1)S(1)} copy-done((bf16[8,1280,128]{2,1,0:T(8,128)(2,1)S(1)}, bf16[8,1280,128]{2,1,0:T(8,128)(2,1)}, u32[]{:S(2)}) %copy-start.15) | copy-done | bytes 2621464
  56.5 3.9 %shard_map.77 = (bf16[128,1280]{1,0:T(8,128)(2,1)S(1)}, bf16[128,1280]{1,0:T(8,128)(2,1)S(1)}, bf16[128,1280]{1,0:T(8,128)(2,1)S(1)}, bf16[128,1280]{1,0:T(8,128)(2,1)S(1)}, f32[8,128]{1,0:T(8,128)}) custom-call(bf16[128,1024]{1,0:T(8,128)(2,1)S(1)} %get-tuple-element.21.refs_0_, bf16[128,1024]{1,0:T(8,128)(2,1)S(1)} %collective-permute-done.refs_1_, ...), custom_call_target="tpu_custom_call" | custom-call | flops 1342177280 | bytes 100000 | tf_op jit(solution)/shard_map/pallas_call | solution.py:37
  60.5 2.8 %collective-permute-start.3 = (bf16[128,1280]{1,0:T(8,128)(2,1)S(1)}, bf16[128,1280]{1,0:T(8,128)(2,1)S(1)}, u32[]{:S(2)}, u32[]{:S(2)}) collective-permute-start(bf16[128,1280]{1,0:T(8,128)(2,1)S(1)} %get-tuple-element.26), channel_id=1, source_target_pairs={{0,3},{1,0},{2,1},{3,2},{128,131},{129,128},{130,129},{131,130},{4... | collective-permute-start | bytes 983048 | tf_op jit(solution)/shard_map/ppermute | solution.py:172
  65.0 4.7 %fusion.4.grad_ref = bf16[128,1024]{1,0:T(8,128)(2,1)S(1)} fusion(bf16[128,4096]{1,0:T(8,128)(2,1)S(1)} %copy-done, bf16[1,4096,1024]{2,1,0:T(8,128)(2,1)} %param.13), kind=kOutput, calls=%fused_computation.4 | convolution fusion | flops 1073872896 | bytes 9699328 | tf_op jit(solution)/shard_map/dot_general | solution.py:25
  69.8 4.6 %collective-permute-done.3.refs_1_ = bf16[128,1280]{1,0:T(8,128)(2,1)S(1)} collective-permute-done((bf16[128,1280]{1,0:T(8,128)(2,1)S(1)}, bf16[128,1280]{1,0:T(8,128)(2,1)S(1)}, u32[]{:S(2)}, u32[]{:S(2)}) %collective-permute-start.3) | collective-permute-done | bytes 327712 | tf_op jit(solution)/shard_map/ppermute | solution.py:172
  74.7 3.4 %collective-permute-done.5.refs_3_ = bf16[128,1280]{1,0:T(8,128)(2,1)S(1)} collective-permute-done((bf16[128,1280]{1,0:T(8,128)(2,1)S(1)}, bf16[128,1280]{1,0:T(8,128)(2,1)S(1)}, u32[]{:S(2)}, u32[]{:S(2)}) %collective-permute-start.5) | collective-permute-done | bytes 327712 | tf_op jit(solution)/shard_map/ppermute | solution.py:172
  79.2 2.1 %collective-permute-start.7 = (bf16[128,1280]{1,0:T(8,128)(2,1)S(1)}, bf16[128,1280]{1,0:T(8,128)(2,1)S(1)}, u32[]{:S(2)}, u32[]{:S(2)}) collective-permute-start(bf16[128,1280]{1,0:T(8,128)(2,1)S(1)} %shard_map.78.refs_0_.upper_ref), channel_id=1, source_target_pairs={{0,2},{1,3},{2,0},{3,1},{128,130},{129,131},{130,128},{131,129},{4... | collective-permute-start | bytes 983048 | tf_op jit(solution)/shard_map/ppermute | solution.py:172
  81.3 1.4 collective-permute-start.8
  82.6 13.4 %collective-permute-done.6.refs_1_ = bf16[128,1280]{1,0:T(8,128)(2,1)S(1)} collective-permute-done((bf16[128,1280]{1,0:T(8,128)(2,1)S(1)}, bf16[128,1280]{1,0:T(8,128)(2,1)S(1)}, u32[]{:S(2)}, u32[]{:S(2)}) %collective-permute-start.6) | collective-permute-done | bytes 327712 | tf_op jit(solution)/shard_map/ppermute | solution.py:172
  96.7 2.7 %shard_map.79 = (bf16[16,32,1024]{2,1,0:T(8,128)(2,1)}, f32[8,128]{1,0:T(8,128)S(1)}) custom-call(bf16[128,1280]{1,0:T(8,128)(2,1)S(1)} %shard_map.78.refs_0_.upper_ref, bf16[128,1280]{1,0:T(8,128)(2,1)S(1)} %collective-permute-done.6.refs_1_, bf16[128,1280]{1,0:T(8,128)(2,1)S(1)} %collective-permute-done.7.refs_2_, ...), custom_call_target="tpu_custom_call" | custom-call | flops 1342177280 | bytes 100000 | tf_op jit(solution)/shard_map/pallas_call | solution.py:37
  99.4 6.6 %all-to-all-start = ((bf16[16,32,1024]{2,1,0:T(8,128)(2,1)}), bf16[16,32,1024]{2,1,0:T(8,128)(2,1)S(1)}, u32[]{:S(2)}, u32[]{:S(2)}) async-start(bf16[16,32,1024]{2,1,0:T(8,128)(2,1)} %get-tuple-element.29), calls=%async_computation | async-start | bytes 2097152 | tf_op jit(solution)/shard_map/all_to_all | solution.py:213
  106.0 1.8 %copy-done.17 = bf16[10240,128]{1,0:T(8,128)(2,1)S(1)} copy-done((bf16[10240,128]{1,0:T(8,128)(2,1)S(1)}, bf16[10240,128]{1,0:T(8,128)(2,1)}, u32[]{:S(2)}) %copy-start.17) | copy-done | bytes 2621464
  111.6 3.4 %shard_map.80 = (bf16[128,1280]{1,0:T(8,128)(2,1)S(1)}, bf16[128,1280]{1,0:T(8,128)(2,1)S(1)}, bf16[128,1280]{1,0:T(8,128)(2,1)S(1)}, bf16[128,1280]{1,0:T(8,128)(2,1)S(1)}, f32[8,128]{1,0:T(8,128)S(1)}) custom-call(bf16[128,1024]{1,0:T(8,128)(2,1)S(1)} %copy-done.25, bf16[128,1024]{1,0:T(8,128)(2,1)S(1)} %copy-done.27, bf16[128,1024]{1,0:T(8,128)(2,1)S(1)} %copy-done.29, ...), custom_call_target="tpu_custom_call" | custom-call | flops 1342177280 | bytes 100000 | tf_op jit(solution)/shard_map/pallas_call | solution.py:37
  118.0 2.9 %all-to-all-done.terms_ref = bf16[16,32,1024]{2,1,0:T(8,128)(2,1)S(1)} async-done(((bf16[16,32,1024]{2,1,0:T(8,128)(2,1)}), bf16[16,32,1024]{2,1,0:T(8,128)(2,1)S(1)}, u32[]{:S(2)}, u32[]{:S(2)}) %all-to-all-start) | async-done | bytes 1048608 | tf_op jit(solution)/shard_map/all_to_all | solution.py:213
  121.5 1.3 collective-permute-start.12
  122.8 1.3 collective-permute-start.11
  124.1 1.3 collective-permute-start.10
  126.7 1.5 collective-permute-start.13
  129.1 2.0 %collective-permute-start.14 = (bf16[128,1280]{1,0:T(8,128)(2,1)S(1)}, bf16[128,1280]{1,0:T(8,128)(2,1)S(1)}, u32[]{:S(2)}, u32[]{:S(2)}) collective-permute-start(bf16[128,1280]{1,0:T(8,128)(2,1)S(1)} %copy-done.21), channel_id=1, source_target_pairs={{0,2},{1,3},{2,0},{3,1},{128,130},{129,131},{130,128},{131,129},{4... | collective-permute-start | bytes 983048 | tf_op jit(solution)/shard_map/ppermute | solution.py:172
  131.2 1.5 collective-permute-done.11
  133.3 1.3 collective-permute-done.10
  134.7 4.7 %fusion.7.mixed_ref = bf16[128,1024]{1,0:T(8,128)(2,1)S(1)} fusion(bf16[1,4096,1024]{2,1,0:T(8,128)(2,1)} %param.13, bf16[32,4096]{1,0:T(8,128)(2,1)S(1)} %collective-permute-done.12, bf16[32,4096]{1,0:T(8,128)(2,1)S(1)} %collective-permute-done.11, bf16[32,4096]{1,0:T(8,128)(2,1)S(1)} %collective-permute-done.10, ...), kind=kOutput, calls=%fused_computation.5 | convolution fusion | flops 1078067200 | bytes 9699328 | tf_op jit(solution)/shard_map/dot_general | solution.py:25
  139.4 1.7 collective-permute-done.14.refs_6_
  141.1 7.2 %collective-permute-done.15.refs_7_ = bf16[128,1280]{1,0:T(8,128)(2,1)S(1)} collective-permute-done((bf16[128,1280]{1,0:T(8,128)(2,1)S(1)}, bf16[128,1280]{1,0:T(8,128)(2,1)S(1)}, u32[]{:S(2)}, u32[]{:S(2)}) %collective-permute-start.15) | collective-permute-done | bytes 327712 | tf_op jit(solution)/shard_map/ppermute | solution.py:172
  149.5 17.2 %all_to_all.11 = f32[32,1,1280]{2,1,0:T(1,128)S(1)} all-to-all(f32[32,1,1280]{2,1,0:T(1,128)S(1)} %broadcast_in_dim.8), channel_id=1, replica_groups=mesh['pipe'=2,'tensor'=4,'z'=8,'y'=4] {'z','y'}, dimensions={0} | all-to-all | bytes 327680 | tf_op jit(solution)/shard_map/all_to_all | solution.py:231
  (88 shorter events, 19.2 us)
Async XLA Ops:
  6.5 48.2 %all-gather.4.cloned.1.call-start = ((), (), s32[]{:S(2)}) async-start(), calls=%async_computation.2 | async-start | bytes 2949120 | tf_op jit(solution)/shard_map/all_gather | solution.py:187
  9.3 96.7 %all-gather.6.cloned.1.call-start = ((), (), s32[]{:S(2)}) async-start(), calls=%async_computation.3 | async-start | bytes 2949120 | tf_op jit(solution)/shard_map/all_gather | solution.py:193
  12.1 48.4 %copy-start.24 = (bf16[128,1024]{1,0:T(8,128)(2,1)}, bf16[128,1024]{1,0:T(8,128)(2,1)S(1)}, u32[]{:S(2)}) copy-start(bf16[128,1024]{1,0:T(8,128)(2,1)S(1)} %get-tuple-element.21.refs_0_) | copy-start | bytes 786436
  12.1 9.4 %collective-permute-start = (bf16[128,1024]{1,0:T(8,128)(2,1)S(1)}, bf16[128,1024]{1,0:T(8,128)(2,1)S(1)}, u32[]{:S(2)}, u32[]{:S(2)}) collective-permute-start(bf16[128,1024]{1,0:T(8,128)(2,1)S(1)} %get-tuple-element.22), channel_id=1, source_target_pairs={{0,1},{1,2},{2,3},{3,0},{128,129},{129,130},{130,131},{131,128},{4... | collective-permute-start | bytes 786440 | tf_op jit(solution)/shard_map/ppermute | solution.py:172
  13.7 14.5 %collective-permute-start.1 = (bf16[128,1024]{1,0:T(8,128)(2,1)S(1)}, bf16[128,1024]{1,0:T(8,128)(2,1)S(1)}, u32[]{:S(2)}, u32[]{:S(2)}) collective-permute-start(bf16[128,1024]{1,0:T(8,128)(2,1)S(1)} %get-tuple-element.23), channel_id=1, source_target_pairs={{0,2},{1,3},{2,0},{3,1},{128,130},{129,131},{130,128},{131,129},{4... | collective-permute-start | bytes 786440 | tf_op jit(solution)/shard_map/ppermute | solution.py:172
  16.6 11.6 %collective-permute-start.2 = (bf16[128,1024]{1,0:T(8,128)(2,1)S(1)}, bf16[128,1024]{1,0:T(8,128)(2,1)S(1)}, u32[]{:S(2)}, u32[]{:S(2)}) collective-permute-start(bf16[128,1024]{1,0:T(8,128)(2,1)S(1)} %get-tuple-element.24), channel_id=1, source_target_pairs={{0,3},{1,0},{2,1},{3,2},{128,131},{129,128},{130,129},{131,130},{4... | collective-permute-start | bytes 786440 | tf_op jit(solution)/shard_map/ppermute | solution.py:172
  21.5 39.0 %copy-start.26 = (bf16[128,1024]{1,0:T(8,128)(2,1)}, bf16[128,1024]{1,0:T(8,128)(2,1)S(1)}, u32[]{:S(2)}) copy-start(bf16[128,1024]{1,0:T(8,128)(2,1)S(1)} %collective-permute-done.refs_1_) | copy-start | bytes 786436
  28.3 32.2 %copy-start.28 = (bf16[128,1024]{1,0:T(8,128)(2,1)}, bf16[128,1024]{1,0:T(8,128)(2,1)S(1)}, u32[]{:S(2)}) copy-start(bf16[128,1024]{1,0:T(8,128)(2,1)S(1)} %collective-permute-done.1.refs_2_) | copy-start | bytes 786436
  28.3 32.2 %copy-start.30 = (bf16[128,1024]{1,0:T(8,128)(2,1)}, bf16[128,1024]{1,0:T(8,128)(2,1)S(1)}, u32[]{:S(2)}) copy-start(bf16[128,1024]{1,0:T(8,128)(2,1)S(1)} %collective-permute-done.2.refs_3_) | copy-start | bytes 786436
  60.5 13.9 %collective-permute-start.3 = (bf16[128,1280]{1,0:T(8,128)(2,1)S(1)}, bf16[128,1280]{1,0:T(8,128)(2,1)S(1)}, u32[]{:S(2)}, u32[]{:S(2)}) collective-permute-start(bf16[128,1280]{1,0:T(8,128)(2,1)S(1)} %get-tuple-element.26), channel_id=1, source_target_pairs={{0,3},{1,0},{2,1},{3,2},{128,131},{129,128},{130,129},{131,130},{4... | collective-permute-start | bytes 983048 | tf_op jit(solution)/shard_map/ppermute | solution.py:172
  63.3 11.4 %collective-permute-start.4 = (bf16[128,1280]{1,0:T(8,128)(2,1)S(1)}, bf16[128,1280]{1,0:T(8,128)(2,1)S(1)}, u32[]{:S(2)}, u32[]{:S(2)}) collective-permute-start(bf16[128,1280]{1,0:T(8,128)(2,1)S(1)} %get-tuple-element.27), channel_id=1, source_target_pairs={{0,2},{1,3},{2,0},{3,1},{128,130},{129,131},{130,128},{131,129},{4... | collective-permute-start | bytes 983048 | tf_op jit(solution)/shard_map/ppermute | solution.py:172
  64.1 32.5 %copy-start.16 = (bf16[8,1280,128]{2,1,0:T(8,128)(2,1)S(1)}, bf16[8,1280,128]{2,1,0:T(8,128)(2,1)}, u32[]{:S(2)}) copy-start(bf16[8,1280,128]{2,1,0:T(8,128)(2,1)} %all-gather.4.cloned.1.call-done.refs_4_) | copy-start | bytes 7864324
  64.1 13.9 %collective-permute-start.5 = (bf16[128,1280]{1,0:T(8,128)(2,1)S(1)}, bf16[128,1280]{1,0:T(8,128)(2,1)S(1)}, u32[]{:S(2)}, u32[]{:S(2)}) collective-permute-start(bf16[128,1280]{1,0:T(8,128)(2,1)S(1)} %get-tuple-element.28), channel_id=1, source_target_pairs={{0,1},{1,2},{2,3},{3,0},{128,129},{129,130},{130,131},{131,128},{4... | collective-permute-start | bytes 983048 | tf_op jit(solution)/shard_map/ppermute | solution.py:172
  74.4 25.0 %copy-start.3 = (bf16[128,1280]{1,0:T(8,128)(2,1)}, bf16[128,1280]{1,0:T(8,128)(2,1)S(1)}, u32[]{:S(2)}) copy-start(bf16[128,1280]{1,0:T(8,128)(2,1)S(1)} %collective-permute-done.3.refs_1_) | copy-start | bytes 983044
  74.7 24.7 %copy-start.5 = (bf16[128,1280]{1,0:T(8,128)(2,1)}, bf16[128,1280]{1,0:T(8,128)(2,1)S(1)}, u32[]{:S(2)}) copy-start(bf16[128,1280]{1,0:T(8,128)(2,1)S(1)} %collective-permute-done.4.refs_2_) | copy-start | bytes 983044
  78.1 21.3 %copy-start.7 = (bf16[128,1280]{1,0:T(8,128)(2,1)}, bf16[128,1280]{1,0:T(8,128)(2,1)S(1)}, u32[]{:S(2)}) copy-start(bf16[128,1280]{1,0:T(8,128)(2,1)S(1)} %collective-permute-done.5.refs_3_) | copy-start | bytes 983044
  79.1 20.3 %copy-start.9 = (bf16[128,1280]{1,0:T(8,128)(2,1)}, bf16[128,1280]{1,0:T(8,128)(2,1)S(1)}, u32[]{:S(2)}) copy-start(bf16[128,1280]{1,0:T(8,128)(2,1)S(1)} %shard_map.78.refs_0_.upper_ref) | copy-start | bytes 983044
  79.1 16.9 %collective-permute-start.6 = (bf16[128,1280]{1,0:T(8,128)(2,1)S(1)}, bf16[128,1280]{1,0:T(8,128)(2,1)S(1)}, u32[]{:S(2)}, u32[]{:S(2)}) collective-permute-start(bf16[128,1280]{1,0:T(8,128)(2,1)S(1)} %shard_map.78.refs_0_.upper_ref), channel_id=1, source_target_pairs={{0,1},{1,2},{2,3},{3,0},{128,129},{129,130},{130,131},{131,128},{4... | collective-permute-start | bytes 983048 | tf_op jit(solution)/shard_map/ppermute | solution.py:172
  79.2 16.9 %collective-permute-start.7 = (bf16[128,1280]{1,0:T(8,128)(2,1)S(1)}, bf16[128,1280]{1,0:T(8,128)(2,1)S(1)}, u32[]{:S(2)}, u32[]{:S(2)}) collective-permute-start(bf16[128,1280]{1,0:T(8,128)(2,1)S(1)} %shard_map.78.refs_0_.upper_ref), channel_id=1, source_target_pairs={{0,2},{1,3},{2,0},{3,1},{128,130},{129,131},{130,128},{131,129},{4... | collective-permute-start | bytes 983048 | tf_op jit(solution)/shard_map/ppermute | solution.py:172
  81.3 15.4 %collective-permute-start.8 = (bf16[128,1280]{1,0:T(8,128)(2,1)S(1)}, bf16[128,1280]{1,0:T(8,128)(2,1)S(1)}, u32[]{:S(2)}, u32[]{:S(2)}) collective-permute-start(bf16[128,1280]{1,0:T(8,128)(2,1)S(1)} %shard_map.78.refs_0_.upper_ref), channel_id=1, source_target_pairs={{0,3},{1,0},{2,1},{3,2},{128,131},{129,128},{130,129},{131,130},{4... | collective-permute-start | bytes 983048 | tf_op jit(solution)/shard_map/ppermute | solution.py:172
  99.4 21.6 %all-to-all-start = ((bf16[16,32,1024]{2,1,0:T(8,128)(2,1)}), bf16[16,32,1024]{2,1,0:T(8,128)(2,1)S(1)}, u32[]{:S(2)}, u32[]{:S(2)}) async-start(bf16[16,32,1024]{2,1,0:T(8,128)(2,1)} %get-tuple-element.29), calls=%async_computation | async-start | bytes 2097152 | tf_op jit(solution)/shard_map/all_to_all | solution.py:213
  121.5 7.7 %collective-permute-start.12 = (bf16[32,4096]{1,0:T(8,128)(2,1)S(1)}, bf16[32,4096]{1,0:T(8,128)(2,1)S(1)}, u32[]{:S(2)}, u32[]{:S(2)}) collective-permute-start(bf16[32,4096]{1,0:T(8,128)(2,1)S(1)} %shard_map.81), channel_id=1, source_target_pairs={{128,96},{160,0},{192,32},{224,64},{129,97},{161,1},{193,33},{225,... | collective-permute-start | bytes 786440 | tf_op jit(solution)/shard_map/ppermute | solution.py:176
  122.8 9.9 %collective-permute-start.11 = (bf16[32,4096]{1,0:T(8,128)(2,1)S(1)}, bf16[32,4096]{1,0:T(8,128)(2,1)S(1)}, u32[]{:S(2)}, u32[]{:S(2)}) collective-permute-start(bf16[32,4096]{1,0:T(8,128)(2,1)S(1)} %shard_map.81), channel_id=1, source_target_pairs={{128,64},{160,96},{192,0},{224,32},{129,65},{161,97},{193,1},{225,... | collective-permute-start | bytes 786440 | tf_op jit(solution)/shard_map/ppermute | solution.py:176
  124.1 10.6 %collective-permute-start.10 = (bf16[32,4096]{1,0:T(8,128)(2,1)S(1)}, bf16[32,4096]{1,0:T(8,128)(2,1)S(1)}, u32[]{:S(2)}, u32[]{:S(2)}) collective-permute-start(bf16[32,4096]{1,0:T(8,128)(2,1)S(1)} %shard_map.81), channel_id=1, source_target_pairs={{128,32},{160,64},{192,96},{224,0},{129,33},{161,65},{193,97},{225... | collective-permute-start | bytes 786440 | tf_op jit(solution)/shard_map/ppermute | solution.py:176
  125.4 9.3 %collective-permute-start.9 = (bf16[32,4096]{1,0:T(8,128)(2,1)S(1)}, bf16[32,4096]{1,0:T(8,128)(2,1)S(1)}, u32[]{:S(2)}, u32[]{:S(2)}) collective-permute-start(bf16[32,4096]{1,0:T(8,128)(2,1)S(1)} %shard_map.81), channel_id=1, source_target_pairs={{128,0},{160,32},{192,64},{224,96},{129,1},{161,33},{193,65},{225,... | collective-permute-start | bytes 786440 | tf_op jit(solution)/shard_map/ppermute | solution.py:176
  126.7 12.7 %collective-permute-start.13 = (bf16[128,1280]{1,0:T(8,128)(2,1)S(1)}, bf16[128,1280]{1,0:T(8,128)(2,1)S(1)}, u32[]{:S(2)}, u32[]{:S(2)}) collective-permute-start(bf16[128,1280]{1,0:T(8,128)(2,1)S(1)} %copy-done.23), channel_id=1, source_target_pairs={{0,3},{1,0},{2,1},{3,2},{128,131},{129,128},{130,129},{131,130},{4... | collective-permute-start | bytes 983048 | tf_op jit(solution)/shard_map/ppermute | solution.py:172
  129.1 12.0 %collective-permute-start.14 = (bf16[128,1280]{1,0:T(8,128)(2,1)S(1)}, bf16[128,1280]{1,0:T(8,128)(2,1)S(1)}, u32[]{:S(2)}, u32[]{:S(2)}) collective-permute-start(bf16[128,1280]{1,0:T(8,128)(2,1)S(1)} %copy-done.21), channel_id=1, source_target_pairs={{0,2},{1,3},{2,0},{3,1},{128,130},{129,131},{130,128},{131,129},{4... | collective-permute-start | bytes 983048 | tf_op jit(solution)/shard_map/ppermute | solution.py:172
  132.7 15.6 %copy-start.6 = (bf16[128,1280]{1,0:T(8,128)(2,1)S(1)}, bf16[128,1280]{1,0:T(8,128)(2,1)}, u32[]{:S(2)}) copy-start(bf16[128,1280]{1,0:T(8,128)(2,1)} %copy-done.5) | copy-start | bytes 983044
  132.7 15.6 %copy-start.8 = (bf16[128,1280]{1,0:T(8,128)(2,1)S(1)}, bf16[128,1280]{1,0:T(8,128)(2,1)}, u32[]{:S(2)}) copy-start(bf16[128,1280]{1,0:T(8,128)(2,1)} %copy-done.7) | copy-start | bytes 983044
  132.7 15.6 %copy-start.10 = (bf16[128,1280]{1,0:T(8,128)(2,1)S(1)}, bf16[128,1280]{1,0:T(8,128)(2,1)}, u32[]{:S(2)}) copy-start(bf16[128,1280]{1,0:T(8,128)(2,1)} %copy-done.9) | copy-start | bytes 983044
  132.7 15.6 %copy-start.12 = (bf16[128,1280]{1,0:T(8,128)(2,1)S(1)}, bf16[128,1280]{1,0:T(8,128)(2,1)}, u32[]{:S(2)}) copy-start(bf16[128,1280]{1,0:T(8,128)(2,1)} %copy-done.11) | copy-start | bytes 983044
  132.7 15.5 %collective-permute-start.15 = (bf16[128,1280]{1,0:T(8,128)(2,1)S(1)}, bf16[128,1280]{1,0:T(8,128)(2,1)S(1)}, u32[]{:S(2)}, u32[]{:S(2)}) collective-permute-start(bf16[128,1280]{1,0:T(8,128)(2,1)S(1)} %copy-done.19), channel_id=1, source_target_pairs={{0,1},{1,2},{2,3},{3,0},{128,129},{129,130},{130,131},{131,128},{4... | collective-permute-start | bytes 983048 | tf_op jit(solution)/shard_map/ppermute | solution.py:172
  (19 other events, 93.8 us)
Sparse Core Ops, SparseCore 0:
  9.4 45.2 all-gather.3
  56.5 40.9 all-gather.5

commit v6 on v5

--- a/solution.py
+++ b/solution.py
@@ -46,7 +46,8 @@
 
 
 def norm_kernel(inputs_ref, gain_ref, *refs):
-    turned_ref = refs[-1]
+    quarter_ref, turned_ref = refs[-2:]
+    quarter_ref[...] = quarter(inputs_ref)
     y_index = lax.axis_index("y")
     values = inputs_ref[...].astype(F32)
     factor = lax.rsqrt(jnp.mean(values * values, axis=-1, keepdims=True) + 1e-05)
@@ -80,16 +81,27 @@
     return heads + [dot_tn(grad_scores, queries), dot_tn(weights.astype(BF16), grads)]
 
 
-def slab_kernel(*refs):
-    hidden, slab_ref, outs, done_ref = refs[:NY], refs[NY], refs[-NY - 1 : -1], refs[-1]
-    done_ref[...] = jnp.zeros_like(done_ref)
+def slab_products(hidden, slab_ref):
     for k in range(NY):
         total = None
         for z in range(0, NZ, 2):
             pair = jnp.concatenate([slab_ref[z], slab_ref[z + 1]], axis=1)
             term = dot_nt(hidden[k][:, z * HD : (z + 2) * HD], pair)
             total = term if total is None else total + term
-        outs[k][...] = total.astype(BF16)
+        yield k, total.astype(BF16)
+
+
+def packed_kernel(*refs):
+    for k, product in slab_products(refs[:NY], refs[NY]):
+        refs[NY + 1 + k][...] = product
+
+
+def sign_kernel(*refs):
+    out_ref, done_ref = refs[-2:]
+    done_ref[...] = jnp.zeros_like(done_ref)
+    y_index = lax.axis_index("y")
+    for k, product in slab_products(refs[:NY], refs[NY]):
+        out_ref[(y_index - k + NY) % NY] = product
 
 
 def summed(parts, h):
@@ -125,11 +137,9 @@
 
 
 def norm_back_kernel(inputs_ref, gain_ref, cotangent_ref, terms_ref, *refs):
-    x_index = lax.axis_index("tensor")
     out_ref = refs[-1]
-    chunk, width = out_ref.shape
-    rows = pl.ds(pl.multiple_of(x_index * chunk, chunk), chunk)
-    values = inputs_ref[rows, :].astype(F32)
+    width = out_ref.shape[1]
+    values = inputs_ref[...].astype(F32)
     factor = lax.rsqrt(jnp.mean(values * values, axis=-1, keepdims=True) + 1e-05)
     normed = values * factor
     blocks = []
@@ -142,11 +152,30 @@
             blocks.append(block)
     grad = jnp.concatenate(blocks, axis=1) * gain_ref[...]
     mean = jnp.sum(grad * normed, axis=-1, keepdims=True) * (1.0 / width)
-    out_ref[...] = (cotangent_ref[rows, :].astype(F32) + factor * (grad - normed * mean)).astype(BF16)
-
-
-def lower_kernel(count, mixed_ref, upper_ref, *refs):
-    parts, projected, out_ref, turned_ref = refs[:NY], refs[NY:-2], refs[-2], refs[-1]
+    out_ref[...] = (cotangent_ref[...].astype(F32) + factor * (grad - normed * mean)).astype(BF16)
+
+
+def quarter(ref):
+    chunk = ref.shape[0] // NX
+    return ref[pl.ds(pl.multiple_of(lax.axis_index("tensor") * chunk, chunk), chunk), :]
+
+
+def mixed_kernel(rows_ref, weight_ref, out_ref, quarter_ref, total_ref):
+    depth = 512
+    quarter_ref[...] = quarter(rows_ref)
+    total_ref[...] = jnp.zeros_like(total_ref)
+
+    def step(i, _):
+        at = pl.ds(pl.multiple_of(i * depth, depth), depth)
+        total_ref[...] += dot_nn(rows_ref[:, at], weight_ref[at, :])
+        return 0
+
+    lax.fori_loop(0, weight_ref.shape[0] // depth, step, 0)
+    out_ref[...] = total_ref[...].astype(BF16)
+
+
+def lower_kernel(count, mixed_ref, upper_ref, projected_ref, *refs):
+    parts, out_ref, turned_ref = refs[:NY], refs[-2], refs[-1]
     pipe_index = lax.axis_index("pipe")
     x_index = lax.axis_index("tensor")
     chunk = turned_ref.shape[0] // NX
@@ -161,9 +190,7 @@
         at = slice(h * HD, (h + 1) * HD)
         lower = column.astype(BF16).astype(F32)
         kept = jnp.where(pipe_index == 1, upper_ref[:, at].astype(F32), lower)
-        product = projected[0][:, at].astype(F32)
-        for other in projected[1:]:
-            product = product + other[:, at].astype(F32)
+        product = projected_ref[:, at].astype(F32)
         out_ref[:, at] = jnp.sum(kept * product, axis=0, keepdims=True) * (1.0 / count)
 
 
@@ -187,35 +214,42 @@
     weight_slab = lax.all_gather(weight, "z", axis=0, tiled=False)
 
     slab = jax.ShapeDtypeStruct((tokens, NZ * HD), BF16)
-    hidden = call(norm_kernel, (slab,) * NY, (inputs, norm_gain), 10**7, scratch=[pltpu.VMEM((NY, *slab.shape), BF16)])
+    quarter_rows = jax.ShapeDtypeStruct((chunk, width), BF16)
+    *hidden, own_inputs = call(norm_kernel, (slab,) * NY + (quarter_rows,), (inputs, norm_gain), 10**7, scratch=[pltpu.VMEM((NY, *slab.shape), BF16)])
     hidden_slab = [hidden[0]] + [send_y(hidden[k], k) for k in range(1, NY)]
     later_sign = lax.optimization_barrier((sign, weight_slab, *hidden_slab))[0]
     sign_slab = lax.all_gather(later_sign, "z", axis=0, tiled=False)
-    grad_mixed = dot_nn(cotangent, weight_out).astype(BF16)
-
+    mixed_rows = jax.ShapeDtypeStruct((tokens, QH * HD), BF16)
+    mixed_total = [pltpu.VMEM(mixed_rows.shape, F32)]
+    grad_mixed, own_cotangent = call(mixed_kernel, (mixed_rows, quarter_rows), (cotangent, weight_out), 10**9, scratch=mixed_total)
     flops = 2 * tokens * rows * width
     packed_rows = jax.ShapeDtypeStruct((tokens, rows), BF16)
     done = jax.ShapeDtypeStruct((8, HD), F32)
-    *partial, _ = call(slab_kernel, (packed_rows,) * NY + (done,), (*hidden_slab, weight_slab), flops)
-    parts = [partial[0]] + [send_y(partial[k], -k) for k in range(1, NY)]
+    partial = call(packed_kernel, (packed_rows,) * NY, (*hidden_slab, weight_slab), flops)
+    parts = [partial[0]] + [send_y(partial[k], -k) for k in (1, 3, 2)]
     grad_upper = call(upper_kernel, packed_rows, (grad_mixed, *parts), 10**8)
-    slab_rows = [grad_upper] + [send_y(grad_upper, k) for k in range(1, NY)]
+    near, back_near, far = (send_y(grad_upper, k) for k in (1, 3, 2))
+    slab_rows = [grad_upper, near, far, back_near]
     back, after_back = call(
         back_kernel,
         (jax.ShapeDtypeStruct((NX * NY, chunk, NZ * HD), BF16), done),
         (*slab_rows, weight_slab),
         flops,
     )
-    *signed, after_signed = call(
-        slab_kernel, (packed_rows,) * NY + (done,), (*hidden_slab, sign_slab, after_back), flops, unread=1
-    )
-    projected = [signed[0]] + [send_y(signed[k], -k) for k in range(1, NY)]
+    signed, after_signed = call(
+        sign_kernel,
+        (jax.ShapeDtypeStruct((NY, tokens, rows), BF16), done),
+        (*hidden_slab, sign_slab, after_back),
+        flops,
+        unread=1,
+    )
+    projected = lax.psum_scatter(signed, "y", scatter_dimension=0)
     terms = lax.all_to_all(back, ("tensor", "y"), 0, 0)
     backward = call(
         norm_back_kernel,
         jax.ShapeDtypeStruct((chunk, width), BF16),
-        (inputs, norm_gain, cotangent, terms, after_signed),
-        10**6,
+        (own_inputs, norm_gain, own_cotangent, terms, after_signed),
+        10**11,
         unread=1,
     )
     arrived = [send_down(backward, j) for j in range(NX)]
@@ -223,9 +257,9 @@
     partial_sum = call(
         functools.partial(lower_kernel, tokens * NZ * NY),
         jax.ShapeDtypeStruct((1, rows), F32),
-        (grad_mixed_lower, grad_upper, *parts, *projected),
+        (grad_mixed_lower, grad_upper, projected, *parts),
         10**8,
-        scratch=[pltpu.VMEM((tokens, QH * HD), BF16)],
+        scratch=[pltpu.VMEM(mixed_rows.shape, BF16)],
     )
     copies = jnp.broadcast_to(partial_sum, (NZ * NY, rows))
     return jnp.sum(lax.all_to_all(copies, ("z", "y"), 0, 0), axis=0, keepdims=True)

time: 175 us -> 164 us (0.937)
  waiting for transfers between devices: 74.8 us -> 67.4 us
  matrix products: 9.45 us -> 4.78 us
  starting transfers between devices: 29.8 us -> 26 us
  Pallas kernels: 13.3 us -> 15.4 us
  blocking collectives: 17.2 us -> 19 us
    ppermute x12 -> x9, waiting for transfers between devices: 41.5 us -> 26.5 us  [send_y(): return lax.ppermute(value, ('pipe', 'y'), pairs)]
    dot_general x2 -> x1, matrix products: 9.45 us -> 4.78 us  [dot_nn(): lax.dot_general(a, b, (((1,), (0,)), ((), ())), preferred_element_type=F32)]
    ppermute x4, waiting for transfers between devices: 3.89 us -> 7.83 us  [send_down(): lax.ppermute(value, ('pipe', 'tensor'), [(NX + i, (i + steps) % NX) for i...]
    ppermute x12 -> x9, starting transfers between devices: 18 us -> 14.3 us  [send_y(): return lax.ppermute(value, ('pipe', 'y'), pairs)]
    reduce_scatter x0 -> x1, waiting for transfers between devices: none -> 3.66 us  [local(): projected = lax.psum_scatter(signed, 'y', scatter_dimension=0)]
    pallas_call x7 -> x8, Pallas kernels: 13.3 us -> 15.4 us  [call(): pl.pallas_call(kernel, out_shape=outs, in_specs=[VMEM] * (len(args) - unr...]
    unnamed x64 -> x32, local copies, waits for them, and re-layouts: 12.3 us -> 13.7 us
  transfers between devices with their start and end apart: 19 -> 17, of which waited for: 14 -> 11; matrix products, arithmetic and copies ran while one was open for 5% -> 3% of each run, Pallas kernels for 7% -> 9%
where the time goes in v6:
time: 164 us; the launch traced here: 163 us
  waiting for transfers between devices  67.4 us (41%)
  starting transfers between devices  26 us (16%)
  blocking collectives  19 us (12%)
  Pallas kernels  15.4 us (9%)
  local copies, waits for them, and re-layouts  14.4 us (9%)
  between operations  13.3 us (8%)
  matrix products  4.78 us (3%)
  other arithmetic  2.89 us (2%)
    ppermute x9, waiting for transfers between devices, send_y(): return lax.ppermute(value, ('pipe', 'y'), pairs)  26.5 us
    all_gather x1, waiting for transfers between devices, local(): weight_slab = lax.all_gather(weight, 'z', axis=0, tiled=False)  26.4 us
    all_to_all x1, blocking collectives, local(): lax.all_to_all(copies, ('z', 'y'), 0, 0)  19 us
    pallas_call x8, Pallas kernels, call(): pl.pallas_call(kernel, out_shape=outs, in_specs=[VMEM] * (len(args) - unr...  15.4 us
    ppermute x9, starting transfers between devices, send_y(): return lax.ppermute(value, ('pipe', 'y'), pairs)  14.3 us
    unnamed x32, local copies, waits for them, and re-layouts  13.7 us
    ppermute x4, waiting for transfers between devices, send_down(): lax.ppermute(value, ('pipe', 'tensor'), [(NX + i, (i + steps) % NX) for i...  7.83 us
    all_to_all x1, starting transfers between devices, local(): terms = lax.all_to_all(back, ('tensor', 'y'), 0, 0)  6.41 us
  transfers between devices with their start and end apart: 17, of which 11 were waited for; matrix products, arithmetic and copies ran while one was open for 3% of the time, Pallas kernels for 9%

profile of v6, /device:TPU:2, one launch (start us, length us, event | category | flops | bytes accessed | tf_op | source)
XLA Modules:
  0.0 163.2 jit_solution(7102631373667554110)
XLA Ops:
  7.2 2.0 %add_convert_fusion = bf16[1,1280,128]{2,1,0:T(8,128)(2,1)} fusion(bf16[1,1280,128]{2,1,0:T(8,128)(2,1)} %param.11, bf16[1,1280,128]{2,1,0:T(8,128)(2,1)} %param.10, f32[1280]{0:T(1024)S(1)} %reduce.1), kind=kLoop, calls=%fused_computation.8 | loop fusion | flops 819200 | bytes 988160 | tf_op jit(solution)/shard_map/convert_element_type | solution.py:213
  12.1 1.7 %collective-permute-start = (bf16[128,1024]{1,0:T(8,128)(2,1)S(1)}, bf16[128,1024]{1,0:T(8,128)(2,1)S(1)}, u32[]{:S(2)}, u32[]{:S(2)}) collective-permute-start(bf16[128,1024]{1,0:T(8,128)(2,1)S(1)} %get-tuple-element.25), channel_id=1, source_target_pairs={{0,1},{1,2},{2,3},{3,0},{128,129},{129,130},{130,131},{131,128},{4... | collective-permute-start | bytes 786440 | tf_op jit(solution)/shard_map/ppermute | solution.py:199
  13.8 2.9 %collective-permute-start.1 = (bf16[128,1024]{1,0:T(8,128)(2,1)S(1)}, bf16[128,1024]{1,0:T(8,128)(2,1)S(1)}, u32[]{:S(2)}, u32[]{:S(2)}) collective-permute-start(bf16[128,1024]{1,0:T(8,128)(2,1)S(1)} %get-tuple-element.26), channel_id=1, source_target_pairs={{0,2},{1,3},{2,0},{3,1},{128,130},{129,131},{130,128},{131,129},{4... | collective-permute-start | bytes 786440 | tf_op jit(solution)/shard_map/ppermute | solution.py:199
  16.7 1.3 collective-permute-start.2
  18.0 3.5 %collective-permute-done.refs_1_ = bf16[128,1024]{1,0:T(8,128)(2,1)S(1)} collective-permute-done((bf16[128,1024]{1,0:T(8,128)(2,1)S(1)}, bf16[128,1024]{1,0:T(8,128)(2,1)S(1)}, u32[]{:S(2)}, u32[]{:S(2)}) %collective-permute-start) | collective-permute-done | bytes 262176 | tf_op jit(solution)/shard_map/ppermute | solution.py:199
  21.5 6.8 %collective-permute-done.1.refs_2_ = bf16[128,1024]{1,0:T(8,128)(2,1)S(1)} collective-permute-done((bf16[128,1024]{1,0:T(8,128)(2,1)S(1)}, bf16[128,1024]{1,0:T(8,128)(2,1)S(1)}, u32[]{:S(2)}, u32[]{:S(2)}) %collective-permute-start.1) | collective-permute-done | bytes 262176 | tf_op jit(solution)/shard_map/ppermute | solution.py:199
  28.3 26.4 %all-gather.4.cloned.1.call-done.refs_4_ = bf16[8,1280,128]{2,1,0:T(8,128)(2,1)} async-done(((bf16[1,1280,128]{2,1,0:T(8,128)(2,1)}), bf16[8,1280,128]{2,1,0:T(8,128)(2,1)}) %all-gather.4.cloned.1.call-update) | async-done | bytes 2621456 | tf_op jit(solution)/shard_map/all_gather | solution.py:214
  54.7 1.7 %copy-done.7 = bf16[8,1280,128]{2,1,0:T(8,128)(2,1)S(1)} copy-done((bf16[8,1280,128]{2,1,0:T(8,128)(2,1)S(1)}, bf16[8,1280,128]{2,1,0:T(8,128)(2,1)}, u32[]{:S(2)}) %copy-start.7) | copy-done | bytes 2621464
  56.5 3.4 %shard_map.78 = (bf16[128,1280]{1,0:T(8,128)(2,1)S(1)}, bf16[128,1280]{1,0:T(8,128)(2,1)S(1)}, bf16[128,1280]{1,0:T(8,128)(2,1)S(1)}, bf16[128,1280]{1,0:T(8,128)(2,1)S(1)}) custom-call(bf16[128,1024]{1,0:T(8,128)(2,1)S(1)} %get-tuple-element.24.refs_0_, bf16[128,1024]{1,0:T(8,128)(2,1)S(1)} %collective-permute-done.refs_1_, ...), custom_call_target="tpu_custom_call" | custom-call | flops 1342177280 | bytes 100000 | tf_op jit(solution)/shard_map/pallas_call | solution.py:37
  60.0 2.8 %collective-permute-start.3 = (bf16[128,1280]{1,0:T(8,128)(2,1)S(1)}, bf16[128,1280]{1,0:T(8,128)(2,1)S(1)}, u32[]{:S(2)}, u32[]{:S(2)}) collective-permute-start(bf16[128,1280]{1,0:T(8,128)(2,1)S(1)} %get-tuple-element.29), channel_id=1, source_target_pairs={{0,3},{1,0},{2,1},{3,2},{128,131},{129,128},{130,129},{131,130},{4... | collective-permute-start | bytes 983048 | tf_op jit(solution)/shard_map/ppermute | solution.py:199
  62.8 2.3 %collective-permute-start.5 = (bf16[128,1280]{1,0:T(8,128)(2,1)S(1)}, bf16[128,1280]{1,0:T(8,128)(2,1)S(1)}, u32[]{:S(2)}, u32[]{:S(2)}) collective-permute-start(bf16[128,1280]{1,0:T(8,128)(2,1)S(1)} %get-tuple-element.31), channel_id=1, source_target_pairs={{0,2},{1,3},{2,0},{3,1},{128,130},{129,131},{130,128},{131,129},{4... | collective-permute-start | bytes 983048 | tf_op jit(solution)/shard_map/ppermute | solution.py:199
  65.1 3.5 %copy-done = bf16[1,4096,1024]{2,1,0:T(8,128)(2,1)S(1)} copy-done((bf16[1,4096,1024]{2,1,0:T(8,128)(2,1)S(1)}, bf16[1,4096,1024]{2,1,0:T(8,128)(2,1)}, u32[]{:S(2)}) %copy-start) | copy-done | bytes 8388632
  68.6 2.6 %shard_map.77 = (bf16[128,1024]{1,0:T(8,128)(2,1)S(1)}, bf16[32,4096]{1,0:T(8,128)(2,1)S(1)}) custom-call(bf16[128,4096]{1,0:T(8,128)(2,1)S(1)} %copy-done.1, bf16[4096,1024]{1,0:T(8,128)(2,1)S(1)} %bitcast.7), custom_call_target="tpu_custom_call" | custom-call | flops 1000000000 | bytes 100000 | tf_op jit(solution)/shard_map/pallas_call | solution.py:37
  71.2 2.7 %collective-permute-done.3.refs_1_ = bf16[128,1280]{1,0:T(8,128)(2,1)S(1)} collective-permute-done((bf16[128,1280]{1,0:T(8,128)(2,1)S(1)}, bf16[128,1280]{1,0:T(8,128)(2,1)S(1)}, u32[]{:S(2)}, u32[]{:S(2)}) %collective-permute-start.3) | collective-permute-done | bytes 327712 | tf_op jit(solution)/shard_map/ppermute | solution.py:199
  73.9 3.9 %collective-permute-done.4.refs_2_ = bf16[128,1280]{1,0:T(8,128)(2,1)S(1)} collective-permute-done((bf16[128,1280]{1,0:T(8,128)(2,1)S(1)}, bf16[128,1280]{1,0:T(8,128)(2,1)S(1)}, u32[]{:S(2)}, u32[]{:S(2)}) %collective-permute-start.4) | collective-permute-done | bytes 327712 | tf_op jit(solution)/shard_map/ppermute | solution.py:199
  80.1 2.0 %collective-permute-start.8 = (bf16[128,1280]{1,0:T(8,128)(2,1)S(1)}, bf16[128,1280]{1,0:T(8,128)(2,1)S(1)}, u32[]{:S(2)}, u32[]{:S(2)}) collective-permute-start(bf16[128,1280]{1,0:T(8,128)(2,1)S(1)} %shard_map.79.refs_0_.upper_ref), channel_id=1, source_target_pairs={{0,3},{1,0},{2,1},{3,2},{128,131},{129,128},{130,129},{131,130},{4... | collective-permute-start | bytes 983048 | tf_op jit(solution)/shard_map/ppermute | solution.py:199
  82.1 9.6 %collective-permute-done.6.refs_1_ = bf16[128,1280]{1,0:T(8,128)(2,1)S(1)} collective-permute-done((bf16[128,1280]{1,0:T(8,128)(2,1)S(1)}, bf16[128,1280]{1,0:T(8,128)(2,1)S(1)}, u32[]{:S(2)}, u32[]{:S(2)}) %collective-permute-start.6) | collective-permute-done | bytes 327712 | tf_op jit(solution)/shard_map/ppermute | solution.py:199
  91.8 1.6 shard_map.80
  94.4 6.4 %all-to-all-start = ((bf16[16,32,1024]{2,1,0:T(8,128)(2,1)}), bf16[16,32,1024]{2,1,0:T(8,128)(2,1)S(1)}, u32[]{:S(2)}, u32[]{:S(2)}) async-start(bf16[16,32,1024]{2,1,0:T(8,128)(2,1)} %copy-done.3), calls=%async_computation | async-start | bytes 2097152 | tf_op jit(solution)/shard_map/all_to_all | solution.py:247
  100.9 1.7 %copy-done.9 = bf16[10240,128]{1,0:T(8,128)(2,1)S(1)} copy-done((bf16[10240,128]{1,0:T(8,128)(2,1)S(1)}, bf16[10240,128]{1,0:T(8,128)(2,1)}, u32[]{:S(2)}) %copy-start.9) | copy-done | bytes 2621464
  104.5 4.5 %shard_map.81 = (bf16[4,128,1280]{2,1,0:T(8,128)(2,1)}, f32[8,128]{1,0:T(8,128)S(1)}) custom-call(bf16[128,1024]{1,0:T(8,128)(2,1)S(1)} %get-tuple-element.24.refs_0_, bf16[128,1024]{1,0:T(8,128)(2,1)S(1)} %collective-permute-done.refs_1_, bf16[128,1024]{1,0:T(8,128)(2,1)S(1)} %copy-done.11, bf16[128,1024]{1,0:T(8,128)(2,1)S(1)} %copy-done.13, ...), custom_call_target="tpu_custom_call" | custom-call | flops 1342177280 | bytes 100000 | tf_op jit(solution)/shard_map/pallas_call | solution.py:37
  109.1 2.9 %all-to-all-done.terms_ref = bf16[16,32,1024]{2,1,0:T(8,128)(2,1)S(1)} async-done(((bf16[16,32,1024]{2,1,0:T(8,128)(2,1)}), bf16[16,32,1024]{2,1,0:T(8,128)(2,1)S(1)}, u32[]{:S(2)}, u32[]{:S(2)}) %all-to-all-start) | async-done | bytes 1048608 | tf_op jit(solution)/shard_map/all_to_all | solution.py:247
  113.4 1.3 collective-permute-start.12
  114.7 1.3 collective-permute-start.11
  116.0 1.3 collective-permute-start.10
  117.3 1.3 collective-permute-start.9
  118.6 2.5 %collective-permute-done.12 = bf16[32,4096]{1,0:T(8,128)(2,1)S(1)} collective-permute-done((bf16[32,4096]{1,0:T(8,128)(2,1)S(1)}, bf16[32,4096]{1,0:T(8,128)(2,1)S(1)}, u32[]{:S(2)}, u32[]{:S(2)}) %collective-permute-start.12) | collective-permute-done | bytes 262176 | tf_op jit(solution)/shard_map/ppermute | solution.py:203
  121.1 3.2 %collective-permute-done.11 = bf16[32,4096]{1,0:T(8,128)(2,1)S(1)} collective-permute-done((bf16[32,4096]{1,0:T(8,128)(2,1)S(1)}, bf16[32,4096]{1,0:T(8,128)(2,1)S(1)}, u32[]{:S(2)}, u32[]{:S(2)}) %collective-permute-start.11) | collective-permute-done | bytes 262176 | tf_op jit(solution)/shard_map/ppermute | solution.py:203
  124.3 2.1 %collective-permute-done.10 = bf16[32,4096]{1,0:T(8,128)(2,1)S(1)} collective-permute-done((bf16[32,4096]{1,0:T(8,128)(2,1)S(1)}, bf16[32,4096]{1,0:T(8,128)(2,1)S(1)}, u32[]{:S(2)}, u32[]{:S(2)}) %collective-permute-start.10) | collective-permute-done | bytes 262176 | tf_op jit(solution)/shard_map/ppermute | solution.py:203
  126.5 4.8 %convolution_convert_fusion.mixed_ref = bf16[128,1024]{1,0:T(8,128)(2,1)S(1)} fusion(bf16[32,4096]{1,0:T(8,128)(2,1)S(1)} %collective-permute-done.12, bf16[32,4096]{1,0:T(8,128)(2,1)S(1)} %collective-permute-done.11, bf16[32,4096]{1,0:T(8,128)(2,1)S(1)} %collective-permute-done.10, bf16[32,4096]{1,0:T(8,128)(2,1)S(1)} %collective-permute-done.9, ...), kind=kOutput, calls=%fused_computation | convolution fusion | flops 1078067200 | bytes 9699328 | tf_op jit(solution)/shard_map/dot_general | solution.py:25
  131.2 3.7 %reduce-scatter.2.cloned.1.call-done = bf16[1,128,1280]{2,1,0:T(8,128)(2,1)} async-done(((bf16[4,128,1280]{2,1,0:T(8,128)(2,1)}), bf16[1,128,1280]{2,1,0:T(8,128)(2,1)}) %reduce-scatter.2.cloned.1.call-update) | async-done | bytes 327696 | tf_op jit(solution)/shard_map/reduce_scatter | solution.py:246
  137.0 19.0 %all_to_all.11 = f32[32,1,1280]{2,1,0:T(1,128)S(1)} all-to-all(f32[32,1,1280]{2,1,0:T(1,128)S(1)} %broadcast_in_dim.8), channel_id=1, replica_groups=mesh['pipe'=2,'tensor'=4,'z'=8,'y'=4] {'z','y'}, dimensions={0} | all-to-all | bytes 327680 | tf_op jit(solution)/shard_map/all_to_all | solution.py:265
  (53 shorter events, 13.0 us)
Async XLA Ops:
  6.5 48.2 %all-gather.4.cloned.1.call-start = ((), (), s32[]{:S(2)}) async-start(), calls=%async_computation.3 | async-start | bytes 2949120 | tf_op jit(solution)/shard_map/all_gather | solution.py:214
  9.3 91.6 %all-gather.6.cloned.1.call-start = ((), (), s32[]{:S(2)}) async-start(), calls=%async_computation.5 | async-start | bytes 2949120 | tf_op jit(solution)/shard_map/all_gather | solution.py:221
  9.4 1.2 copy-start.2
  12.1 9.4 %collective-permute-start = (bf16[128,1024]{1,0:T(8,128)(2,1)S(1)}, bf16[128,1024]{1,0:T(8,128)(2,1)S(1)}, u32[]{:S(2)}, u32[]{:S(2)}) collective-permute-start(bf16[128,1024]{1,0:T(8,128)(2,1)S(1)} %get-tuple-element.25), channel_id=1, source_target_pairs={{0,1},{1,2},{2,3},{3,0},{128,129},{129,130},{130,131},{131,128},{4... | collective-permute-start | bytes 786440 | tf_op jit(solution)/shard_map/ppermute | solution.py:199
  13.8 14.5 %collective-permute-start.1 = (bf16[128,1024]{1,0:T(8,128)(2,1)S(1)}, bf16[128,1024]{1,0:T(8,128)(2,1)S(1)}, u32[]{:S(2)}, u32[]{:S(2)}) collective-permute-start(bf16[128,1024]{1,0:T(8,128)(2,1)S(1)} %get-tuple-element.26), channel_id=1, source_target_pairs={{0,2},{1,3},{2,0},{3,1},{128,130},{129,131},{130,128},{131,129},{4... | collective-permute-start | bytes 786440 | tf_op jit(solution)/shard_map/ppermute | solution.py:199
  16.7 11.6 %collective-permute-start.2 = (bf16[128,1024]{1,0:T(8,128)(2,1)S(1)}, bf16[128,1024]{1,0:T(8,128)(2,1)S(1)}, u32[]{:S(2)}, u32[]{:S(2)}) collective-permute-start(bf16[128,1024]{1,0:T(8,128)(2,1)S(1)} %get-tuple-element.27), channel_id=1, source_target_pairs={{0,3},{1,0},{2,1},{3,2},{128,131},{129,128},{130,129},{131,130},{4... | collective-permute-start | bytes 786440 | tf_op jit(solution)/shard_map/ppermute | solution.py:199
  28.3 31.6 %copy-start.10 = (bf16[128,1024]{1,0:T(8,128)(2,1)}, bf16[128,1024]{1,0:T(8,128)(2,1)S(1)}, u32[]{:S(2)}) copy-start(bf16[128,1024]{1,0:T(8,128)(2,1)S(1)} %collective-permute-done.1.refs_2_) | copy-start | bytes 786436
  28.3 31.6 %copy-start.12 = (bf16[128,1024]{1,0:T(8,128)(2,1)}, bf16[128,1024]{1,0:T(8,128)(2,1)S(1)}, u32[]{:S(2)}) copy-start(bf16[128,1024]{1,0:T(8,128)(2,1)S(1)} %collective-permute-done.2.refs_3_) | copy-start | bytes 786436
  54.7 1.7 %copy-start.7 = (bf16[8,1280,128]{2,1,0:T(8,128)(2,1)S(1)}, bf16[8,1280,128]{2,1,0:T(8,128)(2,1)}, u32[]{:S(2)}) copy-start(bf16[8,1280,128]{2,1,0:T(8,128)(2,1)} %all-gather.4.cloned.1.call-done.refs_4_) | copy-start | bytes 7864324
  56.5 8.6 %copy-start.1 = (bf16[128,4096]{1,0:T(8,128)(2,1)S(1)}, bf16[128,4096]{1,0:T(8,128)(2,1)}, u32[]{:S(2)}) copy-start(bf16[128,4096]{1,0:T(8,128)(2,1)} %rows_ref.1) | copy-start | bytes 3145732
  60.0 13.9 %collective-permute-start.3 = (bf16[128,1280]{1,0:T(8,128)(2,1)S(1)}, bf16[128,1280]{1,0:T(8,128)(2,1)S(1)}, u32[]{:S(2)}, u32[]{:S(2)}) collective-permute-start(bf16[128,1280]{1,0:T(8,128)(2,1)S(1)} %get-tuple-element.29), channel_id=1, source_target_pairs={{0,3},{1,0},{2,1},{3,2},{128,131},{129,128},{130,129},{131,130},{4... | collective-permute-start | bytes 983048 | tf_op jit(solution)/shard_map/ppermute | solution.py:199
  62.8 15.0 %collective-permute-start.4 = (bf16[128,1280]{1,0:T(8,128)(2,1)S(1)}, bf16[128,1280]{1,0:T(8,128)(2,1)S(1)}, u32[]{:S(2)}, u32[]{:S(2)}) collective-permute-start(bf16[128,1280]{1,0:T(8,128)(2,1)S(1)} %get-tuple-element.30), channel_id=1, source_target_pairs={{0,1},{1,2},{2,3},{3,0},{128,129},{129,130},{130,131},{131,128},{4... | collective-permute-start | bytes 983048 | tf_op jit(solution)/shard_map/ppermute | solution.py:199
  62.8 15.0 %collective-permute-start.5 = (bf16[128,1280]{1,0:T(8,128)(2,1)S(1)}, bf16[128,1280]{1,0:T(8,128)(2,1)S(1)}, u32[]{:S(2)}, u32[]{:S(2)}) collective-permute-start(bf16[128,1280]{1,0:T(8,128)(2,1)S(1)} %get-tuple-element.31), channel_id=1, source_target_pairs={{0,2},{1,3},{2,0},{3,1},{128,130},{129,131},{130,128},{131,129},{4... | collective-permute-start | bytes 983048 | tf_op jit(solution)/shard_map/ppermute | solution.py:199
  65.1 3.5 %copy-start = (bf16[1,4096,1024]{2,1,0:T(8,128)(2,1)S(1)}, bf16[1,4096,1024]{2,1,0:T(8,128)(2,1)}, u32[]{:S(2)}) copy-start(bf16[1,4096,1024]{2,1,0:T(8,128)(2,1)} %param.13) | copy-start | bytes 25165828
  68.6 23.2 %copy-start.8 = (bf16[8,1280,128]{2,1,0:T(8,128)(2,1)S(1)}, bf16[8,1280,128]{2,1,0:T(8,128)(2,1)}, u32[]{:S(2)}) copy-start(bf16[8,1280,128]{2,1,0:T(8,128)(2,1)} %all-gather.4.cloned.1.call-done.refs_4_) | copy-start | bytes 7864324
  71.2 22.2 %copy-start.14 = (bf16[32,4096]{1,0:T(8,128)(2,1)}, bf16[32,4096]{1,0:T(8,128)(2,1)S(1)}, u32[]{:S(2)}) copy-start(bf16[32,4096]{1,0:T(8,128)(2,1)S(1)} %get-tuple-element.22.cotangent_ref) | copy-start | bytes 786436
  78.8 13.0 %collective-permute-start.6 = (bf16[128,1280]{1,0:T(8,128)(2,1)S(1)}, bf16[128,1280]{1,0:T(8,128)(2,1)S(1)}, u32[]{:S(2)}, u32[]{:S(2)}) collective-permute-start(bf16[128,1280]{1,0:T(8,128)(2,1)S(1)} %shard_map.79.refs_0_.upper_ref), channel_id=1, source_target_pairs={{0,1},{1,2},{2,3},{3,0},{128,129},{129,130},{130,131},{131,128},{4... | collective-permute-start | bytes 983048 | tf_op jit(solution)/shard_map/ppermute | solution.py:199
  78.9 12.9 %collective-permute-start.7 = (bf16[128,1280]{1,0:T(8,128)(2,1)S(1)}, bf16[128,1280]{1,0:T(8,128)(2,1)S(1)}, u32[]{:S(2)}, u32[]{:S(2)}) collective-permute-start(bf16[128,1280]{1,0:T(8,128)(2,1)S(1)} %shard_map.79.refs_0_.upper_ref), channel_id=1, source_target_pairs={{0,2},{1,3},{2,0},{3,1},{128,130},{129,131},{130,128},{131,129},{4... | collective-permute-start | bytes 983048 | tf_op jit(solution)/shard_map/ppermute | solution.py:199
  80.1 11.7 %collective-permute-start.8 = (bf16[128,1280]{1,0:T(8,128)(2,1)S(1)}, bf16[128,1280]{1,0:T(8,128)(2,1)S(1)}, u32[]{:S(2)}, u32[]{:S(2)}) collective-permute-start(bf16[128,1280]{1,0:T(8,128)(2,1)S(1)} %shard_map.79.refs_0_.upper_ref), channel_id=1, source_target_pairs={{0,3},{1,0},{2,1},{3,2},{128,131},{129,128},{130,129},{131,130},{4... | collective-permute-start | bytes 983048 | tf_op jit(solution)/shard_map/ppermute | solution.py:199
  93.4 1.0 copy-start.3
  94.4 17.6 %all-to-all-start = ((bf16[16,32,1024]{2,1,0:T(8,128)(2,1)}), bf16[16,32,1024]{2,1,0:T(8,128)(2,1)S(1)}, u32[]{:S(2)}, u32[]{:S(2)}) async-start(bf16[16,32,1024]{2,1,0:T(8,128)(2,1)} %copy-done.3), calls=%async_computation | async-start | bytes 2097152 | tf_op jit(solution)/shard_map/all_to_all | solution.py:247
  100.8 34.1 %reduce-scatter.2.cloned.1.call-start = ((), (), s32[]{:S(2)}) async-start(), calls=%async_computation.4 | async-start | bytes 1638400 | tf_op jit(solution)/shard_map/reduce_scatter | solution.py:246
  100.9 1.7 %copy-start.9 = (bf16[10240,128]{1,0:T(8,128)(2,1)S(1)}, bf16[10240,128]{1,0:T(8,128)(2,1)}, u32[]{:S(2)}) copy-start(bf16[10240,128]{1,0:T(8,128)(2,1)} %all-gather.6.cloned.1.call-done) | copy-start | bytes 7864324
  102.6 0.9 copy-start.11
  103.6 0.9 copy-start.13
  104.5 7.5 %copy-start.6 = (f32[1,4096]{1,0:T(1,128)S(1)}, f32[1,4096]{1,0:T(1,128)}, u32[]{:S(2)}) copy-start(f32[1,4096]{1,0:T(1,128)} %gain_ref.3) | copy-start | bytes 49156
  112.0 1.0 copy-start.15
  113.4 7.7 %collective-permute-start.12 = (bf16[32,4096]{1,0:T(8,128)(2,1)S(1)}, bf16[32,4096]{1,0:T(8,128)(2,1)S(1)}, u32[]{:S(2)}, u32[]{:S(2)}) collective-permute-start(bf16[32,4096]{1,0:T(8,128)(2,1)S(1)} %shard_map.82), channel_id=1, source_target_pairs={{128,96},{160,0},{192,32},{224,64},{129,97},{161,1},{193,33},{225,... | collective-permute-start | bytes 786440 | tf_op jit(solution)/shard_map/ppermute | solution.py:203
  114.7 9.6 %collective-permute-start.11 = (bf16[32,4096]{1,0:T(8,128)(2,1)S(1)}, bf16[32,4096]{1,0:T(8,128)(2,1)S(1)}, u32[]{:S(2)}, u32[]{:S(2)}) collective-permute-start(bf16[32,4096]{1,0:T(8,128)(2,1)S(1)} %shard_map.82), channel_id=1, source_target_pairs={{128,64},{160,96},{192,0},{224,32},{129,65},{161,97},{193,1},{225,... | collective-permute-start | bytes 786440 | tf_op jit(solution)/shard_map/ppermute | solution.py:203
  116.0 10.4 %collective-permute-start.10 = (bf16[32,4096]{1,0:T(8,128)(2,1)S(1)}, bf16[32,4096]{1,0:T(8,128)(2,1)S(1)}, u32[]{:S(2)}, u32[]{:S(2)}) collective-permute-start(bf16[32,4096]{1,0:T(8,128)(2,1)S(1)} %shard_map.82), channel_id=1, source_target_pairs={{128,32},{160,64},{192,96},{224,0},{129,33},{161,65},{193,97},{225... | collective-permute-start | bytes 786440 | tf_op jit(solution)/shard_map/ppermute | solution.py:203
  117.3 9.1 %collective-permute-start.9 = (bf16[32,4096]{1,0:T(8,128)(2,1)S(1)}, bf16[32,4096]{1,0:T(8,128)(2,1)S(1)}, u32[]{:S(2)}, u32[]{:S(2)}) collective-permute-start(bf16[32,4096]{1,0:T(8,128)(2,1)S(1)} %shard_map.82), channel_id=1, source_target_pairs={{128,0},{160,32},{192,64},{224,96},{129,1},{161,33},{193,65},{225,... | collective-permute-start | bytes 786440 | tf_op jit(solution)/shard_map/ppermute | solution.py:203
  134.9 1.0 copy-start.4
  (1 other events, 0.7 us)
Sparse Core Ops, SparseCore 0:
  9.4 45.2 all-gather.3
  56.5 40.9 all-gather.5
  109.2 25.6 reduce-scatter.1

commit v7 on v6

--- a/solution.py
+++ b/solution.py
@@ -97,11 +97,15 @@
 
 
 def sign_kernel(*refs):
-    out_ref, done_ref = refs[-2:]
-    done_ref[...] = jnp.zeros_like(done_ref)
+    hidden, slab_ref, rows = refs[:NY], refs[NY], refs[NY + 1 : 2 * NY + 1]
+    out_ref, upper_ref = refs[-2:]
     y_index = lax.axis_index("y")
-    for k, product in slab_products(refs[:NY], refs[NY]):
+    upper = None
+    for k, product in slab_products(hidden, slab_ref):
         out_ref[(y_index - k + NY) % NY] = product
+        term = jnp.sum(rows[k][...].astype(F32) * product.astype(F32), axis=0, keepdims=True)
+        upper = term if upper is None else upper + term
+    upper_ref[...] = upper
 
 
 def summed(parts, h):
@@ -123,8 +127,7 @@
 
 
 def back_kernel(*refs):
-    rows, slab_ref, out_ref, done_ref = refs[:NY], refs[NY], refs[-2], refs[-1]
-    done_ref[...] = jnp.zeros_like(done_ref)
+    rows, slab_ref, out_ref = refs[:NY], refs[NY], refs[-1]
     y_index = lax.axis_index("y")
     chunk = out_ref.shape[1]
     for k in range(NY):
@@ -136,8 +139,7 @@
                 out_ref[place, :, z * HD : (z + 2) * HD] = term[c * chunk : (c + 1) * chunk]
 
 
-def norm_back_kernel(inputs_ref, gain_ref, cotangent_ref, terms_ref, *refs):
-    out_ref = refs[-1]
+def norm_back_kernel(inputs_ref, gain_ref, cotangent_ref, terms_ref, out_ref):
     width = out_ref.shape[1]
     values = inputs_ref[...].astype(F32)
     factor = lax.rsqrt(jnp.mean(values * values, axis=-1, keepdims=True) + 1e-05)
@@ -176,6 +178,7 @@
 
 def lower_kernel(count, mixed_ref, upper_ref, projected_ref, *refs):
     parts, out_ref, turned_ref = refs[:NY], refs[-2], refs[-1]
+    projected = [projected_ref.at[k] for k in range(NY)]
     pipe_index = lax.axis_index("pipe")
     x_index = lax.axis_index("tensor")
     chunk = turned_ref.shape[0] // NX
@@ -189,9 +192,9 @@
     for h, column in enumerate(columns):
         at = slice(h * HD, (h + 1) * HD)
         lower = column.astype(BF16).astype(F32)
-        kept = jnp.where(pipe_index == 1, upper_ref[:, at].astype(F32), lower)
-        product = projected_ref[:, at].astype(F32)
-        out_ref[:, at] = jnp.sum(kept * product, axis=0, keepdims=True) * (1.0 / count)
+        product = summed(projected, h).astype(F32)
+        lower = jnp.sum(lower * product, axis=0, keepdims=True)
+        out_ref[:, at] = jnp.where(pipe_index == 1, upper_ref[:, at], lower) * (1.0 / count)
 
 
 def send_y(value, steps, pipes=(0, 1)):
@@ -224,40 +227,51 @@
     grad_mixed, own_cotangent = call(mixed_kernel, (mixed_rows, quarter_rows), (cotangent, weight_out), 10**9, scratch=mixed_total)
     flops = 2 * tokens * rows * width
     packed_rows = jax.ShapeDtypeStruct((tokens, rows), BF16)
-    done = jax.ShapeDtypeStruct((8, HD), F32)
     partial = call(packed_kernel, (packed_rows,) * NY, (*hidden_slab, weight_slab), flops)
     parts = [partial[0]] + [send_y(partial[k], -k) for k in (1, 3, 2)]
+    is_last = lax.axis_index("pipe") == 1
+
     grad_upper = call(upper_kernel, packed_rows, (grad_mixed, *parts), 10**8)
-    near, back_near, far = (send_y(grad_upper, k) for k in (1, 3, 2))
-    slab_rows = [grad_upper, near, far, back_near]
-    back, after_back = call(
-        back_kernel,
-        (jax.ShapeDtypeStruct((NX * NY, chunk, NZ * HD), BF16), done),
-        (*slab_rows, weight_slab),
-        flops,
-    )
-    signed, after_signed = call(
+
+    def last_layer():
+        near, back_near, far = (send_y(grad_upper, k) for k in (1, 3, 2))
+        slab_rows = [grad_upper, near, far, back_near]
+        back = call(
+            back_kernel,
+            jax.ShapeDtypeStruct((NX * NY, chunk, NZ * HD), BF16),
+            (*slab_rows, weight_slab),
+            flops,
+        )
+        terms = lax.all_to_all(back, ("tensor", "y"), 0, 0)
+        backward = call(
+            norm_back_kernel, quarter_rows, (own_inputs, norm_gain, own_cotangent, terms), 10**6
+        )
+        return (backward, *slab_rows)
+
+    def no_last_layer():
+        return (jnp.zeros(quarter_rows.shape, BF16),) + (jnp.zeros(packed_rows.shape, BF16),) * NY
+
+    backward, *slab_rows = lax.cond(is_last, last_layer, no_last_layer)
+    arrived = [send_down(backward, j) for j in range(NX)]
+    by_y = jax.ShapeDtypeStruct((NY, tokens, rows), BF16)
+    signed, upper_total = call(
         sign_kernel,
-        (jax.ShapeDtypeStruct((NY, tokens, rows), BF16), done),
-        (*hidden_slab, sign_slab, after_back),
+        (by_y, jax.ShapeDtypeStruct((1, rows), F32)),
+        (*hidden_slab, sign_slab, *slab_rows, backward),
         flops,
         unread=1,
     )
-    projected = lax.psum_scatter(signed, "y", scatter_dimension=0)
-    terms = lax.all_to_all(back, ("tensor", "y"), 0, 0)
-    backward = call(
-        norm_back_kernel,
-        jax.ShapeDtypeStruct((chunk, width), BF16),
-        (own_inputs, norm_gain, own_cotangent, terms, after_signed),
-        10**11,
-        unread=1,
-    )
-    arrived = [send_down(backward, j) for j in range(NX)]
+    projected = lax.cond(
+        is_last,
+        lambda: jnp.zeros(by_y.shape, BF16),
+        lambda: lax.all_to_all(signed, "y", 0, 0),
+    )
+    arrived = lax.optimization_barrier((*arrived, projected))[:NX]
     grad_mixed_lower = dot_nn(jnp.concatenate(arrived, axis=0), weight_out).astype(BF16)
     partial_sum = call(
         functools.partial(lower_kernel, tokens * NZ * NY),
         jax.ShapeDtypeStruct((1, rows), F32),
-        (grad_mixed_lower, grad_upper, projected, *parts),
+        (grad_mixed_lower, upper_total, projected, *parts),
         10**8,
         scratch=[pltpu.VMEM(mixed_rows.shape, BF16)],
     )

time: 164 us -> 153 us (0.933)
  waiting for transfers between devices: 67.4 us -> 51.8 us
  blocking collectives: 19 us -> 33.4 us
  starting transfers between devices: 26 us -> 16.1 us
  local copies, waits for them, and re-layouts: 14.4 us -> 10.8 us
  Pallas kernels: 15.4 us -> 17.7 us
    all_to_all x0 -> x1, blocking collectives: none -> 16.4 us  [local(): lax.all_to_all(signed, 'y', 0, 0)]
    ppermute x9 -> x6, waiting for transfers between devices: 26.5 us -> 16.7 us  [send_y(): return lax.ppermute(value, ('pipe', 'y'), pairs)]
    all_gather x1, waiting for transfers between devices: 0.02 us -> 8.71 us  [local(): sign_slab = lax.all_gather(later_sign, 'z', axis=0, tiled=False)]
    ppermute x4, waiting for transfers between devices: 7.83 us -> 0.01 us  [send_down(): lax.ppermute(value, ('pipe', 'tensor'), [(NX + i, (i + steps) % NX) for i...]
    unnamed x32 -> x14, local copies, waits for them, and re-layouts: 13.7 us -> 6.41 us
    all_to_all x1 -> x0, starting transfers between devices: 6.41 us -> none  [local(): terms = lax.all_to_all(back, ('tensor', 'y'), 0, 0)]
    another operation x0 -> x5, local copies, waits for them, and re-layouts: none -> 3.75 us
    reduce_scatter x1 -> x0, waiting for transfers between devices: 3.66 us -> none  [local(): projected = lax.psum_scatter(signed, 'y', scatter_dimension=0)]
  transfers between devices with their start and end apart: 17 -> 12, of which waited for: 11 -> 6; matrix products, arithmetic and copies ran while one was open for 3% -> 2% of each run, Pallas kernels for 9% -> 11%
where the time goes in v7:
time: 153 us; the launch traced here: 151 us
  waiting for transfers between devices  51.8 us (34%)
  blocking collectives  33.4 us (22%)
  Pallas kernels  17.7 us (12%)
  starting transfers between devices  16.1 us (11%)
  between operations  13.5 us (9%)
  local copies, waits for them, and re-layouts  10.8 us (7%)
  matrix products  4.81 us (3%)
  other arithmetic  2.88 us (2%)
    all_gather x1, waiting for transfers between devices, local(): weight_slab = lax.all_gather(weight, 'z', axis=0, tiled=False)  26.3 us
    pallas_call x6, Pallas kernels, call(): pl.pallas_call(kernel, out_shape=outs, in_specs=[VMEM] * (len(args) - unr...  17.7 us
    all_to_all x1, blocking collectives, local(): lax.all_to_all(copies, ('z', 'y'), 0, 0)  17 us
    ppermute x6, waiting for transfers between devices, send_y(): return lax.ppermute(value, ('pipe', 'y'), pairs)  16.7 us
    all_to_all x1, blocking collectives, local(): lax.all_to_all(signed, 'y', 0, 0)  16.4 us
    ppermute x6, starting transfers between devices, send_y(): return lax.ppermute(value, ('pipe', 'y'), pairs)  10.9 us
    all_gather x1, waiting for transfers between devices, local(): sign_slab = lax.all_gather(later_sign, 'z', axis=0, tiled=False)  8.71 us
    unnamed x14, local copies, waits for them, and re-layouts  6.41 us
  transfers between devices with their start and end apart: 12, of which 6 were waited for; matrix products, arithmetic and copies ran while one was open for 2% of the time, Pallas kernels for 11%

profile of v7, /device:TPU:2, one launch (start us, length us, event | category | flops | bytes accessed | tf_op | source)
XLA Modules:
  0.0 151.1 jit_solution(8054455624162538642)
XLA Ops:
  7.2 2.0 %add_convert_fusion = bf16[1,1280,128]{2,1,0:T(8,128)(2,1)} fusion(bf16[1,1280,128]{2,1,0:T(8,128)(2,1)} %param.15, bf16[1,1280,128]{2,1,0:T(8,128)(2,1)} %param.14, f32[1280]{0:T(1024)S(1)} %reduce.1), kind=kLoop, calls=%fused_computation.8 | loop fusion | flops 819200 | bytes 988160 | tf_op jit(solution)/shard_map/convert_element_type | solution.py:216
  9.4 1.2 copy-done.3
  10.6 1.7 %shard_map.77 = (bf16[128,1024]{1,0:T(8,128)(2,1)S(1)}, bf16[128,1024]{1,0:T(8,128)(2,1)S(1)}, bf16[128,1024]{1,0:T(8,128)(2,1)S(1)}, bf16[128,1024]{1,0:T(8,128)(2,1)S(1)}, bf16[32,4096]{1,0:T(8,128)(2,1)}) custom-call(bf16[128,4096]{1,0:T(8,128)(2,1)S(1)} %bitcast.8, f32[1,4096]{1,0:T(1,128)} %gain_ref.1), custom_call_target="tpu_custom_call" | custom-call | flops 10000000 | bytes 100000 | tf_op jit(solution)/shard_map/pallas_call | solution.py:37
  12.3 1.6 %collective-permute-start.3 = (bf16[128,1024]{1,0:T(8,128)(2,1)S(1)}, bf16[128,1024]{1,0:T(8,128)(2,1)S(1)}, u32[]{:S(2)}, u32[]{:S(2)}) collective-permute-start(bf16[128,1024]{1,0:T(8,128)(2,1)S(1)} %get-tuple-element.49), channel_id=1, source_target_pairs={{0,1},{1,2},{2,3},{3,0},{128,129},{129,130},{130,131},{131,128},{4... | collective-permute-start | bytes 786440 | tf_op jit(solution)/shard_map/ppermute | solution.py:202
  13.9 2.9 %collective-permute-start.4 = (bf16[128,1024]{1,0:T(8,128)(2,1)S(1)}, bf16[128,1024]{1,0:T(8,128)(2,1)S(1)}, u32[]{:S(2)}, u32[]{:S(2)}) collective-permute-start(bf16[128,1024]{1,0:T(8,128)(2,1)S(1)} %get-tuple-element.50), channel_id=1, source_target_pairs={{0,2},{1,3},{2,0},{3,1},{128,130},{129,131},{130,128},{131,129},{4... | collective-permute-start | bytes 786440 | tf_op jit(solution)/shard_map/ppermute | solution.py:202
  16.8 1.3 collective-permute-start.5
  18.1 3.5 %collective-permute-done.3.refs_1_ = bf16[128,1024]{1,0:T(8,128)(2,1)S(1)} collective-permute-done((bf16[128,1024]{1,0:T(8,128)(2,1)S(1)}, bf16[128,1024]{1,0:T(8,128)(2,1)S(1)}, u32[]{:S(2)}, u32[]{:S(2)}) %collective-permute-start.3) | collective-permute-done | bytes 262176 | tf_op jit(solution)/shard_map/ppermute | solution.py:202
  21.6 6.8 %collective-permute-done.4.refs_2_ = bf16[128,1024]{1,0:T(8,128)(2,1)S(1)} collective-permute-done((bf16[128,1024]{1,0:T(8,128)(2,1)S(1)}, bf16[128,1024]{1,0:T(8,128)(2,1)S(1)}, u32[]{:S(2)}, u32[]{:S(2)}) %collective-permute-start.4) | collective-permute-done | bytes 262176 | tf_op jit(solution)/shard_map/ppermute | solution.py:202
  28.4 26.3 %all-gather.4.cloned.1.call-done.refs_4_ = bf16[8,1280,128]{2,1,0:T(8,128)(2,1)} async-done(((bf16[1,1280,128]{2,1,0:T(8,128)(2,1)}), bf16[8,1280,128]{2,1,0:T(8,128)(2,1)}) %all-gather.4.cloned.1.call-update) | async-done | bytes 2621456 | tf_op jit(solution)/shard_map/all_gather | solution.py:217
  54.7 6.2 %shard_map.78 = (bf16[128,1280]{1,0:T(8,128)(2,1)S(1)}, bf16[128,1280]{1,0:T(8,128)(2,1)}, bf16[128,1280]{1,0:T(8,128)(2,1)}, bf16[128,1280]{1,0:T(8,128)(2,1)}) custom-call(bf16[128,1024]{1,0:T(8,128)(2,1)S(1)} %get-tuple-element.48.refs_0_, bf16[128,1024]{1,0:T(8,128)(2,1)S(1)} %collective-permute-done.3.refs_1_, ...), custom_call_target="tpu_custom_call" | custom-call | flops 1342177280 | bytes 100000 | tf_op jit(solution)/shard_map/pallas_call | solution.py:37
  60.9 2.7 %collective-permute-start.6 = (bf16[128,1280]{1,0:T(8,128)(2,1)}, bf16[128,1280]{1,0:T(8,128)(2,1)S(1)}, u32[]{:S(2)}, u32[]{:S(2)}) collective-permute-start(bf16[128,1280]{1,0:T(8,128)(2,1)} %get-tuple-element.53), channel_id=1, source_target_pairs={{0,3},{1,0},{2,1},{3,2},{128,131},{129,128},{130,129},{131,130},{4... | collective-permute-start | bytes 983048 | tf_op jit(solution)/shard_map/ppermute | solution.py:202
  63.6 2.3 %collective-permute-start.8 = (bf16[128,1280]{1,0:T(8,128)(2,1)}, bf16[128,1280]{1,0:T(8,128)(2,1)S(1)}, u32[]{:S(2)}, u32[]{:S(2)}) collective-permute-start(bf16[128,1280]{1,0:T(8,128)(2,1)} %get-tuple-element.55), channel_id=1, source_target_pairs={{0,2},{1,3},{2,0},{3,1},{128,130},{129,131},{130,128},{131,129},{4... | collective-permute-start | bytes 983048 | tf_op jit(solution)/shard_map/ppermute | solution.py:202
  65.9 3.4 %copy-done = bf16[1,4096,1024]{2,1,0:T(8,128)(2,1)S(1)} copy-done((bf16[1,4096,1024]{2,1,0:T(8,128)(2,1)S(1)}, bf16[1,4096,1024]{2,1,0:T(8,128)(2,1)}, u32[]{:S(2)}) %copy-start) | copy-done | bytes 8388632
  69.4 3.0 %shard_map.76 = (bf16[128,1024]{1,0:T(8,128)(2,1)S(1)}, bf16[32,4096]{1,0:T(8,128)(2,1)}) custom-call(bf16[128,4096]{1,0:T(8,128)(2,1)S(1)} %copy-done.2, bf16[4096,1024]{1,0:T(8,128)(2,1)S(1)} %bitcast.6), custom_call_target="tpu_custom_call" | custom-call | flops 1000000000 | bytes 100000 | tf_op jit(solution)/shard_map/pallas_call | solution.py:37
  72.4 2.6 %collective-permute-done.6.refs_1_ = bf16[128,1280]{1,0:T(8,128)(2,1)S(1)} collective-permute-done((bf16[128,1280]{1,0:T(8,128)(2,1)}, bf16[128,1280]{1,0:T(8,128)(2,1)S(1)}, u32[]{:S(2)}, u32[]{:S(2)}) %collective-permute-start.6) | collective-permute-done | bytes 327712 | tf_op jit(solution)/shard_map/ppermute | solution.py:202
  75.0 3.8 %collective-permute-done.7.refs_2_ = bf16[128,1280]{1,0:T(8,128)(2,1)S(1)} collective-permute-done((bf16[128,1280]{1,0:T(8,128)(2,1)}, bf16[128,1280]{1,0:T(8,128)(2,1)S(1)}, u32[]{:S(2)}, u32[]{:S(2)}) %collective-permute-start.7) | collective-permute-done | bytes 327712 | tf_op jit(solution)/shard_map/ppermute | solution.py:202
  78.8 1.0 shard_map.79
  79.8 3.8 %conditional.2 = (bf16[32,4096]{1,0:T(8,128)(2,1)}, bf16[128,1280]{1,0:T(8,128)(2,1)}, bf16[128,1280]{1,0:T(8,128)(2,1)}, bf16[128,1280]{1,0:T(8,128)(2,1)}, bf16[128,1280]{1,0:T(8,128)(2,1)}) conditional(s32[]{:T(128)} %convert_element_type.19, () %tuple.21, (bf16[128,1280]{1,0:T(8,128)(2,1)S(1)}, bf16[8,1280,128]{2,1,0:T(8,128)(2,1)S(1)}, ...), branch_computations={%region_0.0_spmd, %region_1.0_spmd} | conditional | flops 1343177216 | bytes 9244188 | solution.py:254
  80.6 0.8 broadcast.15.clone
  82.1 0.8 broadcast.15.clone.2
  83.6 1.3 collective-permute-start.10
  84.9 1.3 collective-permute-start.11
  86.2 1.3 collective-permute-start.12
  87.5 1.3 collective-permute-start.9
  88.8 8.7 %all-gather.6.cloned.1.call-done = bf16[10240,128]{1,0:T(8,128)(2,1)} async-done(((bf16[1280,128]{1,0:T(8,128)(2,1)}), bf16[10240,128]{1,0:T(8,128)(2,1)}) %all-gather.6.cloned.1.call-update) | async-done | bytes 2621456 | tf_op jit(solution)/shard_map/all_gather | solution.py:224
  97.5 1.7 %copy-done.1 = bf16[10240,128]{1,0:T(8,128)(2,1)S(1)} copy-done((bf16[10240,128]{1,0:T(8,128)(2,1)S(1)}, bf16[10240,128]{1,0:T(8,128)(2,1)}, u32[]{:S(2)}) %copy-start.1) | copy-done | bytes 2621464
  99.2 4.8 %shard_map.80 = (bf16[4,128,1280]{2,1,0:T(8,128)(2,1)S(1)}, f32[1,1280]{1,0:T(1,128)S(1)}) custom-call(bf16[128,1024]{1,0:T(8,128)(2,1)S(1)} %get-tuple-element.48.refs_0_, bf16[128,1024]{1,0:T(8,128)(2,1)S(1)} %collective-permute-done.3.refs_1_, bf16[128,1024]{1,0:T(8,128)(2,1)S(1)} %collective-permute-done.4.refs_2_, ...), custom_call_target="tpu_custom_call" | custom-call | flops 1342177280 | bytes 100000 | tf_op jit(solution)/shard_map/pallas_call | solution.py:37
  104.1 16.4 %conditional.3 = (bf16[4,128,1280]{2,1,0:T(8,128)(2,1)}) conditional(s32[]{:T(128)} %convert_element_type.19, bf16[4,128,1280]{2,1,0:T(8,128)(2,1)S(1)} %get-tuple-element.64, () %tuple.24), branch_computations={%region_2.0_spmd, %region_3.0_spmd} | conditional | bytes 2621448 | solution.py:264
  104.1 16.4 %all_to_all.14 = bf16[4,128,1280]{2,1,0:T(8,128)(2,1)} all-to-all(bf16[4,128,1280]{2,1,0:T(8,128)(2,1)S(1)} %param.2), channel_id=1, replica_groups=mesh['pipe'=2,'tensor'=4,'z'=8,'y'=4] {'y'}, dimensions={0} | all-to-all | bytes 2621440 | tf_op jit(solution)/shard_map/cond/branch_0_fun/all_to_all | solution.py:267
  120.6 4.8 %convolution_convert_fusion.mixed_ref = bf16[128,1024]{1,0:T(8,128)(2,1)S(1)} fusion(bf16[32,4096]{1,0:T(8,128)(2,1)S(1)} %collective-permute-done.12, bf16[32,4096]{1,0:T(8,128)(2,1)S(1)} %collective-permute-done.11, bf16[32,4096]{1,0:T(8,128)(2,1)S(1)} %collective-permute-done.10, bf16[32,4096]{1,0:T(8,128)(2,1)S(1)} %collective-permute-done.9, ...), kind=kOutput, calls=%fused_computation | convolution fusion | flops 1078067200 | bytes 9699328 | tf_op jit(solution)/shard_map/dot_general | solution.py:25
  125.4 1.0 shard_map.81
  126.5 17.0 %all_to_all.15 = f32[32,1,1280]{2,1,0:T(1,128)S(1)} all-to-all(f32[32,1,1280]{2,1,0:T(1,128)S(1)} %broadcast_in_dim.8), channel_id=1, replica_groups=mesh['pipe'=2,'tensor'=4,'z'=8,'y'=4] {'z','y'}, dimensions={0} | all-to-all | bytes 327680 | tf_op jit(solution)/shard_map/all_to_all | solution.py:279
  (30 shorter events, 3.9 us)
Async XLA Ops:
  6.5 48.2 %all-gather.4.cloned.1.call-start = ((), (), s32[]{:S(2)}) async-start(), calls=%async_computation.3 | async-start | bytes 2949120 | tf_op jit(solution)/shard_map/all_gather | solution.py:217
  9.3 88.2 %all-gather.6.cloned.1.call-start = ((), (), s32[]{:S(2)}) async-start(), calls=%async_computation.4 | async-start | bytes 2949120 | tf_op jit(solution)/shard_map/all_gather | solution.py:224
  9.4 1.2 copy-start.3
  12.3 9.3 %collective-permute-start.3 = (bf16[128,1024]{1,0:T(8,128)(2,1)S(1)}, bf16[128,1024]{1,0:T(8,128)(2,1)S(1)}, u32[]{:S(2)}, u32[]{:S(2)}) collective-permute-start(bf16[128,1024]{1,0:T(8,128)(2,1)S(1)} %get-tuple-element.49), channel_id=1, source_target_pairs={{0,1},{1,2},{2,3},{3,0},{128,129},{129,130},{130,131},{131,128},{4... | collective-permute-start | bytes 786440 | tf_op jit(solution)/shard_map/ppermute | solution.py:202
  13.9 14.5 %collective-permute-start.4 = (bf16[128,1024]{1,0:T(8,128)(2,1)S(1)}, bf16[128,1024]{1,0:T(8,128)(2,1)S(1)}, u32[]{:S(2)}, u32[]{:S(2)}) collective-permute-start(bf16[128,1024]{1,0:T(8,128)(2,1)S(1)} %get-tuple-element.50), channel_id=1, source_target_pairs={{0,2},{1,3},{2,0},{3,1},{128,130},{129,131},{130,128},{131,129},{4... | collective-permute-start | bytes 786440 | tf_op jit(solution)/shard_map/ppermute | solution.py:202
  16.8 11.6 %collective-permute-start.5 = (bf16[128,1024]{1,0:T(8,128)(2,1)S(1)}, bf16[128,1024]{1,0:T(8,128)(2,1)S(1)}, u32[]{:S(2)}, u32[]{:S(2)}) collective-permute-start(bf16[128,1024]{1,0:T(8,128)(2,1)S(1)} %get-tuple-element.51), channel_id=1, source_target_pairs={{0,3},{1,0},{2,1},{3,2},{128,131},{129,128},{130,129},{131,130},{4... | collective-permute-start | bytes 786440 | tf_op jit(solution)/shard_map/ppermute | solution.py:202
  54.7 11.2 %copy-start.2 = (bf16[128,4096]{1,0:T(8,128)(2,1)S(1)}, bf16[128,4096]{1,0:T(8,128)(2,1)}, u32[]{:S(2)}) copy-start(bf16[128,4096]{1,0:T(8,128)(2,1)} %rows_ref.1) | copy-start | bytes 3145732
  60.9 14.2 %collective-permute-start.6 = (bf16[128,1280]{1,0:T(8,128)(2,1)}, bf16[128,1280]{1,0:T(8,128)(2,1)S(1)}, u32[]{:S(2)}, u32[]{:S(2)}) collective-permute-start(bf16[128,1280]{1,0:T(8,128)(2,1)} %get-tuple-element.53), channel_id=1, source_target_pairs={{0,3},{1,0},{2,1},{3,2},{128,131},{129,128},{130,129},{131,130},{4... | collective-permute-start | bytes 983048 | tf_op jit(solution)/shard_map/ppermute | solution.py:202
  63.6 15.2 %collective-permute-start.7 = (bf16[128,1280]{1,0:T(8,128)(2,1)}, bf16[128,1280]{1,0:T(8,128)(2,1)S(1)}, u32[]{:S(2)}, u32[]{:S(2)}) collective-permute-start(bf16[128,1280]{1,0:T(8,128)(2,1)} %get-tuple-element.54), channel_id=1, source_target_pairs={{0,1},{1,2},{2,3},{3,0},{128,129},{129,130},{130,131},{131,128},{4... | collective-permute-start | bytes 983048 | tf_op jit(solution)/shard_map/ppermute | solution.py:202
  63.6 15.2 %collective-permute-start.8 = (bf16[128,1280]{1,0:T(8,128)(2,1)}, bf16[128,1280]{1,0:T(8,128)(2,1)S(1)}, u32[]{:S(2)}, u32[]{:S(2)}) collective-permute-start(bf16[128,1280]{1,0:T(8,128)(2,1)} %get-tuple-element.55), channel_id=1, source_target_pairs={{0,2},{1,3},{2,0},{3,1},{128,130},{129,131},{130,128},{131,129},{4... | collective-permute-start | bytes 983048 | tf_op jit(solution)/shard_map/ppermute | solution.py:202
  65.9 3.4 %copy-start = (bf16[1,4096,1024]{2,1,0:T(8,128)(2,1)S(1)}, bf16[1,4096,1024]{2,1,0:T(8,128)(2,1)}, u32[]{:S(2)}) copy-start(bf16[1,4096,1024]{2,1,0:T(8,128)(2,1)} %param.17) | copy-start | bytes 25165828
  69.4 10.4 %copy-start.6 = (bf16[8,1280,128]{2,1,0:T(8,128)(2,1)S(1)}, bf16[8,1280,128]{2,1,0:T(8,128)(2,1)}, u32[]{:S(2)}) copy-start(bf16[8,1280,128]{2,1,0:T(8,128)(2,1)} %all-gather.4.cloned.1.call-done.refs_4_) | copy-start | bytes 7864324
  69.4 10.4 %copy-start.7 = (f32[1,4096]{1,0:T(1,128)S(1)}, f32[1,4096]{1,0:T(1,128)}, u32[]{:S(2)}) copy-start(f32[1,4096]{1,0:T(1,128)} %gain_ref.1) | copy-start | bytes 49156
  83.6 36.9 %collective-permute-start.10 = (bf16[32,4096]{1,0:T(8,128)(2,1)}, bf16[32,4096]{1,0:T(8,128)(2,1)S(1)}, u32[]{:S(2)}, u32[]{:S(2)}) collective-permute-start(bf16[32,4096]{1,0:T(8,128)(2,1)} %get-tuple-element.58.refs_9_), channel_id=1, source_target_pairs={{128,32},{160,64},{192,96},{224,0},{129,33},{161,65},{193,97},{225... | collective-permute-start | bytes 786440 | tf_op jit(solution)/shard_map/ppermute | solution.py:206
  84.9 35.6 %collective-permute-start.11 = (bf16[32,4096]{1,0:T(8,128)(2,1)}, bf16[32,4096]{1,0:T(8,128)(2,1)S(1)}, u32[]{:S(2)}, u32[]{:S(2)}) collective-permute-start(bf16[32,4096]{1,0:T(8,128)(2,1)} %get-tuple-element.58.refs_9_), channel_id=1, source_target_pairs={{128,64},{160,96},{192,0},{224,32},{129,65},{161,97},{193,1},{225,... | collective-permute-start | bytes 786440 | tf_op jit(solution)/shard_map/ppermute | solution.py:206
  86.2 34.3 %collective-permute-start.12 = (bf16[32,4096]{1,0:T(8,128)(2,1)}, bf16[32,4096]{1,0:T(8,128)(2,1)S(1)}, u32[]{:S(2)}, u32[]{:S(2)}) collective-permute-start(bf16[32,4096]{1,0:T(8,128)(2,1)} %get-tuple-element.58.refs_9_), channel_id=1, source_target_pairs={{128,96},{160,0},{192,32},{224,64},{129,97},{161,1},{193,33},{225,... | collective-permute-start | bytes 786440 | tf_op jit(solution)/shard_map/ppermute | solution.py:206
  87.5 33.0 %collective-permute-start.9 = (bf16[32,4096]{1,0:T(8,128)(2,1)}, bf16[32,4096]{1,0:T(8,128)(2,1)S(1)}, u32[]{:S(2)}, u32[]{:S(2)}) collective-permute-start(bf16[32,4096]{1,0:T(8,128)(2,1)} %get-tuple-element.58.refs_9_), channel_id=1, source_target_pairs={{128,0},{160,32},{192,64},{224,96},{129,1},{161,33},{193,65},{225,... | collective-permute-start | bytes 786440 | tf_op jit(solution)/shard_map/ppermute | solution.py:206
  97.5 1.7 %copy-start.1 = (bf16[10240,128]{1,0:T(8,128)(2,1)S(1)}, bf16[10240,128]{1,0:T(8,128)(2,1)}, u32[]{:S(2)}) copy-start(bf16[10240,128]{1,0:T(8,128)(2,1)} %all-gather.6.cloned.1.call-done) | copy-start | bytes 7864324
  120.5 4.9 %copy-start.4 = (bf16[4,128,1280]{2,1,0:T(8,128)(2,1)S(1)}, bf16[4,128,1280]{2,1,0:T(8,128)(2,1)}, u32[]{:S(2)}) copy-start(bf16[4,128,1280]{2,1,0:T(8,128)(2,1)} %get-tuple-element.80.projected_ref) | copy-start | bytes 3932164
Sparse Core Ops, SparseCore 0:
  9.4 45.2 all-gather.3
  56.5 40.9 all-gather.5

commit v8 on v7

--- a/solution.py
+++ b/solution.py
@@ -267,7 +267,11 @@
         lambda: lax.all_to_all(signed, "y", 0, 0),
     )
     arrived = lax.optimization_barrier((*arrived, projected))[:NX]
-    grad_mixed_lower = dot_nn(jnp.concatenate(arrived, axis=0), weight_out).astype(BF16)
+    grad_mixed_lower = lax.cond(
+        is_last,
+        lambda: jnp.zeros(mixed_rows.shape, BF16),
+        lambda: dot_nn(jnp.concatenate(arrived, axis=0), weight_out).astype(BF16),
+    )
     partial_sum = call(
         functools.partial(lower_kernel, tokens * NZ * NY),
         jax.ShapeDtypeStruct((1, rows), F32),

time: 153 us -> 152 us (level)
  Pallas kernels: 17.7 us -> 22.6 us
  local copies, waits for them, and re-layouts: 10.8 us -> 7.41 us
    pallas_call x6, Pallas kernels: 17.7 us -> 22.6 us  [call(): pl.pallas_call(kernel, out_shape=outs, in_specs=[VMEM] * (len(args) - unr...]
    unnamed x14 -> x10, local copies, waits for them, and re-layouts: 6.41 us -> 2.97 us
  transfers between devices with their start and end apart: 12 -> 12, of which waited for: 6 -> 6; matrix products, arithmetic and copies ran while one was open for 2% -> 2% of each run, Pallas kernels for 11% -> 13%
where the time goes in v8:
time: 152 us; the launch traced here: 151 us
  waiting for transfers between devices  51.7 us (34%)
  blocking collectives  32.3 us (21%)
  Pallas kernels  22.6 us (15%)
  starting transfers between devices  16.1 us (11%)
  between operations  13.5 us (9%)
  local copies, waits for them, and re-layouts  7.41 us (5%)
  matrix products  4.71 us (3%)
  other arithmetic  2.88 us (2%)
    all_gather x1, waiting for transfers between devices, local(): weight_slab = lax.all_gather(weight, 'z', axis=0, tiled=False)  26.3 us
    pallas_call x6, Pallas kernels, call(): pl.pallas_call(kernel, out_shape=outs, in_specs=[VMEM] * (len(args) - unr...  22.6 us
    ppermute x6, waiting for transfers between devices, send_y(): return lax.ppermute(value, ('pipe', 'y'), pairs)  16.6 us
    all_to_all x1, blocking collectives, local(): lax.all_to_all(signed, 'y', 0, 0)  16.4 us
    all_to_all x1, blocking collectives, local(): lax.all_to_all(copies, ('z', 'y'), 0, 0)  15.9 us
    ppermute x6, starting transfers between devices, send_y(): return lax.ppermute(value, ('pipe', 'y'), pairs)  10.9 us
    all_gather x1, waiting for transfers between devices, local(): sign_slab = lax.all_gather(later_sign, 'z', axis=0, tiled=False)  8.71 us
    ppermute x4, starting transfers between devices, send_down(): lax.ppermute(value, ('pipe', 'tensor'), [(NX + i, (i + steps) % NX) for i...  5.16 us
  transfers between devices with their start and end apart: 12, of which 6 were waited for; matrix products, arithmetic and copies ran while one was open for 2% of the time, Pallas kernels for 13%

profile of v8, /device:TPU:2, one launch (start us, length us, event | category | flops | bytes accessed | tf_op | source)
XLA Modules:
  0.0 151.2 jit_solution(14312687439509380513)
XLA Ops:
  7.2 2.0 %add_convert_fusion = bf16[1,1280,128]{2,1,0:T(8,128)(2,1)} fusion(bf16[1,1280,128]{2,1,0:T(8,128)(2,1)} %param.17, bf16[1,1280,128]{2,1,0:T(8,128)(2,1)} %param.16, f32[1280]{0:T(1024)S(1)} %reduce.1), kind=kLoop, calls=%fused_computation.9 | loop fusion | flops 819200 | bytes 988160 | tf_op jit(solution)/shard_map/convert_element_type | solution.py:216
  9.4 1.2 copy-done.2
  10.6 1.7 %shard_map.77 = (bf16[128,1024]{1,0:T(8,128)(2,1)S(1)}, bf16[128,1024]{1,0:T(8,128)(2,1)S(1)}, bf16[128,1024]{1,0:T(8,128)(2,1)S(1)}, bf16[128,1024]{1,0:T(8,128)(2,1)S(1)}, bf16[32,4096]{1,0:T(8,128)(2,1)}) custom-call(bf16[128,4096]{1,0:T(8,128)(2,1)S(1)} %bitcast.6, f32[1,4096]{1,0:T(1,128)} %gain_ref.1), custom_call_target="tpu_custom_call" | custom-call | flops 10000000 | bytes 100000 | tf_op jit(solution)/shard_map/pallas_call | solution.py:37
  12.3 1.6 %collective-permute-start.3 = (bf16[128,1024]{1,0:T(8,128)(2,1)S(1)}, bf16[128,1024]{1,0:T(8,128)(2,1)S(1)}, u32[]{:S(2)}, u32[]{:S(2)}) collective-permute-start(bf16[128,1024]{1,0:T(8,128)(2,1)S(1)} %get-tuple-element.67), channel_id=1, source_target_pairs={{0,1},{1,2},{2,3},{3,0},{128,129},{129,130},{130,131},{131,128},{4... | collective-permute-start | bytes 786440 | tf_op jit(solution)/shard_map/ppermute | solution.py:202
  13.9 2.9 %collective-permute-start.4 = (bf16[128,1024]{1,0:T(8,128)(2,1)S(1)}, bf16[128,1024]{1,0:T(8,128)(2,1)S(1)}, u32[]{:S(2)}, u32[]{:S(2)}) collective-permute-start(bf16[128,1024]{1,0:T(8,128)(2,1)S(1)} %get-tuple-element.68), channel_id=1, source_target_pairs={{0,2},{1,3},{2,0},{3,1},{128,130},{129,131},{130,128},{131,129},{4... | collective-permute-start | bytes 786440 | tf_op jit(solution)/shard_map/ppermute | solution.py:202
  16.8 1.3 collective-permute-start.5
  18.1 3.5 %collective-permute-done.3.refs_1_ = bf16[128,1024]{1,0:T(8,128)(2,1)S(1)} collective-permute-done((bf16[128,1024]{1,0:T(8,128)(2,1)S(1)}, bf16[128,1024]{1,0:T(8,128)(2,1)S(1)}, u32[]{:S(2)}, u32[]{:S(2)}) %collective-permute-start.3) | collective-permute-done | bytes 262176 | tf_op jit(solution)/shard_map/ppermute | solution.py:202
  21.6 6.8 %collective-permute-done.4.refs_2_ = bf16[128,1024]{1,0:T(8,128)(2,1)S(1)} collective-permute-done((bf16[128,1024]{1,0:T(8,128)(2,1)S(1)}, bf16[128,1024]{1,0:T(8,128)(2,1)S(1)}, u32[]{:S(2)}, u32[]{:S(2)}) %collective-permute-start.4) | collective-permute-done | bytes 262176 | tf_op jit(solution)/shard_map/ppermute | solution.py:202
  28.4 26.3 %all-gather.4.cloned.1.call-done.refs_4_ = bf16[8,1280,128]{2,1,0:T(8,128)(2,1)} async-done(((bf16[1,1280,128]{2,1,0:T(8,128)(2,1)}), bf16[8,1280,128]{2,1,0:T(8,128)(2,1)}) %all-gather.4.cloned.1.call-update) | async-done | bytes 2621456 | tf_op jit(solution)/shard_map/all_gather | solution.py:217
  54.7 6.2 %shard_map.78 = (bf16[128,1280]{1,0:T(8,128)(2,1)S(1)}, bf16[128,1280]{1,0:T(8,128)(2,1)}, bf16[128,1280]{1,0:T(8,128)(2,1)}, bf16[128,1280]{1,0:T(8,128)(2,1)}) custom-call(bf16[128,1024]{1,0:T(8,128)(2,1)S(1)} %get-tuple-element.66.refs_0_, bf16[128,1024]{1,0:T(8,128)(2,1)S(1)} %collective-permute-done.3.refs_1_, ...), custom_call_target="tpu_custom_call" | custom-call | flops 1342177280 | bytes 100000 | tf_op jit(solution)/shard_map/pallas_call | solution.py:37
  60.9 2.7 %collective-permute-start.6 = (bf16[128,1280]{1,0:T(8,128)(2,1)}, bf16[128,1280]{1,0:T(8,128)(2,1)S(1)}, u32[]{:S(2)}, u32[]{:S(2)}) collective-permute-start(bf16[128,1280]{1,0:T(8,128)(2,1)} %get-tuple-element.71), channel_id=1, source_target_pairs={{0,3},{1,0},{2,1},{3,2},{128,131},{129,128},{130,129},{131,130},{4... | collective-permute-start | bytes 983048 | tf_op jit(solution)/shard_map/ppermute | solution.py:202
  63.6 2.3 %collective-permute-start.8 = (bf16[128,1280]{1,0:T(8,128)(2,1)}, bf16[128,1280]{1,0:T(8,128)(2,1)S(1)}, u32[]{:S(2)}, u32[]{:S(2)}) collective-permute-start(bf16[128,1280]{1,0:T(8,128)(2,1)} %get-tuple-element.73), channel_id=1, source_target_pairs={{0,2},{1,3},{2,0},{3,1},{128,130},{129,131},{130,128},{131,129},{4... | collective-permute-start | bytes 983048 | tf_op jit(solution)/shard_map/ppermute | solution.py:202
  65.9 6.5 %shard_map.76 = (bf16[128,1024]{1,0:T(8,128)(2,1)S(1)}, bf16[32,4096]{1,0:T(8,128)(2,1)}) custom-call(bf16[128,4096]{1,0:T(8,128)(2,1)S(1)} %copy-done.1, bf16[4096,1024]{1,0:T(8,128)(2,1)} %bitcast.7), custom_call_target="tpu_custom_call" | custom-call | flops 1000000000 | bytes 100000 | tf_op jit(solution)/shard_map/pallas_call | solution.py:37
  72.5 2.5 %collective-permute-done.6.refs_1_ = bf16[128,1280]{1,0:T(8,128)(2,1)S(1)} collective-permute-done((bf16[128,1280]{1,0:T(8,128)(2,1)}, bf16[128,1280]{1,0:T(8,128)(2,1)S(1)}, u32[]{:S(2)}, u32[]{:S(2)}) %collective-permute-start.6) | collective-permute-done | bytes 327712 | tf_op jit(solution)/shard_map/ppermute | solution.py:202
  75.0 3.8 %collective-permute-done.7.refs_2_ = bf16[128,1280]{1,0:T(8,128)(2,1)S(1)} collective-permute-done((bf16[128,1280]{1,0:T(8,128)(2,1)}, bf16[128,1280]{1,0:T(8,128)(2,1)S(1)}, u32[]{:S(2)}, u32[]{:S(2)}) %collective-permute-start.7) | collective-permute-done | bytes 327712 | tf_op jit(solution)/shard_map/ppermute | solution.py:202
  78.8 1.0 shard_map.79
  79.8 3.8 %conditional.3 = (bf16[32,4096]{1,0:T(8,128)(2,1)}, bf16[128,1280]{1,0:T(8,128)(2,1)}, bf16[128,1280]{1,0:T(8,128)(2,1)}, bf16[128,1280]{1,0:T(8,128)(2,1)}, bf16[128,1280]{1,0:T(8,128)(2,1)}) conditional(s32[]{:T(128)} %convert_element_type.20, () %tuple.27, (bf16[128,1280]{1,0:T(8,128)(2,1)S(1)}, bf16[8,1280,128]{2,1,0:T(8,128)(2,1)S(1)}, ...), branch_computations={%region_0.0_spmd, %region_1.0_spmd} | conditional | flops 1343177216 | bytes 9244188 | solution.py:254
  80.6 0.8 broadcast.17.clone
  82.1 0.8 broadcast.17.clone.2
  83.6 1.3 collective-permute-start.10
  84.9 1.3 collective-permute-start.11
  86.2 1.3 collective-permute-start.12
  87.5 1.3 collective-permute-start.9
  88.8 8.7 %all-gather.6.cloned.1.call-done = bf16[10240,128]{1,0:T(8,128)(2,1)} async-done(((bf16[1280,128]{1,0:T(8,128)(2,1)}), bf16[10240,128]{1,0:T(8,128)(2,1)}) %all-gather.6.cloned.1.call-update) | async-done | bytes 2621456 | tf_op jit(solution)/shard_map/all_gather | solution.py:224
  97.5 1.7 %copy-done = bf16[10240,128]{1,0:T(8,128)(2,1)S(1)} copy-done((bf16[10240,128]{1,0:T(8,128)(2,1)S(1)}, bf16[10240,128]{1,0:T(8,128)(2,1)}, u32[]{:S(2)}) %copy-start) | copy-done | bytes 2621464
  99.2 4.8 %shard_map.80 = (bf16[4,128,1280]{2,1,0:T(8,128)(2,1)S(1)}, f32[1,1280]{1,0:T(1,128)S(1)}) custom-call(bf16[128,1024]{1,0:T(8,128)(2,1)S(1)} %get-tuple-element.66.refs_0_, bf16[128,1024]{1,0:T(8,128)(2,1)S(1)} %collective-permute-done.3.refs_1_, bf16[128,1024]{1,0:T(8,128)(2,1)S(1)} %collective-permute-done.4.refs_2_, ...), custom_call_target="tpu_custom_call" | custom-call | flops 1342177280 | bytes 100000 | tf_op jit(solution)/shard_map/pallas_call | solution.py:37
  104.1 16.4 %conditional.4 = (bf16[4,128,1280]{2,1,0:T(8,128)(2,1)}) conditional(s32[]{:T(128)} %convert_element_type.20, bf16[4,128,1280]{2,1,0:T(8,128)(2,1)S(1)} %get-tuple-element.82, () %tuple.30), branch_computations={%region_2.0_spmd, %region_3.0_spmd} | conditional | bytes 2621448 | solution.py:264
  104.1 16.4 %all_to_all.14 = bf16[4,128,1280]{2,1,0:T(8,128)(2,1)} all-to-all(bf16[4,128,1280]{2,1,0:T(8,128)(2,1)S(1)} %param.2), channel_id=1, replica_groups=mesh['pipe'=2,'tensor'=4,'z'=8,'y'=4] {'y'}, dimensions={0} | all-to-all | bytes 2621440 | tf_op jit(solution)/shard_map/cond/branch_0_fun/all_to_all | solution.py:267
  120.5 4.7 %conditional.5 = (bf16[128,1024]{1,0:T(8,128)(2,1)S(1)}) conditional(s32[]{:T(128)} %convert_element_type.20, (bf16[32,4096]{1,0:T(8,128)(2,1)S(1)}, bf16[32,4096]{1,0:T(8,128)(2,1)S(1)}, bf16[32,4096]{1,0:T(8,128)(2,1)S(1)}, bf16[32,4096]{1,0:T(8,128)(2,1)S(1)}, bf16[4096,1024]{1,0:T(8,128)(2,1)}) %tuple.44, () %tuple.33), branch_computations={%region_4.0_spmd, %region_5.0_spmd} | conditional | flops 1078067200 | bytes 9699336 | solution.py:270
  120.5 4.7 %convolution_convert_fusion = bf16[128,1024]{1,0:T(8,128)(2,1)S(1)} fusion(bf16[4096,1024]{1,0:T(8,128)(2,1)} %get-tuple-element.41, bf16[32,4096]{1,0:T(8,128)(2,1)S(1)} %get-tuple-element.40, bf16[32,4096]{1,0:T(8,128)(2,1)S(1)} %get-tuple-element.39, bf16[32,4096]{1,0:T(8,128)(2,1)S(1)} %get-tuple-element.38, bf16[32,4096]{1,0:T(8,128)(2,1)S(1)} %get-tuple-element.37), kind=kOutput, calls=%fused_computation | convolution fusion | flops 1078067200 | bytes 9699328 | tf_op jit(solution)/shard_map/cond/branch_0_fun/dot_general | solution.py:25
  125.3 2.3 %shard_map.81 = f32[1,1280]{1,0:T(1,128)S(1)} custom-call(bf16[128,1024]{1,0:T(8,128)(2,1)S(1)} %get-tuple-element.99.mixed_ref, f32[1,1280]{1,0:T(1,128)S(1)} %get-tuple-element.87.upper_ref, bf16[4,128,1280]{2,1,0:T(8,128)(2,1)} %get-tuple-element.98.projected_ref, bf16[128,1280]{1,0:T(8,128)(2,1)S(1)} %get-tuple-element.70.refs_0_, ...), custom_call_target="tpu_custom_call" | custom-call | flops 100000000 | bytes 100000 | tf_op jit(solution)/shard_map/pallas_call | solution.py:37
  127.7 15.9 %all_to_all.15 = f32[32,1,1280]{2,1,0:T(1,128)S(1)} all-to-all(f32[32,1,1280]{2,1,0:T(1,128)S(1)} %broadcast_in_dim.8), channel_id=1, replica_groups=mesh['pipe'=2,'tensor'=4,'z'=8,'y'=4] {'z','y'}, dimensions={0} | all-to-all | bytes 327680 | tf_op jit(solution)/shard_map/all_to_all | solution.py:283
  (27 shorter events, 3.9 us)
Async XLA Ops:
  6.5 48.2 %all-gather.4.cloned.1.call-start = ((), (), s32[]{:S(2)}) async-start(), calls=%async_computation.3 | async-start | bytes 2949120 | tf_op jit(solution)/shard_map/all_gather | solution.py:217
  9.3 88.2 %all-gather.6.cloned.1.call-start = ((), (), s32[]{:S(2)}) async-start(), calls=%async_computation.4 | async-start | bytes 2949120 | tf_op jit(solution)/shard_map/all_gather | solution.py:224
  9.4 1.2 copy-start.2
  12.3 9.3 %collective-permute-start.3 = (bf16[128,1024]{1,0:T(8,128)(2,1)S(1)}, bf16[128,1024]{1,0:T(8,128)(2,1)S(1)}, u32[]{:S(2)}, u32[]{:S(2)}) collective-permute-start(bf16[128,1024]{1,0:T(8,128)(2,1)S(1)} %get-tuple-element.67), channel_id=1, source_target_pairs={{0,1},{1,2},{2,3},{3,0},{128,129},{129,130},{130,131},{131,128},{4... | collective-permute-start | bytes 786440 | tf_op jit(solution)/shard_map/ppermute | solution.py:202
  13.9 14.5 %collective-permute-start.4 = (bf16[128,1024]{1,0:T(8,128)(2,1)S(1)}, bf16[128,1024]{1,0:T(8,128)(2,1)S(1)}, u32[]{:S(2)}, u32[]{:S(2)}) collective-permute-start(bf16[128,1024]{1,0:T(8,128)(2,1)S(1)} %get-tuple-element.68), channel_id=1, source_target_pairs={{0,2},{1,3},{2,0},{3,1},{128,130},{129,131},{130,128},{131,129},{4... | collective-permute-start | bytes 786440 | tf_op jit(solution)/shard_map/ppermute | solution.py:202
  16.8 11.6 %collective-permute-start.5 = (bf16[128,1024]{1,0:T(8,128)(2,1)S(1)}, bf16[128,1024]{1,0:T(8,128)(2,1)S(1)}, u32[]{:S(2)}, u32[]{:S(2)}) collective-permute-start(bf16[128,1024]{1,0:T(8,128)(2,1)S(1)} %get-tuple-element.69), channel_id=1, source_target_pairs={{0,3},{1,0},{2,1},{3,2},{128,131},{129,128},{130,129},{131,130},{4... | collective-permute-start | bytes 786440 | tf_op jit(solution)/shard_map/ppermute | solution.py:202
  54.7 11.2 %copy-start.1 = (bf16[128,4096]{1,0:T(8,128)(2,1)S(1)}, bf16[128,4096]{1,0:T(8,128)(2,1)}, u32[]{:S(2)}) copy-start(bf16[128,4096]{1,0:T(8,128)(2,1)} %rows_ref.1) | copy-start | bytes 3145732
  60.9 14.2 %collective-permute-start.6 = (bf16[128,1280]{1,0:T(8,128)(2,1)}, bf16[128,1280]{1,0:T(8,128)(2,1)S(1)}, u32[]{:S(2)}, u32[]{:S(2)}) collective-permute-start(bf16[128,1280]{1,0:T(8,128)(2,1)} %get-tuple-element.71), channel_id=1, source_target_pairs={{0,3},{1,0},{2,1},{3,2},{128,131},{129,128},{130,129},{131,130},{4... | collective-permute-start | bytes 983048 | tf_op jit(solution)/shard_map/ppermute | solution.py:202
  63.6 15.2 %collective-permute-start.7 = (bf16[128,1280]{1,0:T(8,128)(2,1)}, bf16[128,1280]{1,0:T(8,128)(2,1)S(1)}, u32[]{:S(2)}, u32[]{:S(2)}) collective-permute-start(bf16[128,1280]{1,0:T(8,128)(2,1)} %get-tuple-element.72), channel_id=1, source_target_pairs={{0,1},{1,2},{2,3},{3,0},{128,129},{129,130},{130,131},{131,128},{4... | collective-permute-start | bytes 983048 | tf_op jit(solution)/shard_map/ppermute | solution.py:202
  63.6 15.2 %collective-permute-start.8 = (bf16[128,1280]{1,0:T(8,128)(2,1)}, bf16[128,1280]{1,0:T(8,128)(2,1)S(1)}, u32[]{:S(2)}, u32[]{:S(2)}) collective-permute-start(bf16[128,1280]{1,0:T(8,128)(2,1)} %get-tuple-element.73), channel_id=1, source_target_pairs={{0,2},{1,3},{2,0},{3,1},{128,130},{129,131},{130,128},{131,129},{4... | collective-permute-start | bytes 983048 | tf_op jit(solution)/shard_map/ppermute | solution.py:202
  65.9 13.9 %copy-start.4 = (bf16[8,1280,128]{2,1,0:T(8,128)(2,1)S(1)}, bf16[8,1280,128]{2,1,0:T(8,128)(2,1)}, u32[]{:S(2)}) copy-start(bf16[8,1280,128]{2,1,0:T(8,128)(2,1)} %all-gather.4.cloned.1.call-done.refs_4_) | copy-start | bytes 7864324
  65.9 13.9 %copy-start.5 = (f32[1,4096]{1,0:T(1,128)S(1)}, f32[1,4096]{1,0:T(1,128)}, u32[]{:S(2)}) copy-start(f32[1,4096]{1,0:T(1,128)} %gain_ref.1) | copy-start | bytes 49156
  83.6 36.9 %collective-permute-start.10 = (bf16[32,4096]{1,0:T(8,128)(2,1)}, bf16[32,4096]{1,0:T(8,128)(2,1)S(1)}, u32[]{:S(2)}, u32[]{:S(2)}) collective-permute-start(bf16[32,4096]{1,0:T(8,128)(2,1)} %get-tuple-element.76.refs_9_), channel_id=1, source_target_pairs={{128,32},{160,64},{192,96},{224,0},{129,33},{161,65},{193,97},{225... | collective-permute-start | bytes 786440 | tf_op jit(solution)/shard_map/ppermute | solution.py:206
  84.9 35.6 %collective-permute-start.11 = (bf16[32,4096]{1,0:T(8,128)(2,1)}, bf16[32,4096]{1,0:T(8,128)(2,1)S(1)}, u32[]{:S(2)}, u32[]{:S(2)}) collective-permute-start(bf16[32,4096]{1,0:T(8,128)(2,1)} %get-tuple-element.76.refs_9_), channel_id=1, source_target_pairs={{128,64},{160,96},{192,0},{224,32},{129,65},{161,97},{193,1},{225,... | collective-permute-start | bytes 786440 | tf_op jit(solution)/shard_map/ppermute | solution.py:206
  86.2 34.3 %collective-permute-start.12 = (bf16[32,4096]{1,0:T(8,128)(2,1)}, bf16[32,4096]{1,0:T(8,128)(2,1)S(1)}, u32[]{:S(2)}, u32[]{:S(2)}) collective-permute-start(bf16[32,4096]{1,0:T(8,128)(2,1)} %get-tuple-element.76.refs_9_), channel_id=1, source_target_pairs={{128,96},{160,0},{192,32},{224,64},{129,97},{161,1},{193,33},{225,... | collective-permute-start | bytes 786440 | tf_op jit(solution)/shard_map/ppermute | solution.py:206
  87.5 33.0 %collective-permute-start.9 = (bf16[32,4096]{1,0:T(8,128)(2,1)}, bf16[32,4096]{1,0:T(8,128)(2,1)S(1)}, u32[]{:S(2)}, u32[]{:S(2)}) collective-permute-start(bf16[32,4096]{1,0:T(8,128)(2,1)} %get-tuple-element.76.refs_9_), channel_id=1, source_target_pairs={{128,0},{160,32},{192,64},{224,96},{129,1},{161,33},{193,65},{225,... | collective-permute-start | bytes 786440 | tf_op jit(solution)/shard_map/ppermute | solution.py:206
  97.5 1.7 %copy-start = (bf16[10240,128]{1,0:T(8,128)(2,1)S(1)}, bf16[10240,128]{1,0:T(8,128)(2,1)}, u32[]{:S(2)}) copy-start(bf16[10240,128]{1,0:T(8,128)(2,1)} %all-gather.6.cloned.1.call-done) | copy-start | bytes 7864324
Sparse Core Ops, SparseCore 0:
  9.4 45.2 all-gather.3
  56.5 40.9 all-gather.5

commit v9 on v8

--- a/solution.py
+++ b/solution.py
@@ -82,30 +82,39 @@
 
 
 def slab_products(hidden, slab_ref):
-    for k in range(NY):
-        total = None
-        for z in range(0, NZ, 2):
-            pair = jnp.concatenate([slab_ref[z], slab_ref[z + 1]], axis=1)
-            term = dot_nt(hidden[k][:, z * HD : (z + 2) * HD], pair)
-            total = term if total is None else total + term
-        yield k, total.astype(BF16)
+    rows = jnp.concatenate([ref[...] for ref in hidden], axis=0)
+    step = 2 * HD
+    for c in range(0, slab_ref.shape[1], step):
+        part = jnp.concatenate([slab_ref[z, c : c + step, :] for z in range(NZ)], axis=1)
+        yield slice(c, c + step), dot_nt(rows, part).astype(BF16)
 
 
 def packed_kernel(*refs):
-    for k, product in slab_products(refs[:NY], refs[NY]):
-        refs[NY + 1 + k][...] = product
+    length = refs[0].shape[0]
+    for at, product in slab_products(refs[:NY], refs[NY]):
+        for k in range(NY):
+            refs[NY + 1 + k][:, at] = product[k * length : (k + 1) * length]
 
 
 def sign_kernel(*refs):
     hidden, slab_ref, rows = refs[:NY], refs[NY], refs[NY + 1 : 2 * NY + 1]
-    out_ref, upper_ref = refs[-2:]
+    out_ref, upper_ref, held_ref, sems = refs[-4:]
     y_index = lax.axis_index("y")
-    upper = None
-    for k, product in slab_products(hidden, slab_ref):
-        out_ref[(y_index - k + NY) % NY] = product
-        term = jnp.sum(rows[k][...].astype(F32) * product.astype(F32), axis=0, keepdims=True)
-        upper = term if upper is None else upper + term
-    upper_ref[...] = upper
+    length = refs[0].shape[0]
+    for at, product in slab_products(hidden, slab_ref):
+        for k in range(NY):
+            out_ref[(y_index - k + NY) % NY, :, at] = product[k * length : (k + 1) * length]
+    upper_ref[...] = jnp.zeros_like(upper_ref)
+
+    @pl.when(lax.axis_index("pipe") == 1)
+    def _():
+        copies = [pltpu.make_async_copy(rows[k], held_ref.at[k], sems.at[k]) for k in range(NY)]
+        for copy in copies:
+            copy.start()
+        for k in range(NY):
+            copies[k].wait()
+            product = out_ref[(y_index - k + NY) % NY].astype(F32)
+            upper_ref[...] += jnp.sum(held_ref[k].astype(F32) * product, axis=0, keepdims=True)
 
 
 def summed(parts, h):
@@ -130,13 +139,16 @@
     rows, slab_ref, out_ref = refs[:NY], refs[NY], refs[-1]
     y_index = lax.axis_index("y")
     chunk = out_ref.shape[1]
-    for k in range(NY):
-        for z in range(0, NZ, 2):
-            pair = jnp.concatenate([slab_ref[z], slab_ref[z + 1]], axis=1)
-            term = dot_nn(rows[k][...], pair).astype(BF16)
+    length = rows[0].shape[0]
+    grads = jnp.concatenate([ref[...] for ref in rows], axis=0)
+    for z in range(0, NZ, 2):
+        pair = jnp.concatenate([slab_ref[z], slab_ref[z + 1]], axis=1)
+        terms = dot_nn(grads, pair).astype(BF16)
+        for k in range(NY):
             for c in range(NX):
                 place = c * NY + (y_index - k + NY) % NY
-                out_ref[place, :, z * HD : (z + 2) * HD] = term[c * chunk : (c + 1) * chunk]
+                start = k * length + c * chunk
+                out_ref[place, :, z * HD : (z + 2) * HD] = terms[start : start + chunk]
 
 
 def norm_back_kernel(inputs_ref, gain_ref, cotangent_ref, terms_ref, out_ref):
@@ -176,9 +188,11 @@
     out_ref[...] = total_ref[...].astype(BF16)
 
 
-def lower_kernel(count, mixed_ref, upper_ref, projected_ref, *refs):
-    parts, out_ref, turned_ref = refs[:NY], refs[-2], refs[-1]
-    projected = [projected_ref.at[k] for k in range(NY)]
+def lower_kernel(count, mixed_ref, upper_ref, *refs):
+    parts, projected_ref, out_ref, turned_ref, held_ref, sem = refs[:NY], *refs[NY:]
+    copy = pltpu.make_async_copy(projected_ref, held_ref, sem)
+    copy.start()
+    projected = [held_ref.at[k] for k in range(NY)]
     pipe_index = lax.axis_index("pipe")
     x_index = lax.axis_index("tensor")
     chunk = turned_ref.shape[0] // NX
@@ -189,6 +203,7 @@
         lambda h: summed(parts, h),
         lambda h: turned_ref[:, h * HD : (h + 1) * HD],
     )
+    copy.wait()
     for h, column in enumerate(columns):
         at = slice(h * HD, (h + 1) * HD)
         lower = column.astype(BF16).astype(F32)
@@ -259,7 +274,8 @@
         (by_y, jax.ShapeDtypeStruct((1, rows), F32)),
         (*hidden_slab, sign_slab, *slab_rows, backward),
         flops,
-        unread=1,
+        unread=NY + 1,
+        scratch=[pltpu.VMEM(by_y.shape, BF16), pltpu.SemaphoreType.DMA((NY,))],
     )
     projected = lax.cond(
         is_last,
@@ -275,9 +291,14 @@
     partial_sum = call(
         functools.partial(lower_kernel, tokens * NZ * NY),
         jax.ShapeDtypeStruct((1, rows), F32),
-        (grad_mixed_lower, upper_total, projected, *parts),
+        (grad_mixed_lower, upper_total, *parts, projected),
         10**8,
-        scratch=[pltpu.VMEM(mixed_rows.shape, BF16)],
+        unread=1,
+        scratch=[
+            pltpu.VMEM(mixed_rows.shape, BF16),
+            pltpu.VMEM(by_y.shape, BF16),
+            pltpu.SemaphoreType.DMA,
+        ],
     )
     copies = jnp.broadcast_to(partial_sum, (NZ * NY, rows))
     return jnp.sum(lax.all_to_all(copies, ("z", "y"), 0, 0), axis=0, keepdims=True)

time: 152 us -> 148 us (0.974)
  Pallas kernels: 22.6 us -> 17.1 us
    pallas_call x6, Pallas kernels: 22.6 us -> 17.1 us  [call(): pl.pallas_call(kernel, out_shape=outs, in_specs=[VMEM] * (len(args) - unr...]
    all_gather x1, waiting for transfers between devices: 8.71 us -> 10.3 us  [local(): sign_slab = lax.all_gather(later_sign, 'z', axis=0, tiled=False)]
  transfers between devices with their start and end apart: 12 -> 12, of which waited for: 6 -> 6; matrix products, arithmetic and copies ran while one was open for 2% -> 3% of each run, Pallas kernels for 13% -> 10%
where the time goes in v9:
time: 148 us
  waiting for transfers between devices  53.2 us (36%)
  blocking collectives  32.5 us (22%)
  Pallas kernels  17.1 us (12%)
  starting transfers between devices  16.2 us (11%)
  between operations  13.5 us (9%)
  local copies, waits for them, and re-layouts  7.41 us (5%)
  matrix products  4.71 us (3%)
  other arithmetic  2.88 us (2%)
    all_gather x1, waiting for transfers between devices, local(): weight_slab = lax.all_gather(weight, 'z', axis=0, tiled=False)  26.3 us
    pallas_call x6, Pallas kernels, call(): pl.pallas_call(kernel, out_shape=outs, in_specs=[VMEM] * (len(args) - unr...  17.1 us
    ppermute x6, waiting for transfers between devices, send_y(): return lax.ppermute(value, ('pipe', 'y'), pairs)  16.5 us
    all_to_all x1, blocking collectives, local(): lax.all_to_all(signed, 'y', 0, 0)  16.5 us
    all_to_all x1, blocking collectives, local(): lax.all_to_all(copies, ('z', 'y'), 0, 0)  16 us
    ppermute x6, starting transfers between devices, send_y(): return lax.ppermute(value, ('pipe', 'y'), pairs)  10.9 us
    all_gather x1, waiting for transfers between devices, local(): sign_slab = lax.all_gather(later_sign, 'z', axis=0, tiled=False)  10.3 us
    ppermute x4, starting transfers between devices, send_down(): lax.ppermute(value, ('pipe', 'tensor'), [(NX + i, (i + steps) % NX) for i...  5.34 us
  transfers between devices with their start and end apart: 12, of which 6 were waited for; matrix products, arithmetic and copies ran while one was open for 3% of the time, Pallas kernels for 10%

profile of v9, /device:TPU:2, one launch (start us, length us, event | category | flops | bytes accessed | tf_op | source)
XLA Modules:
  0.0 147.6 jit_solution(11786053998233046547)
XLA Ops:
  7.2 2.0 %add_convert_fusion = bf16[1,1280,128]{2,1,0:T(8,128)(2,1)} fusion(bf16[1,1280,128]{2,1,0:T(8,128)(2,1)} %param.17, bf16[1,1280,128]{2,1,0:T(8,128)(2,1)} %param.16, f32[1280]{0:T(1024)S(1)} %reduce.1), kind=kLoop, calls=%fused_computation.9 | loop fusion | flops 819200 | bytes 988160 | tf_op jit(solution)/shard_map/convert_element_type | solution.py:231
  9.4 1.2 copy-done.2
  10.6 1.7 %shard_map.77 = (bf16[128,1024]{1,0:T(8,128)(2,1)S(1)}, bf16[128,1024]{1,0:T(8,128)(2,1)S(1)}, bf16[128,1024]{1,0:T(8,128)(2,1)S(1)}, bf16[128,1024]{1,0:T(8,128)(2,1)S(1)}, bf16[32,4096]{1,0:T(8,128)(2,1)}) custom-call(bf16[128,4096]{1,0:T(8,128)(2,1)S(1)} %bitcast.6, f32[1,4096]{1,0:T(1,128)} %gain_ref.1), custom_call_target="tpu_custom_call" | custom-call | flops 10000000 | bytes 100000 | tf_op jit(solution)/shard_map/pallas_call | solution.py:37
  12.3 1.6 %collective-permute-start.3 = (bf16[128,1024]{1,0:T(8,128)(2,1)S(1)}, bf16[128,1024]{1,0:T(8,128)(2,1)S(1)}, u32[]{:S(2)}, u32[]{:S(2)}) collective-permute-start(bf16[128,1024]{1,0:T(8,128)(2,1)S(1)} %get-tuple-element.67), channel_id=1, source_target_pairs={{0,1},{1,2},{2,3},{3,0},{128,129},{129,130},{130,131},{131,128},{4... | collective-permute-start | bytes 786440 | tf_op jit(solution)/shard_map/ppermute | solution.py:217
  13.9 2.9 %collective-permute-start.4 = (bf16[128,1024]{1,0:T(8,128)(2,1)S(1)}, bf16[128,1024]{1,0:T(8,128)(2,1)S(1)}, u32[]{:S(2)}, u32[]{:S(2)}) collective-permute-start(bf16[128,1024]{1,0:T(8,128)(2,1)S(1)} %get-tuple-element.68), channel_id=1, source_target_pairs={{0,2},{1,3},{2,0},{3,1},{128,130},{129,131},{130,128},{131,129},{4... | collective-permute-start | bytes 786440 | tf_op jit(solution)/shard_map/ppermute | solution.py:217
  16.8 1.3 collective-permute-start.5
  18.1 3.5 %collective-permute-done.3.refs_1_ = bf16[128,1024]{1,0:T(8,128)(2,1)S(1)} collective-permute-done((bf16[128,1024]{1,0:T(8,128)(2,1)S(1)}, bf16[128,1024]{1,0:T(8,128)(2,1)S(1)}, u32[]{:S(2)}, u32[]{:S(2)}) %collective-permute-start.3) | collective-permute-done | bytes 262176 | tf_op jit(solution)/shard_map/ppermute | solution.py:217
  21.6 6.8 %collective-permute-done.4.refs_2_ = bf16[128,1024]{1,0:T(8,128)(2,1)S(1)} collective-permute-done((bf16[128,1024]{1,0:T(8,128)(2,1)S(1)}, bf16[128,1024]{1,0:T(8,128)(2,1)S(1)}, u32[]{:S(2)}, u32[]{:S(2)}) %collective-permute-start.4) | collective-permute-done | bytes 262176 | tf_op jit(solution)/shard_map/ppermute | solution.py:217
  28.4 26.3 %all-gather.4.cloned.1.call-done.refs_4_ = bf16[8,1280,128]{2,1,0:T(8,128)(2,1)} async-done(((bf16[1,1280,128]{2,1,0:T(8,128)(2,1)}), bf16[8,1280,128]{2,1,0:T(8,128)(2,1)}) %all-gather.4.cloned.1.call-update) | async-done | bytes 2621456 | tf_op jit(solution)/shard_map/all_gather | solution.py:232
  54.7 4.3 %shard_map.78 = (bf16[128,1280]{1,0:T(8,128)(2,1)S(1)}, bf16[128,1280]{1,0:T(8,128)(2,1)}, bf16[128,1280]{1,0:T(8,128)(2,1)}, bf16[128,1280]{1,0:T(8,128)(2,1)}) custom-call(bf16[128,1024]{1,0:T(8,128)(2,1)S(1)} %get-tuple-element.66.refs_0_, bf16[128,1024]{1,0:T(8,128)(2,1)S(1)} %collective-permute-done.3.refs_1_, ...), custom_call_target="tpu_custom_call" | custom-call | flops 1342177280 | bytes 100000 | tf_op jit(solution)/shard_map/pallas_call | solution.py:37
  59.0 2.7 %collective-permute-start.6 = (bf16[128,1280]{1,0:T(8,128)(2,1)}, bf16[128,1280]{1,0:T(8,128)(2,1)S(1)}, u32[]{:S(2)}, u32[]{:S(2)}) collective-permute-start(bf16[128,1280]{1,0:T(8,128)(2,1)} %get-tuple-element.71), channel_id=1, source_target_pairs={{0,3},{1,0},{2,1},{3,2},{128,131},{129,128},{130,129},{131,130},{4... | collective-permute-start | bytes 983048 | tf_op jit(solution)/shard_map/ppermute | solution.py:217
  61.8 2.3 %collective-permute-start.8 = (bf16[128,1280]{1,0:T(8,128)(2,1)}, bf16[128,1280]{1,0:T(8,128)(2,1)S(1)}, u32[]{:S(2)}, u32[]{:S(2)}) collective-permute-start(bf16[128,1280]{1,0:T(8,128)(2,1)} %get-tuple-element.73), channel_id=1, source_target_pairs={{0,2},{1,3},{2,0},{3,1},{128,130},{129,131},{130,128},{131,129},{4... | collective-permute-start | bytes 983048 | tf_op jit(solution)/shard_map/ppermute | solution.py:217
  64.1 6.6 %shard_map.76 = (bf16[128,1024]{1,0:T(8,128)(2,1)S(1)}, bf16[32,4096]{1,0:T(8,128)(2,1)}) custom-call(bf16[128,4096]{1,0:T(8,128)(2,1)S(1)} %copy-done.1, bf16[4096,1024]{1,0:T(8,128)(2,1)} %bitcast.7), custom_call_target="tpu_custom_call" | custom-call | flops 1000000000 | bytes 100000 | tf_op jit(solution)/shard_map/pallas_call | solution.py:37
  70.7 2.4 %collective-permute-done.6.refs_1_ = bf16[128,1280]{1,0:T(8,128)(2,1)S(1)} collective-permute-done((bf16[128,1280]{1,0:T(8,128)(2,1)}, bf16[128,1280]{1,0:T(8,128)(2,1)S(1)}, u32[]{:S(2)}, u32[]{:S(2)}) %collective-permute-start.6) | collective-permute-done | bytes 327712 | tf_op jit(solution)/shard_map/ppermute | solution.py:217
  73.2 3.8 %collective-permute-done.7.refs_2_ = bf16[128,1280]{1,0:T(8,128)(2,1)S(1)} collective-permute-done((bf16[128,1280]{1,0:T(8,128)(2,1)}, bf16[128,1280]{1,0:T(8,128)(2,1)S(1)}, u32[]{:S(2)}, u32[]{:S(2)}) %collective-permute-start.7) | collective-permute-done | bytes 327712 | tf_op jit(solution)/shard_map/ppermute | solution.py:217
  77.0 1.0 shard_map.79
  78.0 3.8 %conditional.3 = (bf16[32,4096]{1,0:T(8,128)(2,1)}, bf16[128,1280]{1,0:T(8,128)(2,1)}, bf16[128,1280]{1,0:T(8,128)(2,1)}, bf16[128,1280]{1,0:T(8,128)(2,1)}, bf16[128,1280]{1,0:T(8,128)(2,1)}) conditional(s32[]{:T(128)} %convert_element_type.20, () %tuple.27, (bf16[128,1280]{1,0:T(8,128)(2,1)S(1)}, bf16[8,1280,128]{2,1,0:T(8,128)(2,1)S(1)}, ...), branch_computations={%region_0.0_spmd, %region_1.0_spmd} | conditional | flops 1343177216 | bytes 9244188 | solution.py:269
  78.8 0.8 broadcast.17.clone
  80.3 0.8 broadcast.17.clone.2
  81.8 1.3 collective-permute-start.10
  83.1 1.3 collective-permute-start.11
  84.4 1.3 collective-permute-start.12
  85.7 1.5 collective-permute-start.9
  87.1 10.3 %all-gather.6.cloned.1.call-done = bf16[10240,128]{1,0:T(8,128)(2,1)} async-done(((bf16[1280,128]{1,0:T(8,128)(2,1)}), bf16[10240,128]{1,0:T(8,128)(2,1)}) %all-gather.6.cloned.1.call-update) | async-done | bytes 2621456 | tf_op jit(solution)/shard_map/all_gather | solution.py:239
  97.4 1.7 %copy-done = bf16[10240,128]{1,0:T(8,128)(2,1)S(1)} copy-done((bf16[10240,128]{1,0:T(8,128)(2,1)S(1)}, bf16[10240,128]{1,0:T(8,128)(2,1)}, u32[]{:S(2)}) %copy-start) | copy-done | bytes 2621464
  99.2 1.6 %shard_map.80 = (bf16[4,128,1280]{2,1,0:T(8,128)(2,1)S(1)}, f32[1,1280]{1,0:T(1,128)S(1)}) custom-call(bf16[128,1024]{1,0:T(8,128)(2,1)S(1)} %get-tuple-element.66.refs_0_, bf16[128,1024]{1,0:T(8,128)(2,1)S(1)} %collective-permute-done.3.refs_1_, bf16[128,1024]{1,0:T(8,128)(2,1)S(1)} %collective-permute-done.4.refs_2_, ...), custom_call_target="tpu_custom_call" | custom-call | flops 1342177280 | bytes 100000 | tf_op jit(solution)/shard_map/pallas_call | solution.py:37
  100.8 16.5 %conditional.4 = (bf16[4,128,1280]{2,1,0:T(8,128)(2,1)}) conditional(s32[]{:T(128)} %convert_element_type.20, bf16[4,128,1280]{2,1,0:T(8,128)(2,1)S(1)} %get-tuple-element.82, () %tuple.30), branch_computations={%region_2.0_spmd, %region_3.0_spmd} | conditional | bytes 2621448 | solution.py:280
  100.8 16.5 %all_to_all.14 = bf16[4,128,1280]{2,1,0:T(8,128)(2,1)} all-to-all(bf16[4,128,1280]{2,1,0:T(8,128)(2,1)S(1)} %param.2), channel_id=1, replica_groups=mesh['pipe'=2,'tensor'=4,'z'=8,'y'=4] {'y'}, dimensions={0} | all-to-all | bytes 2621440 | tf_op jit(solution)/shard_map/cond/branch_0_fun/all_to_all | solution.py:283
  117.3 4.7 %conditional.5 = (bf16[128,1024]{1,0:T(8,128)(2,1)S(1)}) conditional(s32[]{:T(128)} %convert_element_type.20, (bf16[32,4096]{1,0:T(8,128)(2,1)S(1)}, bf16[32,4096]{1,0:T(8,128)(2,1)S(1)}, bf16[32,4096]{1,0:T(8,128)(2,1)S(1)}, bf16[32,4096]{1,0:T(8,128)(2,1)S(1)}, bf16[4096,1024]{1,0:T(8,128)(2,1)}) %tuple.44, () %tuple.33), branch_computations={%region_4.0_spmd, %region_5.0_spmd} | conditional | flops 1078067200 | bytes 9699336 | solution.py:286
  117.4 4.7 %convolution_convert_fusion = bf16[128,1024]{1,0:T(8,128)(2,1)S(1)} fusion(bf16[4096,1024]{1,0:T(8,128)(2,1)} %get-tuple-element.41, bf16[32,4096]{1,0:T(8,128)(2,1)S(1)} %get-tuple-element.40, bf16[32,4096]{1,0:T(8,128)(2,1)S(1)} %get-tuple-element.39, bf16[32,4096]{1,0:T(8,128)(2,1)S(1)} %get-tuple-element.38, bf16[32,4096]{1,0:T(8,128)(2,1)S(1)} %get-tuple-element.37), kind=kOutput, calls=%fused_computation | convolution fusion | flops 1078067200 | bytes 9699328 | tf_op jit(solution)/shard_map/cond/branch_0_fun/dot_general | solution.py:25
  122.1 1.8 %shard_map.81 = f32[1,1280]{1,0:T(1,128)S(1)} custom-call(bf16[128,1024]{1,0:T(8,128)(2,1)S(1)} %get-tuple-element.99.mixed_ref, f32[1,1280]{1,0:T(1,128)S(1)} %get-tuple-element.87.upper_ref, bf16[128,1280]{1,0:T(8,128)(2,1)S(1)} %get-tuple-element.70.refs_0_, bf16[128,1280]{1,0:T(8,128)(2,1)S(1)} %collective-permute-done.6.refs_1_, ...), custom_call_target="tpu_custom_call" | custom-call | flops 100000000 | bytes 100000 | tf_op jit(solution)/shard_map/pallas_call | solution.py:37
  124.1 16.0 %all_to_all.15 = f32[32,1,1280]{2,1,0:T(1,128)S(1)} all-to-all(f32[32,1,1280]{2,1,0:T(1,128)S(1)} %broadcast_in_dim.8), channel_id=1, replica_groups=mesh['pipe'=2,'tensor'=4,'z'=8,'y'=4] {'z','y'}, dimensions={0} | all-to-all | bytes 327680 | tf_op jit(solution)/shard_map/all_to_all | solution.py:304
  (27 shorter events, 3.9 us)
Async XLA Ops:
  6.5 48.2 %all-gather.4.cloned.1.call-start = ((), (), s32[]{:S(2)}) async-start(), calls=%async_computation.3 | async-start | bytes 2949120 | tf_op jit(solution)/shard_map/all_gather | solution.py:232
  9.3 88.1 %all-gather.6.cloned.1.call-start = ((), (), s32[]{:S(2)}) async-start(), calls=%async_computation.4 | async-start | bytes 2949120 | tf_op jit(solution)/shard_map/all_gather | solution.py:239
  9.4 1.2 copy-start.2
  12.3 9.3 %collective-permute-start.3 = (bf16[128,1024]{1,0:T(8,128)(2,1)S(1)}, bf16[128,1024]{1,0:T(8,128)(2,1)S(1)}, u32[]{:S(2)}, u32[]{:S(2)}) collective-permute-start(bf16[128,1024]{1,0:T(8,128)(2,1)S(1)} %get-tuple-element.67), channel_id=1, source_target_pairs={{0,1},{1,2},{2,3},{3,0},{128,129},{129,130},{130,131},{131,128},{4... | collective-permute-start | bytes 786440 | tf_op jit(solution)/shard_map/ppermute | solution.py:217
  13.9 14.5 %collective-permute-start.4 = (bf16[128,1024]{1,0:T(8,128)(2,1)S(1)}, bf16[128,1024]{1,0:T(8,128)(2,1)S(1)}, u32[]{:S(2)}, u32[]{:S(2)}) collective-permute-start(bf16[128,1024]{1,0:T(8,128)(2,1)S(1)} %get-tuple-element.68), channel_id=1, source_target_pairs={{0,2},{1,3},{2,0},{3,1},{128,130},{129,131},{130,128},{131,129},{4... | collective-permute-start | bytes 786440 | tf_op jit(solution)/shard_map/ppermute | solution.py:217
  16.8 11.6 %collective-permute-start.5 = (bf16[128,1024]{1,0:T(8,128)(2,1)S(1)}, bf16[128,1024]{1,0:T(8,128)(2,1)S(1)}, u32[]{:S(2)}, u32[]{:S(2)}) collective-permute-start(bf16[128,1024]{1,0:T(8,128)(2,1)S(1)} %get-tuple-element.69), channel_id=1, source_target_pairs={{0,3},{1,0},{2,1},{3,2},{128,131},{129,128},{130,129},{131,130},{4... | collective-permute-start | bytes 786440 | tf_op jit(solution)/shard_map/ppermute | solution.py:217
  54.7 9.3 %copy-start.1 = (bf16[128,4096]{1,0:T(8,128)(2,1)S(1)}, bf16[128,4096]{1,0:T(8,128)(2,1)}, u32[]{:S(2)}) copy-start(bf16[128,4096]{1,0:T(8,128)(2,1)} %rows_ref.1) | copy-start | bytes 3145732
  59.0 14.1 %collective-permute-start.6 = (bf16[128,1280]{1,0:T(8,128)(2,1)}, bf16[128,1280]{1,0:T(8,128)(2,1)S(1)}, u32[]{:S(2)}, u32[]{:S(2)}) collective-permute-start(bf16[128,1280]{1,0:T(8,128)(2,1)} %get-tuple-element.71), channel_id=1, source_target_pairs={{0,3},{1,0},{2,1},{3,2},{128,131},{129,128},{130,129},{131,130},{4... | collective-permute-start | bytes 983048 | tf_op jit(solution)/shard_map/ppermute | solution.py:217
  61.7 15.2 %collective-permute-start.7 = (bf16[128,1280]{1,0:T(8,128)(2,1)}, bf16[128,1280]{1,0:T(8,128)(2,1)S(1)}, u32[]{:S(2)}, u32[]{:S(2)}) collective-permute-start(bf16[128,1280]{1,0:T(8,128)(2,1)} %get-tuple-element.72), channel_id=1, source_target_pairs={{0,1},{1,2},{2,3},{3,0},{128,129},{129,130},{130,131},{131,128},{4... | collective-permute-start | bytes 983048 | tf_op jit(solution)/shard_map/ppermute | solution.py:217
  61.8 15.2 %collective-permute-start.8 = (bf16[128,1280]{1,0:T(8,128)(2,1)}, bf16[128,1280]{1,0:T(8,128)(2,1)S(1)}, u32[]{:S(2)}, u32[]{:S(2)}) collective-permute-start(bf16[128,1280]{1,0:T(8,128)(2,1)} %get-tuple-element.73), channel_id=1, source_target_pairs={{0,2},{1,3},{2,0},{3,1},{128,130},{129,131},{130,128},{131,129},{4... | collective-permute-start | bytes 983048 | tf_op jit(solution)/shard_map/ppermute | solution.py:217
  64.1 13.9 %copy-start.4 = (bf16[8,1280,128]{2,1,0:T(8,128)(2,1)S(1)}, bf16[8,1280,128]{2,1,0:T(8,128)(2,1)}, u32[]{:S(2)}) copy-start(bf16[8,1280,128]{2,1,0:T(8,128)(2,1)} %all-gather.4.cloned.1.call-done.refs_4_) | copy-start | bytes 7864324
  64.1 13.9 %copy-start.5 = (f32[1,4096]{1,0:T(1,128)S(1)}, f32[1,4096]{1,0:T(1,128)}, u32[]{:S(2)}) copy-start(f32[1,4096]{1,0:T(1,128)} %gain_ref.1) | copy-start | bytes 49156
  81.8 35.6 %collective-permute-start.10 = (bf16[32,4096]{1,0:T(8,128)(2,1)}, bf16[32,4096]{1,0:T(8,128)(2,1)S(1)}, u32[]{:S(2)}, u32[]{:S(2)}) collective-permute-start(bf16[32,4096]{1,0:T(8,128)(2,1)} %get-tuple-element.76.refs_9_), channel_id=1, source_target_pairs={{128,32},{160,64},{192,96},{224,0},{129,33},{161,65},{193,97},{225... | collective-permute-start | bytes 786440 | tf_op jit(solution)/shard_map/ppermute | solution.py:221
  83.1 34.3 %collective-permute-start.11 = (bf16[32,4096]{1,0:T(8,128)(2,1)}, bf16[32,4096]{1,0:T(8,128)(2,1)S(1)}, u32[]{:S(2)}, u32[]{:S(2)}) collective-permute-start(bf16[32,4096]{1,0:T(8,128)(2,1)} %get-tuple-element.76.refs_9_), channel_id=1, source_target_pairs={{128,64},{160,96},{192,0},{224,32},{129,65},{161,97},{193,1},{225,... | collective-permute-start | bytes 786440 | tf_op jit(solution)/shard_map/ppermute | solution.py:221
  84.4 33.0 %collective-permute-start.12 = (bf16[32,4096]{1,0:T(8,128)(2,1)}, bf16[32,4096]{1,0:T(8,128)(2,1)S(1)}, u32[]{:S(2)}, u32[]{:S(2)}) collective-permute-start(bf16[32,4096]{1,0:T(8,128)(2,1)} %get-tuple-element.76.refs_9_), channel_id=1, source_target_pairs={{128,96},{160,0},{192,32},{224,64},{129,97},{161,1},{193,33},{225,... | collective-permute-start | bytes 786440 | tf_op jit(solution)/shard_map/ppermute | solution.py:221
  85.7 31.7 %collective-permute-start.9 = (bf16[32,4096]{1,0:T(8,128)(2,1)}, bf16[32,4096]{1,0:T(8,128)(2,1)S(1)}, u32[]{:S(2)}, u32[]{:S(2)}) collective-permute-start(bf16[32,4096]{1,0:T(8,128)(2,1)} %get-tuple-element.76.refs_9_), channel_id=1, source_target_pairs={{128,0},{160,32},{192,64},{224,96},{129,1},{161,33},{193,65},{225,... | collective-permute-start | bytes 786440 | tf_op jit(solution)/shard_map/ppermute | solution.py:221
  97.4 1.7 %copy-start = (bf16[10240,128]{1,0:T(8,128)(2,1)S(1)}, bf16[10240,128]{1,0:T(8,128)(2,1)}, u32[]{:S(2)}) copy-start(bf16[10240,128]{1,0:T(8,128)(2,1)} %all-gather.6.cloned.1.call-done) | copy-start | bytes 7864324
Sparse Core Ops, SparseCore 0:
  9.4 45.2 all-gather.3
  56.5 40.8 all-gather.5

commit v10 on v9

--- a/solution.py
+++ b/solution.py
@@ -60,19 +60,24 @@
         refs[k][...] = turned_ref[k]
 
 
-def attention_back(packed_of, grads_of):
+def attention_weights(packed_of):
+    queries = jnp.concatenate([packed_of(h) for h in range(QH)], axis=0)
+    keys = packed_of(QH)
+    scores = dot_nt(queries, keys) * (1.0 / math.sqrt(HD))
+    rows = lax.broadcasted_iota(jnp.int32, scores.shape, 0) % keys.shape[0]
+    cols = lax.broadcasted_iota(jnp.int32, scores.shape, 1)
+    scores = jnp.where(cols <= rows, scores, -1000000000.0)
+    top = jnp.max(scores, axis=-1, keepdims=True)
+    raised = jnp.exp(scores - top)
+    return raised / jnp.sum(raised, axis=-1, keepdims=True)
+
+
+def attention_back(packed_of, grads_of, weights):
     factor = 1.0 / math.sqrt(HD)
     queries = jnp.concatenate([packed_of(h) for h in range(QH)], axis=0)
     grads = jnp.concatenate([grads_of(h) for h in range(QH)], axis=0)
     keys, values = packed_of(QH), packed_of(QH + 1)
     length = keys.shape[0]
-    scores = dot_nt(queries, keys) * factor
-    rows = lax.broadcasted_iota(jnp.int32, scores.shape, 0) % length
-    cols = lax.broadcasted_iota(jnp.int32, scores.shape, 1)
-    scores = jnp.where(cols <= rows, scores, -1000000000.0)
-    top = jnp.max(scores, axis=-1, keepdims=True)
-    raised = jnp.exp(scores - top)
-    weights = raised / jnp.sum(raised, axis=-1, keepdims=True)
     grad_weights = dot_nt(grads, values)
     inner = jnp.sum(grad_weights * weights, axis=-1, keepdims=True)
     grad_scores = (weights * (grad_weights - inner) * factor).astype(BF16)
@@ -127,9 +132,9 @@
 
 def upper_kernel(grad_ref, *refs):
     parts, grad_packed_ref = refs[:-1], refs[-1]
+    packed_of = lambda h: summed(parts, h)
     columns = attention_back(
-        lambda h: summed(parts, h),
-        lambda h: grad_ref[:, h * HD : (h + 1) * HD],
+        packed_of, lambda h: grad_ref[:, h * HD : (h + 1) * HD], attention_weights(packed_of)
     )
     for h, column in enumerate(columns):
         grad_packed_ref[:, h * HD : (h + 1) * HD] = column.astype(BF16)
@@ -188,8 +193,15 @@
     out_ref[...] = total_ref[...].astype(BF16)
 
 
-def lower_kernel(count, mixed_ref, upper_ref, *refs):
-    parts, projected_ref, out_ref, turned_ref, held_ref, sem = refs[:NY], *refs[NY:]
+def ready_kernel(*refs):
+    parts, packed_ref, weights_ref = refs[:NY], refs[NY], refs[NY + 1]
+    for h in range(QH + 2):
+        packed_ref[:, h * HD : (h + 1) * HD] = summed(parts, h)
+    weights_ref[...] = attention_weights(lambda h: packed_ref[:, h * HD : (h + 1) * HD])
+
+
+def lower_kernel(count, mixed_ref, upper_ref, packed_ref, weights_ref, *refs):
+    projected_ref, out_ref, turned_ref, held_ref, sem = refs
     copy = pltpu.make_async_copy(projected_ref, held_ref, sem)
     copy.start()
     projected = [held_ref.at[k] for k in range(NY)]
@@ -200,8 +212,9 @@
         place = pl.multiple_of(((x_index - j + NX) % NX) * chunk, chunk)
         turned_ref[pl.ds(place, chunk), :] = mixed_ref[j * chunk : (j + 1) * chunk]
     columns = attention_back(
-        lambda h: summed(parts, h),
+        lambda h: packed_ref[:, h * HD : (h + 1) * HD],
         lambda h: turned_ref[:, h * HD : (h + 1) * HD],
+        weights_ref[...],
     )
     copy.wait()
     for h, column in enumerate(columns):
@@ -277,10 +290,11 @@
         unread=NY + 1,
         scratch=[pltpu.VMEM(by_y.shape, BF16), pltpu.SemaphoreType.DMA((NY,))],
     )
-    projected = lax.cond(
+    ready_shapes = (packed_rows, jax.ShapeDtypeStruct((QH * tokens, tokens), F32))
+    projected, packed, weights = lax.cond(
         is_last,
-        lambda: jnp.zeros(by_y.shape, BF16),
-        lambda: lax.all_to_all(signed, "y", 0, 0),
+        lambda: tuple(jnp.zeros(shape.shape, shape.dtype) for shape in (by_y, *ready_shapes)),
+        lambda: (lax.all_to_all(signed, "y", 0, 0), *call(ready_kernel, ready_shapes, parts, 10**8)),
     )
     arrived = lax.optimization_barrier((*arrived, projected))[:NX]
     grad_mixed_lower = lax.cond(
@@ -291,7 +305,7 @@
     partial_sum = call(
         functools.partial(lower_kernel, tokens * NZ * NY),
         jax.ShapeDtypeStruct((1, rows), F32),
-        (grad_mixed_lower, upper_total, *parts, projected),
+        (grad_mixed_lower, upper_total, packed, weights, projected),
         10**8,
         unread=1,
         scratch=[

time: 148 us -> 149 us (level)
  blocking collectives: 32.5 us -> 15.9 us
  waiting for transfers between devices: 53.2 us -> 65.6 us
  starting transfers between devices: 16.2 us -> 20.6 us
  Pallas kernels: 17.1 us -> 19.4 us
  local copies, waits for them, and re-layouts: 7.41 us -> 5.2 us
    all_to_all x1 -> x0, blocking collectives: 16.5 us -> none  [local(): lax.all_to_all(signed, 'y', 0, 0)]
    all_to_all x0 -> x1, waiting for transfers between devices: none -> 10.5 us  [local(): lax.all_to_all(signed, 'y', 0, 0)]
    all_to_all x0 -> x1, starting transfers between devices: none -> 4.29 us  [local(): lax.all_to_all(signed, 'y', 0, 0)]
    all_gather x1, waiting for transfers between devices: 10.3 us -> 12.7 us  [local(): sign_slab = lax.all_gather(later_sign, 'z', axis=0, tiled=False)]
    pallas_call x6 -> x7, Pallas kernels: 17.1 us -> 19.4 us  [call(): pl.pallas_call(kernel, out_shape=outs, in_specs=[VMEM] * (len(args) - unr...]
    another operation x5, local copies, waits for them, and re-layouts: 3.75 us -> 1.54 us
    unnamed x10 -> x14, local copies, waits for them, and re-layouts: 2.97 us -> 2.98 us
  transfers between devices with their start and end apart: 12 -> 13, of which waited for: 6 -> 7; matrix products, arithmetic and copies ran while one was open for 3% -> 1% of each run, Pallas kernels for 10% -> 12%
where the time goes in v10:
time: 149 us; the launch traced here: 148 us
  waiting for transfers between devices  65.6 us (44%)
  starting transfers between devices  20.6 us (14%)
  Pallas kernels  19.4 us (13%)
  blocking collectives  15.9 us (11%)
  between operations  13.6 us (9%)
  local copies, waits for them, and re-layouts  5.2 us (3%)
  matrix products  4.87 us (3%)
  other arithmetic  2.87 us (2%)
    all_gather x1, waiting for transfers between devices, local(): weight_slab = lax.all_gather(weight, 'z', axis=0, tiled=False)  26.3 us
    pallas_call x7, Pallas kernels, call(): pl.pallas_call(kernel, out_shape=outs, in_specs=[VMEM] * (len(args) - unr...  19.4 us
    ppermute x6, waiting for transfers between devices, send_y(): return lax.ppermute(value, ('pipe', 'y'), pairs)  16 us
    all_to_all x1, blocking collectives, local(): lax.all_to_all(copies, ('z', 'y'), 0, 0)  15.9 us
    all_gather x1, waiting for transfers between devices, local(): sign_slab = lax.all_gather(later_sign, 'z', axis=0, tiled=False)  12.7 us
    ppermute x6, starting transfers between devices, send_y(): return lax.ppermute(value, ('pipe', 'y'), pairs)  10.9 us
    all_to_all x1, waiting for transfers between devices, local(): lax.all_to_all(signed, 'y', 0, 0)  10.5 us
    ppermute x4, starting transfers between devices, send_down(): lax.ppermute(value, ('pipe', 'tensor'), [(NX + i, (i + steps) % NX) for i...  5.34 us
  transfers between devices with their start and end apart: 13, of which 7 were waited for; matrix products, arithmetic and copies ran while one was open for 1% of the time, Pallas kernels for 12%

profile of v10, /device:TPU:2, one launch (start us, length us, event | category | flops | bytes accessed | tf_op | source)
XLA Modules:
  0.0 148.0 jit_solution(11483294742743819552)
XLA Ops:
  7.2 2.0 %add_convert_fusion = bf16[1,1280,128]{2,1,0:T(8,128)(2,1)} fusion(bf16[1,1280,128]{2,1,0:T(8,128)(2,1)} %param.17, bf16[1,1280,128]{2,1,0:T(8,128)(2,1)} %param.16, f32[1280]{0:T(1024)S(1)} %reduce.1), kind=kLoop, calls=%fused_computation.9 | loop fusion | flops 819200 | bytes 988160 | tf_op jit(solution)/shard_map/convert_element_type | solution.py:244
  9.4 1.2 copy-done.2
  10.6 1.7 %shard_map.77 = (bf16[128,1024]{1,0:T(8,128)(2,1)S(1)}, bf16[128,1024]{1,0:T(8,128)(2,1)S(1)}, bf16[128,1024]{1,0:T(8,128)(2,1)S(1)}, bf16[128,1024]{1,0:T(8,128)(2,1)S(1)}, bf16[32,4096]{1,0:T(8,128)(2,1)}) custom-call(bf16[128,4096]{1,0:T(8,128)(2,1)S(1)} %bitcast.6, f32[1,4096]{1,0:T(1,128)} %gain_ref.1), custom_call_target="tpu_custom_call" | custom-call | flops 10000000 | bytes 100000 | tf_op jit(solution)/shard_map/pallas_call | solution.py:37
  12.3 1.6 %collective-permute-start.3 = (bf16[128,1024]{1,0:T(8,128)(2,1)S(1)}, bf16[128,1024]{1,0:T(8,128)(2,1)S(1)}, u32[]{:S(2)}, u32[]{:S(2)}) collective-permute-start(bf16[128,1024]{1,0:T(8,128)(2,1)S(1)} %get-tuple-element.83), channel_id=1, source_target_pairs={{0,1},{1,2},{2,3},{3,0},{128,129},{129,130},{130,131},{131,128},{4... | collective-permute-start | bytes 786440 | tf_op jit(solution)/shard_map/ppermute | solution.py:230
  13.9 2.9 %collective-permute-start.4 = (bf16[128,1024]{1,0:T(8,128)(2,1)S(1)}, bf16[128,1024]{1,0:T(8,128)(2,1)S(1)}, u32[]{:S(2)}, u32[]{:S(2)}) collective-permute-start(bf16[128,1024]{1,0:T(8,128)(2,1)S(1)} %get-tuple-element.84), channel_id=1, source_target_pairs={{0,2},{1,3},{2,0},{3,1},{128,130},{129,131},{130,128},{131,129},{4... | collective-permute-start | bytes 786440 | tf_op jit(solution)/shard_map/ppermute | solution.py:230
  16.8 1.3 collective-permute-start.5
  18.1 3.5 %collective-permute-done.3.refs_1_ = bf16[128,1024]{1,0:T(8,128)(2,1)S(1)} collective-permute-done((bf16[128,1024]{1,0:T(8,128)(2,1)S(1)}, bf16[128,1024]{1,0:T(8,128)(2,1)S(1)}, u32[]{:S(2)}, u32[]{:S(2)}) %collective-permute-start.3) | collective-permute-done | bytes 262176 | tf_op jit(solution)/shard_map/ppermute | solution.py:230
  21.6 6.8 %collective-permute-done.4.refs_2_ = bf16[128,1024]{1,0:T(8,128)(2,1)S(1)} collective-permute-done((bf16[128,1024]{1,0:T(8,128)(2,1)S(1)}, bf16[128,1024]{1,0:T(8,128)(2,1)S(1)}, u32[]{:S(2)}, u32[]{:S(2)}) %collective-permute-start.4) | collective-permute-done | bytes 262176 | tf_op jit(solution)/shard_map/ppermute | solution.py:230
  28.4 26.3 %all-gather.4.cloned.1.call-done.refs_4_ = bf16[8,1280,128]{2,1,0:T(8,128)(2,1)} async-done(((bf16[1,1280,128]{2,1,0:T(8,128)(2,1)}), bf16[8,1280,128]{2,1,0:T(8,128)(2,1)}) %all-gather.4.cloned.1.call-update) | async-done | bytes 2621456 | tf_op jit(solution)/shard_map/all_gather | solution.py:245
  54.7 3.4 %shard_map.78 = (bf16[128,1280]{1,0:T(8,128)(2,1)S(1)}, bf16[128,1280]{1,0:T(8,128)(2,1)S(1)}, bf16[128,1280]{1,0:T(8,128)(2,1)S(1)}, bf16[128,1280]{1,0:T(8,128)(2,1)S(1)}) custom-call(bf16[128,1024]{1,0:T(8,128)(2,1)S(1)} %get-tuple-element.82.refs_0_, bf16[128,1024]{1,0:T(8,128)(2,1)S(1)} %collective-permute-done.3.refs_1_, ...), custom_call_target="tpu_custom_call" | custom-call | flops 1342177280 | bytes 100000 | tf_op jit(solution)/shard_map/pallas_call | solution.py:37
  58.1 2.8 %collective-permute-start.6 = (bf16[128,1280]{1,0:T(8,128)(2,1)S(1)}, bf16[128,1280]{1,0:T(8,128)(2,1)}, u32[]{:S(2)}, u32[]{:S(2)}) collective-permute-start(bf16[128,1280]{1,0:T(8,128)(2,1)S(1)} %get-tuple-element.87), channel_id=1, source_target_pairs={{0,3},{1,0},{2,1},{3,2},{128,131},{129,128},{130,129},{131,130},{4... | collective-permute-start | bytes 983048 | tf_op jit(solution)/shard_map/ppermute | solution.py:230
  60.9 2.3 %collective-permute-start.8 = (bf16[128,1280]{1,0:T(8,128)(2,1)S(1)}, bf16[128,1280]{1,0:T(8,128)(2,1)}, u32[]{:S(2)}, u32[]{:S(2)}) collective-permute-start(bf16[128,1280]{1,0:T(8,128)(2,1)S(1)} %get-tuple-element.89), channel_id=1, source_target_pairs={{0,2},{1,3},{2,0},{3,1},{128,130},{129,131},{130,128},{131,129},{4... | collective-permute-start | bytes 983048 | tf_op jit(solution)/shard_map/ppermute | solution.py:230
  63.3 6.6 %shard_map.76 = (bf16[128,1024]{1,0:T(8,128)(2,1)S(1)}, bf16[32,4096]{1,0:T(8,128)(2,1)}) custom-call(bf16[128,4096]{1,0:T(8,128)(2,1)S(1)} %copy-done.1, bf16[4096,1024]{1,0:T(8,128)(2,1)} %bitcast.7), custom_call_target="tpu_custom_call" | custom-call | flops 1000000000 | bytes 100000 | tf_op jit(solution)/shard_map/pallas_call | solution.py:37
  69.8 2.2 %collective-permute-done.6.refs_1_ = bf16[128,1280]{1,0:T(8,128)(2,1)} collective-permute-done((bf16[128,1280]{1,0:T(8,128)(2,1)S(1)}, bf16[128,1280]{1,0:T(8,128)(2,1)}, u32[]{:S(2)}, u32[]{:S(2)}) %collective-permute-start.6) | collective-permute-done | bytes 327712 | tf_op jit(solution)/shard_map/ppermute | solution.py:230
  72.0 3.5 %collective-permute-done.7.refs_2_ = bf16[128,1280]{1,0:T(8,128)(2,1)} collective-permute-done((bf16[128,1280]{1,0:T(8,128)(2,1)S(1)}, bf16[128,1280]{1,0:T(8,128)(2,1)}, u32[]{:S(2)}, u32[]{:S(2)}) %collective-permute-start.7) | collective-permute-done | bytes 327712 | tf_op jit(solution)/shard_map/ppermute | solution.py:230
  75.5 2.2 %shard_map.79 = bf16[128,1280]{1,0:T(8,128)(2,1)S(1)} custom-call(bf16[128,1024]{1,0:T(8,128)(2,1)S(1)} %get-tuple-element.81.grad_ref, bf16[128,1280]{1,0:T(8,128)(2,1)S(1)} %get-tuple-element.86.refs_0_, bf16[128,1280]{1,0:T(8,128)(2,1)} %collective-permute-done.6.refs_1_, bf16[128,1280]{1,0:T(8,128)(2,1)} %collective-permute-done.7.refs_2_, ...), custom_call_target="tpu_custom_call" | custom-call | flops 100000000 | bytes 100000 | tf_op jit(solution)/shard_map/pallas_call | solution.py:37
  77.7 1.6 %conditional.3 = (bf16[32,4096]{1,0:T(8,128)(2,1)}, bf16[128,1280]{1,0:T(8,128)(2,1)}, bf16[128,1280]{1,0:T(8,128)(2,1)S(1)}, bf16[128,1280]{1,0:T(8,128)(2,1)S(1)}, bf16[128,1280]{1,0:T(8,128)(2,1)S(1)}) conditional(s32[]{:T(128)} %convert_element_type.20, () %tuple.29, (bf16[128,1280]{1,0:T(8,128)(2,1)S(1)}, bf16[8,1280,128]{2,1,0:T(8,128)(2,1)S(1)}, ...), branch_computations={%region_0.0_spmd, %region_1.0_spmd} | conditional | flops 1343177216 | bytes 15797928 | solution.py:282
  79.3 1.3 collective-permute-start.10
  80.6 1.3 collective-permute-start.11
  81.9 1.3 collective-permute-start.12
  83.2 1.5 collective-permute-start.9
  84.7 12.7 %all-gather.6.cloned.1.call-done = bf16[10240,128]{1,0:T(8,128)(2,1)} async-done(((bf16[1280,128]{1,0:T(8,128)(2,1)}), bf16[10240,128]{1,0:T(8,128)(2,1)}) %all-gather.6.cloned.1.call-update) | async-done | bytes 2621456 | tf_op jit(solution)/shard_map/all_gather | solution.py:252
  97.4 1.7 %copy-done = bf16[10240,128]{1,0:T(8,128)(2,1)S(1)} copy-done((bf16[10240,128]{1,0:T(8,128)(2,1)S(1)}, bf16[10240,128]{1,0:T(8,128)(2,1)}, u32[]{:S(2)}) %copy-start) | copy-done | bytes 2621464
  99.2 2.7 %shard_map.80 = (bf16[4,128,1280]{2,1,0:T(8,128)(2,1)}, f32[1,1280]{1,0:T(1,128)S(1)}) custom-call(bf16[128,1024]{1,0:T(8,128)(2,1)S(1)} %get-tuple-element.82.refs_0_, bf16[128,1024]{1,0:T(8,128)(2,1)S(1)} %collective-permute-done.3.refs_1_, bf16[128,1024]{1,0:T(8,128)(2,1)S(1)} %collective-permute-done.4.refs_2_, ...), custom_call_target="tpu_custom_call" | custom-call | flops 1342177280 | bytes 100000 | tf_op jit(solution)/shard_map/pallas_call | solution.py:37
  101.9 16.6 %conditional.4 = (bf16[4,128,1280]{2,1,0:T(8,128)(2,1)S(1)}, bf16[128,1280]{1,0:T(8,128)(2,1)S(1)}, f32[1024,128]{1,0:T(8,128)S(1)}) conditional(s32[]{:T(128)} %convert_element_type.20, (bf16[4,128,1280]{2,1,0:T(8,128)(2,1)}, bf16[128,1280]{1,0:T(8,128)(2,1)S(1)}, bf16[128,1280]{1,0:T(8,128)(2,1)}, bf16[128,1280]{1,0:T(8,128)(2,1)}, ...), branch_computations={%region_2.0_spmd, %region_3.0_spmd} | conditional | flops 100000000 | bytes 4032216 | solution.py:294
  101.9 4.3 %all-to-all-start.1 = ((bf16[4,128,1280]{2,1,0:T(8,128)(2,1)}), bf16[4,128,1280]{2,1,0:T(8,128)(2,1)S(1)}, u32[]{:S(2)}, u32[]{:S(2)}) async-start(bf16[4,128,1280]{2,1,0:T(8,128)(2,1)} %get-tuple-element.43), calls=%async_computation.1 | async-start | bytes 2621440 | tf_op jit(solution)/shard_map/cond/branch_0_fun/all_to_all | solution.py:297
  106.2 1.8 %branch_0_fun.1 = (bf16[128,1280]{1,0:T(8,128)(2,1)S(1)}, f32[1024,128]{1,0:T(8,128)S(1)}) custom-call(bf16[128,1280]{1,0:T(8,128)(2,1)S(1)} %get-tuple-element.44.refs_0_, bf16[128,1280]{1,0:T(8,128)(2,1)} %get-tuple-element.45.refs_1_, bf16[128,1280]{1,0:T(8,128)(2,1)} %get-tuple-element.46.refs_2_, bf16[128,1280]{1,0:T(8,128)(2,1)} %get-tuple-element.47.refs_3_), custom_call_target="tpu_custom_call" | custom-call | flops 100000000 | bytes 100000 | tf_op jit(solution)/shard_map/cond/branch_0_fun/pallas_call | solution.py:37
  108.0 10.5 %all-to-all-done.1 = bf16[4,128,1280]{2,1,0:T(8,128)(2,1)S(1)} async-done(((bf16[4,128,1280]{2,1,0:T(8,128)(2,1)}), bf16[4,128,1280]{2,1,0:T(8,128)(2,1)S(1)}, u32[]{:S(2)}, u32[]{:S(2)}) %all-to-all-start.1) | async-done | bytes 1310752 | tf_op jit(solution)/shard_map/cond/branch_0_fun/all_to_all | solution.py:297
  118.5 4.9 %conditional.5 = (bf16[128,1024]{1,0:T(8,128)(2,1)S(1)}) conditional(s32[]{:T(128)} %convert_element_type.20, (bf16[32,4096]{1,0:T(8,128)(2,1)}, bf16[32,4096]{1,0:T(8,128)(2,1)S(1)}, bf16[32,4096]{1,0:T(8,128)(2,1)S(1)}, bf16[32,4096]{1,0:T(8,128)(2,1)}, bf16[4096,1024]{1,0:T(8,128)(2,1)}) %tuple.47, () %tuple.36), branch_computations={%region_4.0_spmd, %region_5.0_spmd} | conditional | flops 1078067200 | bytes 9699336 | solution.py:300
  118.5 4.9 %convolution_convert_fusion = bf16[128,1024]{1,0:T(8,128)(2,1)S(1)} fusion(bf16[4096,1024]{1,0:T(8,128)(2,1)} %get-tuple-element.54, bf16[32,4096]{1,0:T(8,128)(2,1)} %get-tuple-element.53, bf16[32,4096]{1,0:T(8,128)(2,1)S(1)} %get-tuple-element.52, bf16[32,4096]{1,0:T(8,128)(2,1)S(1)} %get-tuple-element.51, bf16[32,4096]{1,0:T(8,128)(2,1)} %get-tuple-element.50), kind=kOutput, calls=%fused_computation | convolution fusion | flops 1078067200 | bytes 9699328 | tf_op jit(solution)/shard_map/cond/branch_0_fun/dot_general | solution.py:25
  123.4 1.0 shard_map.81
  124.6 15.9 %all_to_all.14 = f32[32,1,1280]{2,1,0:T(1,128)S(1)} all-to-all(f32[32,1,1280]{2,1,0:T(1,128)S(1)} %broadcast_in_dim.8), channel_id=1, replica_groups=mesh['pipe'=2,'tensor'=4,'z'=8,'y'=4] {'z','y'}, dimensions={0} | all-to-all | bytes 327680 | tf_op jit(solution)/shard_map/all_to_all | solution.py:318
  (33 shorter events, 3.2 us)
Async XLA Ops:
  6.5 48.2 %all-gather.4.cloned.1.call-start = ((), (), s32[]{:S(2)}) async-start(), calls=%async_computation.3 | async-start | bytes 2949120 | tf_op jit(solution)/shard_map/all_gather | solution.py:245
  9.3 88.1 %all-gather.6.cloned.1.call-start = ((), (), s32[]{:S(2)}) async-start(), calls=%async_computation.4 | async-start | bytes 2949120 | tf_op jit(solution)/shard_map/all_gather | solution.py:252
  9.4 1.2 copy-start.2
  12.3 9.3 %collective-permute-start.3 = (bf16[128,1024]{1,0:T(8,128)(2,1)S(1)}, bf16[128,1024]{1,0:T(8,128)(2,1)S(1)}, u32[]{:S(2)}, u32[]{:S(2)}) collective-permute-start(bf16[128,1024]{1,0:T(8,128)(2,1)S(1)} %get-tuple-element.83), channel_id=1, source_target_pairs={{0,1},{1,2},{2,3},{3,0},{128,129},{129,130},{130,131},{131,128},{4... | collective-permute-start | bytes 786440 | tf_op jit(solution)/shard_map/ppermute | solution.py:230
  13.9 14.5 %collective-permute-start.4 = (bf16[128,1024]{1,0:T(8,128)(2,1)S(1)}, bf16[128,1024]{1,0:T(8,128)(2,1)S(1)}, u32[]{:S(2)}, u32[]{:S(2)}) collective-permute-start(bf16[128,1024]{1,0:T(8,128)(2,1)S(1)} %get-tuple-element.84), channel_id=1, source_target_pairs={{0,2},{1,3},{2,0},{3,1},{128,130},{129,131},{130,128},{131,129},{4... | collective-permute-start | bytes 786440 | tf_op jit(solution)/shard_map/ppermute | solution.py:230
  16.8 11.6 %collective-permute-start.5 = (bf16[128,1024]{1,0:T(8,128)(2,1)S(1)}, bf16[128,1024]{1,0:T(8,128)(2,1)S(1)}, u32[]{:S(2)}, u32[]{:S(2)}) collective-permute-start(bf16[128,1024]{1,0:T(8,128)(2,1)S(1)} %get-tuple-element.85), channel_id=1, source_target_pairs={{0,3},{1,0},{2,1},{3,2},{128,131},{129,128},{130,129},{131,130},{4... | collective-permute-start | bytes 786440 | tf_op jit(solution)/shard_map/ppermute | solution.py:230
  54.7 8.5 %copy-start.1 = (bf16[128,4096]{1,0:T(8,128)(2,1)S(1)}, bf16[128,4096]{1,0:T(8,128)(2,1)}, u32[]{:S(2)}) copy-start(bf16[128,4096]{1,0:T(8,128)(2,1)} %rows_ref.1) | copy-start | bytes 3145732
  58.1 17.4 %copy-start.10 = (bf16[128,1280]{1,0:T(8,128)(2,1)}, bf16[128,1280]{1,0:T(8,128)(2,1)S(1)}, u32[]{:S(2)}) copy-start(bf16[128,1280]{1,0:T(8,128)(2,1)S(1)} %get-tuple-element.86.refs_0_) | copy-start | bytes 983044
  58.1 13.9 %collective-permute-start.6 = (bf16[128,1280]{1,0:T(8,128)(2,1)S(1)}, bf16[128,1280]{1,0:T(8,128)(2,1)}, u32[]{:S(2)}, u32[]{:S(2)}) collective-permute-start(bf16[128,1280]{1,0:T(8,128)(2,1)S(1)} %get-tuple-element.87), channel_id=1, source_target_pairs={{0,3},{1,0},{2,1},{3,2},{128,131},{129,128},{130,129},{131,130},{4... | collective-permute-start | bytes 983048 | tf_op jit(solution)/shard_map/ppermute | solution.py:230
  60.9 14.6 %collective-permute-start.7 = (bf16[128,1280]{1,0:T(8,128)(2,1)S(1)}, bf16[128,1280]{1,0:T(8,128)(2,1)}, u32[]{:S(2)}, u32[]{:S(2)}) collective-permute-start(bf16[128,1280]{1,0:T(8,128)(2,1)S(1)} %get-tuple-element.88), channel_id=1, source_target_pairs={{0,1},{1,2},{2,3},{3,0},{128,129},{129,130},{130,131},{131,128},{4... | collective-permute-start | bytes 983048 | tf_op jit(solution)/shard_map/ppermute | solution.py:230
  60.9 14.6 %collective-permute-start.8 = (bf16[128,1280]{1,0:T(8,128)(2,1)S(1)}, bf16[128,1280]{1,0:T(8,128)(2,1)}, u32[]{:S(2)}, u32[]{:S(2)}) collective-permute-start(bf16[128,1280]{1,0:T(8,128)(2,1)S(1)} %get-tuple-element.89), channel_id=1, source_target_pairs={{0,2},{1,3},{2,0},{3,1},{128,130},{129,131},{130,128},{131,129},{4... | collective-permute-start | bytes 983048 | tf_op jit(solution)/shard_map/ppermute | solution.py:230
  63.3 14.5 %copy-start.9 = (bf16[8,1280,128]{2,1,0:T(8,128)(2,1)S(1)}, bf16[8,1280,128]{2,1,0:T(8,128)(2,1)}, u32[]{:S(2)}) copy-start(bf16[8,1280,128]{2,1,0:T(8,128)(2,1)} %all-gather.4.cloned.1.call-done.refs_4_) | copy-start | bytes 7864324
  63.3 14.5 %copy-start.12 = (f32[1,4096]{1,0:T(1,128)S(1)}, f32[1,4096]{1,0:T(1,128)}, u32[]{:S(2)}) copy-start(f32[1,4096]{1,0:T(1,128)} %gain_ref.1) | copy-start | bytes 49156
  79.3 39.2 %collective-permute-start.10 = (bf16[32,4096]{1,0:T(8,128)(2,1)}, bf16[32,4096]{1,0:T(8,128)(2,1)S(1)}, u32[]{:S(2)}, u32[]{:S(2)}) collective-permute-start(bf16[32,4096]{1,0:T(8,128)(2,1)} %get-tuple-element.92.refs_9_), channel_id=1, source_target_pairs={{128,32},{160,64},{192,96},{224,0},{129,33},{161,65},{193,97},{225... | collective-permute-start | bytes 786440 | tf_op jit(solution)/shard_map/ppermute | solution.py:234
  80.6 37.9 %collective-permute-start.11 = (bf16[32,4096]{1,0:T(8,128)(2,1)}, bf16[32,4096]{1,0:T(8,128)(2,1)S(1)}, u32[]{:S(2)}, u32[]{:S(2)}) collective-permute-start(bf16[32,4096]{1,0:T(8,128)(2,1)} %get-tuple-element.92.refs_9_), channel_id=1, source_target_pairs={{128,64},{160,96},{192,0},{224,32},{129,65},{161,97},{193,1},{225,... | collective-permute-start | bytes 786440 | tf_op jit(solution)/shard_map/ppermute | solution.py:234
  81.9 36.6 %collective-permute-start.12 = (bf16[32,4096]{1,0:T(8,128)(2,1)}, bf16[32,4096]{1,0:T(8,128)(2,1)}, u32[]{:S(2)}, u32[]{:S(2)}) collective-permute-start(bf16[32,4096]{1,0:T(8,128)(2,1)} %get-tuple-element.92.refs_9_), channel_id=1, source_target_pairs={{128,96},{160,0},{192,32},{224,64},{129,97},{161,1},{193,33},{225,... | collective-permute-start | bytes 786440 | tf_op jit(solution)/shard_map/ppermute | solution.py:234
  83.2 35.3 %collective-permute-start.9 = (bf16[32,4096]{1,0:T(8,128)(2,1)}, bf16[32,4096]{1,0:T(8,128)(2,1)}, u32[]{:S(2)}, u32[]{:S(2)}) collective-permute-start(bf16[32,4096]{1,0:T(8,128)(2,1)} %get-tuple-element.92.refs_9_), channel_id=1, source_target_pairs={{128,0},{160,32},{192,64},{224,96},{129,1},{161,33},{193,65},{225,... | collective-permute-start | bytes 786440 | tf_op jit(solution)/shard_map/ppermute | solution.py:234
  97.4 1.7 %copy-start = (bf16[10240,128]{1,0:T(8,128)(2,1)S(1)}, bf16[10240,128]{1,0:T(8,128)(2,1)}, u32[]{:S(2)}) copy-start(bf16[10240,128]{1,0:T(8,128)(2,1)} %all-gather.6.cloned.1.call-done) | copy-start | bytes 7864324
  99.2 2.7 %copy-start.11 = (bf16[128,1280]{1,0:T(8,128)(2,1)S(1)}, bf16[128,1280]{1,0:T(8,128)(2,1)}, u32[]{:S(2)}) copy-start(bf16[128,1280]{1,0:T(8,128)(2,1)} %copy-done.10) | copy-start | bytes 983044
  101.9 16.6 %all-to-all-start.1 = ((bf16[4,128,1280]{2,1,0:T(8,128)(2,1)}), bf16[4,128,1280]{2,1,0:T(8,128)(2,1)S(1)}, u32[]{:S(2)}, u32[]{:S(2)}) async-start(bf16[4,128,1280]{2,1,0:T(8,128)(2,1)} %get-tuple-element.43), calls=%async_computation.1 | async-start | bytes 2621440 | tf_op jit(solution)/shard_map/cond/branch_0_fun/all_to_all | solution.py:297
Sparse Core Ops, SparseCore 0:
  9.4 45.2 all-gather.3
  56.5 40.8 all-gather.5
